TPU v7x, 256 devices: a whole 4x4x8 slice. The times are simulated.
256 devices in a mesh: tr: 32 (over x, y, core), su: 8 (over z).
Axes of the slice: x: 4, y: 4, z: 8, core: 2. Of those that a mesh axis runs over, the one named last changes fastest.
Arguments:
- amplitudes: bfloat16 [16, 32, 384, 384], P(None, 'tr', 'su'), as said below
- integrals: bfloat16 [32, 384, 32, 384], P('su', None, 'tr'), as said below
- occupied_irreps: int32 [32], replicated, may hold values from 0 to 7, as said below
- virtual_irreps: int32 [384], replicated, may hold values from 0 to 7, as said below
Outputs:
- update: bfloat16 [16, 32, 384, 384], P(None, 'tr', 'su')
Inputs may be any that keep to these rules, and one draw needn't show every extreme that they name: `occupied_irreps`: non-decreasing: the occupied orbitals come grouped by irrep. `virtual_irreps`: non-decreasing: the virtual orbitals come grouped by irrep. amplitudes[i, k, a, c] is 0 unless occupied_irreps[i] xor occupied_irreps[k] xor virtual_irreps[a] xor virtual_irreps[c] is 0. integrals[k, c, j, b] is 0 unless occupied_irreps[k] xor virtual_irreps[c] xor occupied_irreps[j] xor virtual_irreps[b] is 0.
All inputs are finite; a program needn't handle non-finite values.
Results may differ from a plain program's by a relative error of at most 0.001.
Values may be sent and summed in bfloat16 or wider, within the bound.
No kernel may reach another device: no remote copies, remote signals or barrier semaphores. Data moves between devices by JAX's collectives and lax.ppermute only.
A program may use at most 128 MiB of HBM per device.

v0:
```python
import jax
import jax.numpy as jnp
from jax import lax
from jax.sharding import PartitionSpec as P


def body(amplitudes, integrals, occupied_irreps, virtual_irreps):
    rows_i = amplitudes.shape[0]
    cols_j = amplitudes.shape[1]
    width_a = amplitudes.shape[2]
    whole_amps = lax.all_gather(amplitudes, "tr", axis=1, tiled=True)
    summed = jnp.einsum(
        "ikac,kcjb->ijab",
        whole_amps,
        lax.all_gather(integrals, "su", axis=0, tiled=True),
        preferred_element_type=jnp.float32,
    )
    cycle_term = summed.astype(jnp.bfloat16)
    start_a = lax.axis_index("su") * width_a
    start_j = lax.axis_index("tr") * cols_j
    labels_a = lax.dynamic_slice_in_dim(virtual_irreps, start_a, width_a, 0)
    labels_j = lax.dynamic_slice_in_dim(occupied_irreps, start_j, cols_j, 0)
    labels_i = occupied_irreps[:rows_i]
    parity = jnp.bitwise_xor(labels_i[:, None, None, None], labels_j[None, :, None, None])
    parity = jnp.bitwise_xor(parity, labels_a[None, None, :, None])
    parity = jnp.bitwise_xor(parity, virtual_irreps[None, None, None, :])
    return jnp.where(parity == 0, cycle_term, jnp.zeros_like(cycle_term))


def solution(mesh):
    return jax.shard_map(
        body,
        mesh=mesh,
        in_specs=(P(None, "tr", "su", None), P("su", None, "tr", None), P(), P()),
        out_specs=P(None, "tr", "su", None),
        check_vma=False,
    )
```

profile of v0, /device:TPU:1, one launch (start us, length us, event | category | flops | bytes accessed | tf_op | source)
XLA Modules:
  0.0 225.3 jit_solution(6360473805949482573)
XLA Ops:
  6.5 0.0 all-gather.3.cloned.1.call-start
  6.5 0.7 all-gather.3.cloned.1.call-update
  7.3 0.0 all-gather.5.cloned.1.call-start
  7.3 0.7 all-gather.5.cloned.1.call-update
  8.0 1.2 dynamic_slice.6
  9.3 0.8 dynamic_slice.7
  10.0 1.3 slice_xor_fusion
  11.3 0.1 broadcast_xor_fusion
  11.4 105.6 %all-gather.3.cloned.1.call-done = bf16[32,384,1,384]{3,1,2,0:T(8,128)(2,1)} async-done(((bf16[4,384,1,384]{3,1,2,0:T(8,128)(2,1)}), bf16[32,384,1,384]{3,1,2,0:T(8,128)(2,1)}) %all-gather.3.cloned.1.call-update) | async-done | bytes 9437200 | tf_op jit(solution)/shard_map/all_gather | solution.py:15
  117.0 84.1 %all-gather.5.cloned.1.call-done = bf16[16,32,48,384]{3,2,1,0:T(8,128)(2,1)} async-done(((bf16[16,1,48,384]{3,2,1,0:T(8,128)(2,1)}), bf16[16,32,48,384]{3,2,1,0:T(8,128)(2,1)}) %all-gather.5.cloned.1.call-update) | async-done | bytes 18874384 | tf_op jit(solution)/shard_map/all_gather | solution.py:11
  201.1 17.3 %fusion.14 = bf16[16,1,48,384]{3,2,1,0:T(8,128)(2,1)} fusion(bf16[16,32,48,384]{3,2,1,0:T(8,128)(2,1)} %all-gather.5.cloned.1.call-done, bf16[32,384,1,384]{3,1,2,0:T(8,128)(2,1)} %all-gather.3.cloned.1.call-done, s32[384]{0:T(512)} %param.7, s32[16,48]{1,0:T(8,128)S(1)} %broadcast_xor_fusion), kind=kOutput, calls=%fused_computation.6 | convolution fusion | flops 7248936960 | bytes 28905984 | tf_op jit(solution)/shard_map/ikac,kcjb->ijab/dot_general | solution.py:12
Async XLA Ops:
  6.5 110.4 %all-gather.3.cloned.1.call-start = ((), (), s32[]{:S(2)}) async-start(), calls=%async_computation | async-start | bytes 10616832 | tf_op jit(solution)/shard_map/all_gather | solution.py:15
  7.3 193.8 %all-gather.5.cloned.1.call-start = ((), (), s32[]{:S(2)}) async-start(), calls=%async_computation.1 | async-start | bytes 19464192 | tf_op jit(solution)/shard_map/all_gather | solution.py:11
Sparse Core Ops, SparseCore 0:
  9.1 107.7 all-gather.2
  119.6 81.4 all-gather.4
where the time goes:
time: 225 us
  waiting for transfers between devices  191 us (85%)
  matrix products  17.3 us (8%)
  between operations  13.4 us (6%)
    all_gather x1, waiting for transfers between devices, body(): lax.all_gather(integrals, 'su', axis=0, tiled=True)  106 us
    all_gather x1, waiting for transfers between devices, body(): whole_amps = lax.all_gather(amplitudes, 'tr', axis=1, tiled=True)  84.1 us
    dot_general x1, matrix products, body(): jnp.einsum('ikac,kcjb->ijab', whole_amps, lax.all_gather(integrals, 'su',...  17.3 us
  transfers between devices with their start and end apart: 2, of which 2 were waited for; matrix products, arithmetic and copies ran while one was open for 1% of the time, Pallas kernels for 0%

commit v1 on v0

v1 whole, which is shorter than its diff:
```python
import functools

import jax
import jax.numpy as jnp
from jax import lax
from jax.experimental import pallas as pl
from jax.experimental.pallas import tpu as pltpu
from jax.sharding import PartitionSpec as P

BF = jnp.bfloat16
F32 = jnp.float32
CAP = 64
NX = NY = 4
NZ = 8


def shift(step):
    return [(z, (z + step) % NZ) for z in range(NZ)]


def hop(first, step):
    pairs = []
    for x in range(NX):
        for y in range(NY):
            for c in range(2):
                along_x = (c == 0) == first
                to_x = (x + step) % NX if along_x else x
                to_y = y if along_x else (y + step) % NY
                pairs.append(((x * NY + y) * 2 + c, (to_x * NY + to_y) * 2 + c))
    return pairs


SWAP = [(d, d ^ 1) for d in range(2 * NX * NY)]


def positions(labels):
    before = jnp.sum((labels[None, :] < labels[:, None]).astype(jnp.int32), axis=1)
    return jnp.arange(labels.shape[0], dtype=jnp.int32) - before


def pick_matrix(pos_ref, base_ref):
    v = pos_ref.shape[1]
    rows = lax.broadcasted_iota(jnp.int32, (CAP, v), 0) + base_ref[0]
    return (rows == pos_ref[...]).astype(F32).astype(BF)


def pack_w_kernel(base_ref, pos_ref, w_ref, out_ref):
    pick = pick_matrix(pos_ref, base_ref)
    for k in range(w_ref.shape[0]):
        out_ref[k] = jnp.dot(pick, w_ref[k], preferred_element_type=F32).astype(BF)


def pack_w(pos, base, w):
    nk, v, _ = w.shape
    return pl.pallas_call(
        pack_w_kernel,
        out_shape=jax.ShapeDtypeStruct((nk, CAP, v), BF),
        in_specs=[
            pl.BlockSpec(memory_space=pltpu.SMEM),
            pl.BlockSpec(memory_space=pltpu.VMEM),
            pl.BlockSpec(memory_space=pltpu.VMEM),
        ],
        out_specs=pl.BlockSpec(memory_space=pltpu.VMEM),
        compiler_params=pltpu.CompilerParams(vmem_limit_bytes=32 * 2**20),
        name="pack_w",
    )(base, pos, w)


def pack_t_kernel(base_ref, pos_ref, t_ref, out_ref):
    pick = pick_matrix(pos_ref, base_ref)
    none = jnp.zeros_like(pick)
    ni, na, v = t_ref.shape
    half = ni // 2
    low = t_ref[:half].reshape(half * na, v)
    high = t_ref[half:].reshape(half * na, v)
    dims = (((1,), (1,)), ((), ()))
    both = lax.dot_general(low, jnp.concatenate([pick, none], 0), dims, preferred_element_type=F32)
    both += lax.dot_general(high, jnp.concatenate([none, pick], 0), dims, preferred_element_type=F32)
    out_ref[...] = both.astype(BF).reshape(half, na, 2 * CAP)


def pack_t(pos, base, t):
    ni, na, v = t.shape
    return pl.pallas_call(
        pack_t_kernel,
        out_shape=jax.ShapeDtypeStruct((ni // 2, na, 2 * CAP), BF),
        in_specs=[
            pl.BlockSpec(memory_space=pltpu.SMEM),
            pl.BlockSpec(memory_space=pltpu.VMEM),
            pl.BlockSpec(memory_space=pltpu.VMEM),
        ],
        out_specs=pl.BlockSpec(memory_space=pltpu.VMEM),
        compiler_params=pltpu.CompilerParams(vmem_limit_bytes=32 * 2**20),
        name="pack_t",
    )(base, pos, t)


def gather_w(d):
    half = d.shape[0] // 2
    right = left = d
    pieces = [d]
    for _ in range(3):
        right = lax.ppermute(right, "su", shift(1))
        left = lax.ppermute(left, "su", shift(-1))
        pieces += [right, left]
    pieces.append(lax.ppermute(right[:half], "su", shift(1)))
    pieces.append(lax.ppermute(left[half:], "su", shift(-1)))
    return pieces


OFFSETS = (0, 1, -1, 2, -2, 3, -3, 4)


def line(own, first):
    ahead, back = hop(first, 1), hop(first, -1)
    half = own.shape[0] // 2
    r = lax.ppermute(own, "tr", ahead)
    l = lax.ppermute(own, "tr", back)
    ro = lax.ppermute(r[:half], "tr", ahead)
    lo = lax.ppermute(l[half:], "tr", back)
    return own, l, jnp.concatenate([ro, lo], 0), r


def gather_t(t):
    pieces = jnp.stack(line(t, True))
    plane = jnp.concatenate(line(pieces, False), 0)
    return plane, lax.ppermute(plane, "tr", SWAP)


def accumulate(own_ref, other_ref, d_refs, d_cat, t_cat):
    v = d_refs[0].shape[2]
    nk = d_refs[0].shape[0]
    half_i, na = own_ref.shape[1], own_ref.shape[2]
    rows = half_i * na
    tr = lax.axis_index("tr")
    z = lax.axis_index("su")
    x, y, core = tr // (2 * NY), (tr // 2) % NY, tr % 2
    depth = nk * CAP
    for n, off in enumerate(OFFSETS):
        if n < 7:
            d_cat[n * depth : (n + 1) * depth] = d_refs[n][...].reshape(depth, v)
        else:
            d_cat[n * depth : n * depth + depth // 2] = d_refs[7][...].reshape(depth // 2, v)
            d_cat[n * depth + depth // 2 :] = d_refs[8][...].reshape(depth // 2, v)
        block = (z - off + NZ) % NZ
        for e in range(nk // 2):
            chip = block * (nk // 2) + e
            dx = (chip // NY - x + NX) % NX
            dy = (chip % NY - y + NY) % NY
            x_first = dy * NX + dx
            y_first = dx * NY + dy
            own_at = jnp.where(core == 0, x_first, y_first)
            other_at = jnp.where(core == 0, y_first, x_first)
            mine = own_ref[own_at].reshape(rows, 2 * CAP)
            theirs = other_ref[other_at].reshape(rows, 2 * CAP)
            even = jnp.where(core == 0, mine, theirs)
            odd = jnp.where(core == 0, theirs, mine)
            at = n * depth + e * 2 * CAP
            t_cat[0, :, at : at + 2 * CAP] = jnp.concatenate([even[:, :CAP], odd[:, :CAP]], 1)
            t_cat[1, :, at : at + 2 * CAP] = jnp.concatenate([even[:, CAP:], odd[:, CAP:]], 1)


def final_kernel(occ_ref, plane_ref, own_ref, other_ref, *refs):
    d_refs, (out_ref, d_cat, t_cat) = refs[:9], refs[9:]
    accumulate(own_ref, other_ref, d_refs, d_cat, t_cat)
    half_i, na = own_ref.shape[1], own_ref.shape[2]
    label_j = occ_ref[lax.axis_index("tr")]
    step = 2
    for h in range(2):
        for i0 in range(0, half_i, step):
            rows = t_cat[h, i0 * na : (i0 + step) * na, :]
            sums = jnp.dot(rows, d_cat[...], preferred_element_type=F32)
            for u in range(step):
                i = h * half_i + i0 + u
                keep = plane_ref[...] == jnp.bitwise_xor(occ_ref[i], label_j)
                out_ref[i] = jnp.where(keep, sums[u * na : (u + 1) * na], 0.0).astype(BF)


def sum_kernel(own_ref, other_ref, *refs):
    d_refs, (acc_ref, out_ref, d_cat, t_cat) = refs[:9], refs[9:]
    accumulate(own_ref, other_ref, d_refs, d_cat, t_cat)
    half_i, na = own_ref.shape[1], own_ref.shape[2]
    for h in range(2):
        for i in range(half_i):
            rows = t_cat[h, i * na : (i + 1) * na, :]
            out_ref[h * half_i + i] = acc_ref[h * half_i + i] + jnp.dot(rows, d_cat[...], preferred_element_type=F32)


def scratch(t_own, d):
    half_i, na = t_own.shape[1], t_own.shape[2]
    depth = NZ * d.shape[0] * CAP
    return [pltpu.VMEM((depth, d.shape[2]), BF), pltpu.VMEM((2, half_i * na, depth), BF)]


def body(amplitudes, integrals, occupied_irreps, virtual_irreps):
    ni, _, na, v = amplitudes.shape
    t = amplitudes.reshape(ni, na, v)
    w = integrals.reshape(integrals.shape[0], v, v)
    pos = positions(virtual_irreps)
    pos_row = pos.reshape(1, v)

    def one_pass(base):
        base = jnp.full((1,), base, jnp.int32)
        d = pack_w(pos_row, base, w)
        p = pack_t(pos_row, base, t)
        pieces = gather_w(d)
        own, other = gather_t(p)
        return own, other, pieces

    start_a = lax.axis_index("su") * na
    labels_a = lax.dynamic_slice_in_dim(virtual_irreps, start_a, na, 0)
    plane = jnp.bitwise_xor(labels_a[:, None], virtual_irreps[None, :])
    own, other, pieces = one_pass(0)
    vmem = pl.BlockSpec(memory_space=pltpu.VMEM)
    flops = 2 * ni * na * v * NZ * w.shape[0] * CAP
    fast = pl.pallas_call(
        final_kernel,
        out_shape=jax.ShapeDtypeStruct((ni, na, v), BF),
        in_specs=[pl.BlockSpec(memory_space=pltpu.SMEM)] + [vmem] * 12,
        out_specs=vmem,
        scratch_shapes=scratch(own, pieces[0]),
        compiler_params=pltpu.CompilerParams(vmem_limit_bytes=40 * 2**20),
        cost_estimate=pl.CostEstimate(flops=flops, bytes_accessed=6 * 2**20, transcendentals=0),
        name="contract",
    )(occupied_irreps, plane, own, other, *pieces)

    def all_windows():
        def window(n, acc):
            own, other, pieces = one_pass(n * CAP)
            return pl.pallas_call(
                sum_kernel,
                out_shape=jax.ShapeDtypeStruct((ni, na, v), F32),
                in_specs=[vmem] * 12,
                out_specs=vmem,
                scratch_shapes=scratch(own, pieces[0]),
                compiler_params=pltpu.CompilerParams(vmem_limit_bytes=40 * 2**20),
                name="contract_window",
            )(own, other, *pieces, acc)

        windows = jnp.max(pos) // CAP + 1
        acc = lax.fori_loop(0, windows, window, jnp.zeros((ni, na, v), F32))
        label_j = occupied_irreps[lax.axis_index("tr")]
        parity = jnp.bitwise_xor(occupied_irreps[:ni, None, None], label_j)
        keep = jnp.bitwise_xor(parity, plane[None]) == 0
        return jnp.where(keep, acc.astype(BF), jnp.zeros((), BF))

    out = lax.cond(jnp.max(pos) < CAP, lambda: fast, all_windows)
    return out.reshape(ni, 1, na, v)


def solution(mesh):
    return jax.shard_map(
        body,
        mesh=mesh,
        in_specs=(P(None, "tr", "su", None), P("su", None, "tr", None), P(), P()),
        out_specs=P(None, "tr", "su", None),
        check_vma=False,
    )
```

time: 225 us -> 72.8 us (0.32)
  the two profiles are of different devices: /device:TPU:1 before, /device:TPU:126 now
where the time goes in v1:
time: 72.8 us; the launch traced here: 72.6 us
  waiting for transfers between devices  35.3 us (48%)
  starting transfers between devices  22.9 us (31%)
  Pallas kernels  6.45 us (9%)
  local copies, waits for them, and re-layouts  4.85 us (7%)
  other arithmetic  2.37 us (3%)
    ppermute x3, starting transfers between devices, gather_w(): right = lax.ppermute(right, 'su', shift(1))  10.7 us
    ppermute x3, waiting for transfers between devices, gather_w(): right = lax.ppermute(right, 'su', shift(1))  10.3 us
    ppermute x2, waiting for transfers between devices, line(): r = lax.ppermute(own, 'tr', ahead)  8.22 us
    ppermute x2, waiting for transfers between devices, line(): lo = lax.ppermute(l[half:], 'tr', back)  5.72 us
    ppermute x2, waiting for transfers between devices, line(): ro = lax.ppermute(r[:half], 'tr', ahead)  5.43 us
    ppermute x1, waiting for transfers between devices, gather_w(): pieces.append(lax.ppermute(left[half:], 'su', shift(-1)))  4.95 us
    pallas_call x1, Pallas kernels, body(): pl.pallas_call(final_kernel, out_shape=jax.ShapeDtypeStruct((ni, na, v),...  4.77 us
    ppermute x1, starting transfers between devices, gather_w(): pieces.append(lax.ppermute(right[:half], 'su', shift(1)))  3.59 us
  transfers between devices with their start and end apart: 17, of which 11 were waited for; matrix products, arithmetic and copies ran while one was open for 4% of the time, Pallas kernels for 0%

profile of v1, /device:TPU:126, one launch (start us, length us, event | category | flops | bytes accessed | tf_op | source)
XLA Modules:
  0.0 72.6 jit_solution(16869205557176700558)
XLA Ops:
  0.0 1.0 %convert_reduce_fusion = s32[384]{0:T(512)S(1)} fusion(s32[384]{0:T(512)} %param.11), kind=kLoop, calls=%fused_computation.14 | loop fusion | flops 441984 | bytes 3072 | tf_op jit(solution)/shard_map/reduce_sum | solution.py:37
  1.0 1.4 %pack_t.2 = bf16[8,48,128]{2,1,0:T(8,128)(2,1)S(1)} custom-call(s32[1]{0:T(128)} %constant.52.clone.1.base_ref, s32[1,384]{1,0:T(1,128)S(1)} %reshape_subtract_fusion.pos_ref, bf16[16,48,384]{2,1,0:T(8,128)(2,1)} %bitcast.53), custom_call_target="tpu_custom_call" | custom-call | tf_op jit(solution)/shard_map/pack_t/pallas_call | solution.py:84
  2.4 0.6 collective-permute-start.18
  2.9 1.5 %collective-permute-start.17 = (bf16[8,48,128]{2,1,0:T(8,128)(2,1)S(1)}, bf16[8,48,128]{2,1,0:T(8,128)(2,1)S(1)}, u32[]{:S(2)}, u32[]{:S(2)}) collective-permute-start(bf16[8,48,128]{2,1,0:T(8,128)(2,1)S(1)} %pack_t.2), channel_id=1, source_target_pairs={{0,192},{8,56},{16,208},{24,8},{32,224},{40,24},{48,240},{56,40},{... | collective-permute-start | bytes 294920 | tf_op jit(solution)/shard_map/ppermute | solution.py:118
  4.5 2.6 %collective-permute-done.18 = bf16[8,48,128]{2,1,0:T(8,128)(2,1)S(1)} collective-permute-done((bf16[8,48,128]{2,1,0:T(8,128)(2,1)S(1)}, bf16[8,48,128]{2,1,0:T(8,128)(2,1)S(1)}, u32[]{:S(2)}, u32[]{:S(2)}) %collective-permute-start.18) | collective-permute-done | bytes 98336 | tf_op jit(solution)/shard_map/ppermute | solution.py:117
  7.1 1.7 %collective-permute-start.19 = (bf16[4,48,128]{2,1,0:T(8,128)(2,1)S(1)}, bf16[4,48,128]{2,1,0:T(8,128)(2,1)S(1)}, u32[]{:S(2)}, u32[]{:S(2)}) collective-permute-start(bf16[4,48,128]{2,1,0:T(8,128)(2,1)S(1)} %slice.51), channel_id=1, source_target_pairs={{0,64},{8,24},{16,80},{24,40},{32,96},{40,56},{48,112},{56,8},{64,... | collective-permute-start | bytes 147464 | tf_op jit(solution)/shard_map/ppermute | solution.py:119
  9.2 2.0 %collective-permute-done.19 = bf16[4,48,128]{2,1,0:T(8,128)(2,1)S(1)} collective-permute-done((bf16[4,48,128]{2,1,0:T(8,128)(2,1)S(1)}, bf16[4,48,128]{2,1,0:T(8,128)(2,1)S(1)}, u32[]{:S(2)}, u32[]{:S(2)}) %collective-permute-start.19) | collective-permute-done | bytes 49184 | tf_op jit(solution)/shard_map/ppermute | solution.py:119
  11.2 3.0 %collective-permute-done.20 = bf16[4,48,128]{2,1,0:T(8,128)(2,1)S(1)} collective-permute-done((bf16[4,48,128]{2,1,0:T(8,128)(2,1)S(1)}, bf16[4,48,128]{2,1,0:T(8,128)(2,1)S(1)}, u32[]{:S(2)}, u32[]{:S(2)}) %collective-permute-start.20) | collective-permute-done | bytes 49184 | tf_op jit(solution)/shard_map/ppermute | solution.py:120
  14.5 1.9 %collective-permute-start.21 = (bf16[4,8,48,128]{3,2,1,0:T(8,128)(2,1)S(1)}, bf16[4,8,48,128]{3,2,1,0:T(8,128)(2,1)S(1)}, u32[]{:S(2)}, u32[]{:S(2)}) collective-permute-start(bf16[4,8,48,128]{3,2,1,0:T(8,128)(2,1)S(1)} %pad_maximum_fusion.1), channel_id=1, source_target_pairs={{0,48},{8,200},{16,0},{24,216},{32,16},{40,232},{48,32},{56,248},{... | collective-permute-start | bytes 1179656 | tf_op jit(solution)/shard_map/ppermute | solution.py:118
  16.4 5.6 %collective-permute-done.22 = bf16[4,8,48,128]{3,2,1,0:T(8,128)(2,1)S(1)} collective-permute-done((bf16[4,8,48,128]{3,2,1,0:T(8,128)(2,1)S(1)}, bf16[4,8,48,128]{3,2,1,0:T(8,128)(2,1)S(1)}, u32[]{:S(2)}, u32[]{:S(2)}) %collective-permute-start.22) | collective-permute-done | bytes 393248 | tf_op jit(solution)/shard_map/ppermute | solution.py:117
  22.1 1.5 %collective-permute-start.23 = (bf16[2,8,48,128]{3,2,1,0:T(8,128)(2,1)S(1)}, bf16[2,8,48,128]{3,2,1,0:T(8,128)(2,1)S(1)}, u32[]{:S(2)}, u32[]{:S(2)}) collective-permute-start(bf16[2,8,48,128]{3,2,1,0:T(8,128)(2,1)S(1)} %slice.53), channel_id=1, source_target_pairs={{0,16},{8,72},{16,32},{24,88},{32,48},{40,104},{48,0},{56,120},{64... | collective-permute-start | bytes 589832 | tf_op jit(solution)/shard_map/ppermute | solution.py:119
  23.7 0.7 collective-permute-start.24
  24.4 3.4 %collective-permute-done.23 = bf16[2,8,48,128]{3,2,1,0:T(8,128)(2,1)S(1)} collective-permute-done((bf16[2,8,48,128]{3,2,1,0:T(8,128)(2,1)S(1)}, bf16[2,8,48,128]{3,2,1,0:T(8,128)(2,1)S(1)}, u32[]{:S(2)}, u32[]{:S(2)}) %collective-permute-start.23) | collective-permute-done | bytes 196640 | tf_op jit(solution)/shard_map/ppermute | solution.py:119
  27.9 2.7 %collective-permute-done.24 = bf16[2,8,48,128]{3,2,1,0:T(8,128)(2,1)S(1)} collective-permute-done((bf16[2,8,48,128]{3,2,1,0:T(8,128)(2,1)S(1)}, bf16[2,8,48,128]{3,2,1,0:T(8,128)(2,1)S(1)}, u32[]{:S(2)}, u32[]{:S(2)}) %collective-permute-start.24) | collective-permute-done | bytes 196640 | tf_op jit(solution)/shard_map/ppermute | solution.py:120
  31.2 3.2 %collective-permute-start.26 = (bf16[4,64,384]{2,1,0:T(8,128)(2,1)S(1)}, bf16[4,64,384]{2,1,0:T(8,128)(2,1)S(1)}, u32[]{:S(2)}, u32[]{:S(2)}) collective-permute-start(bf16[4,64,384]{2,1,0:T(8,128)(2,1)S(1)} %pack_w.2.refs_0_), channel_id=1, source_target_pairs={{0,1},{1,2},{2,3},{3,4},{4,5},{5,6},{6,7},{7,0},{8,9},{9,10},{10,1... | collective-permute-start | bytes 589832 | tf_op jit(solution)/shard_map/ppermute | solution.py:103
  34.4 4.8 %collective-permute-done.26.refs_1_ = bf16[4,64,384]{2,1,0:T(8,128)(2,1)S(1)} collective-permute-done((bf16[4,64,384]{2,1,0:T(8,128)(2,1)S(1)}, bf16[4,64,384]{2,1,0:T(8,128)(2,1)S(1)}, u32[]{:S(2)}, u32[]{:S(2)}) %collective-permute-start.26) | collective-permute-done | bytes 196640 | tf_op jit(solution)/shard_map/ppermute | solution.py:103
  39.2 3.7 %collective-permute-start.28 = (bf16[4,64,384]{2,1,0:T(8,128)(2,1)S(1)}, bf16[4,64,384]{2,1,0:T(8,128)(2,1)}, u32[]{:S(2)}, u32[]{:S(2)}) collective-permute-start(bf16[4,64,384]{2,1,0:T(8,128)(2,1)S(1)} %collective-permute-done.26.refs_1_), channel_id=1, source_target_pairs={{0,1},{1,2},{2,3},{3,4},{4,5},{5,6},{6,7},{7,0},{8,9},{9,10},{10,1... | collective-permute-start | bytes 589832 | tf_op jit(solution)/shard_map/ppermute | solution.py:103
  42.9 0.7 copy-done.8
  43.6 3.3 %collective-permute-done.28.refs_3_ = bf16[4,64,384]{2,1,0:T(8,128)(2,1)} collective-permute-done((bf16[4,64,384]{2,1,0:T(8,128)(2,1)S(1)}, bf16[4,64,384]{2,1,0:T(8,128)(2,1)}, u32[]{:S(2)}, u32[]{:S(2)}) %collective-permute-start.28) | collective-permute-done | bytes 196640 | tf_op jit(solution)/shard_map/ppermute | solution.py:103
  46.9 3.8 %collective-permute-start.30 = (bf16[4,64,384]{2,1,0:T(8,128)(2,1)}, bf16[4,64,384]{2,1,0:T(8,128)(2,1)S(1)}, u32[]{:S(2)}, u32[]{:S(2)}) collective-permute-start(bf16[4,64,384]{2,1,0:T(8,128)(2,1)} %collective-permute-done.28.refs_3_), channel_id=1, source_target_pairs={{0,1},{1,2},{2,3},{3,4},{4,5},{5,6},{6,7},{7,0},{8,9},{9,10},{10,1... | collective-permute-start | bytes 589832 | tf_op jit(solution)/shard_map/ppermute | solution.py:103
  50.7 0.6 collective-permute-done.29.refs_4_
  51.3 0.7 broadcast_xor_fusion.plane_ref
  52.0 2.2 %collective-permute-done.30.refs_5_ = bf16[4,64,384]{2,1,0:T(8,128)(2,1)S(1)} collective-permute-done((bf16[4,64,384]{2,1,0:T(8,128)(2,1)}, bf16[4,64,384]{2,1,0:T(8,128)(2,1)S(1)}, u32[]{:S(2)}, u32[]{:S(2)}) %collective-permute-start.30) | collective-permute-done | bytes 196640 | tf_op jit(solution)/shard_map/ppermute | solution.py:103
  54.2 0.7 slice.55
  54.9 3.6 %collective-permute-start.32 = (bf16[2,64,384]{2,1,0:T(8,128)(2,1)}, bf16[2,64,384]{2,1,0:T(8,128)(2,1)}, u32[]{:S(2)}, u32[]{:S(2)}) collective-permute-start(bf16[2,64,384]{2,1,0:T(8,128)(2,1)} %slice.55), channel_id=1, source_target_pairs={{0,1},{1,2},{2,3},{3,4},{4,5},{5,6},{6,7},{7,0},{8,9},{9,10},{10,1... | collective-permute-start | bytes 294920 | tf_op jit(solution)/shard_map/ppermute | solution.py:106
  58.5 0.6 slice.56
  59.1 0.7 copy-done.6
  59.8 0.6 iota_subtract_fusion
  61.0 5.0 %collective-permute-done.33.refs_8_ = bf16[2,64,384]{2,1,0:T(8,128)(2,1)} collective-permute-done((bf16[2,64,384]{2,1,0:T(8,128)(2,1)}, bf16[2,64,384]{2,1,0:T(8,128)(2,1)}, u32[]{:S(2)}, u32[]{:S(2)}) %collective-permute-start.33) | collective-permute-done | bytes 98336 | tf_op jit(solution)/shard_map/ppermute | solution.py:107
  65.9 0.9 %copy-done.7 = bf16[4,64,384]{2,1,0:T(8,128)(2,1)S(1)} copy-done((bf16[4,64,384]{2,1,0:T(8,128)(2,1)S(1)}, bf16[4,64,384]{2,1,0:T(8,128)(2,1)}, u32[]{:S(2)}) %copy-start.7) | copy-done | bytes 196632
  66.9 0.9 %copy-done.9 = bf16[4,64,384]{2,1,0:T(8,128)(2,1)S(1)} copy-done((bf16[4,64,384]{2,1,0:T(8,128)(2,1)S(1)}, bf16[4,64,384]{2,1,0:T(8,128)(2,1)}, u32[]{:S(2)}) %copy-start.9) | copy-done | bytes 196632
  67.8 4.8 %contract.1 = bf16[16,48,384]{2,1,0:T(8,128)(2,1)} custom-call(s32[32]{0:T(128)S(1)} %copy-done.14, s32[48,384]{1,0:T(8,128)} %broadcast_xor_fusion.plane_ref, bf16[16,8,48,128]{3,2,1,0:T(8,128)(2,1)S(1)} %constant_dynamic-update-slice_fusion.8.own_ref, bf16[16,8,48,128]{3,2,1,0:T(8,128)(2,1)S(1)} %collective-permute-done.25.other_ref, ...), custom_call_target="tpu_custom_call" | custom-call | flops 1207959552 | bytes 6291456 | tf_op jit(solution)/shard_map/contract/pallas_call | solution.py:216
  (41 shorter events, 1.6 us)
Async XLA Ops:
  2.4 4.7 %collective-permute-start.18 = (bf16[8,48,128]{2,1,0:T(8,128)(2,1)S(1)}, bf16[8,48,128]{2,1,0:T(8,128)(2,1)S(1)}, u32[]{:S(2)}, u32[]{:S(2)}) collective-permute-start(bf16[8,48,128]{2,1,0:T(8,128)(2,1)S(1)} %pack_t.2), channel_id=1, source_target_pairs={{0,64},{8,24},{16,80},{24,40},{32,96},{40,56},{48,112},{56,8},{64,... | collective-permute-start | bytes 294920 | tf_op jit(solution)/shard_map/ppermute | solution.py:117
  2.9 5.8 %collective-permute-start.17 = (bf16[8,48,128]{2,1,0:T(8,128)(2,1)S(1)}, bf16[8,48,128]{2,1,0:T(8,128)(2,1)S(1)}, u32[]{:S(2)}, u32[]{:S(2)}) collective-permute-start(bf16[8,48,128]{2,1,0:T(8,128)(2,1)S(1)} %pack_t.2), channel_id=1, source_target_pairs={{0,192},{8,56},{16,208},{24,8},{32,224},{40,24},{48,240},{56,40},{... | collective-permute-start | bytes 294920 | tf_op jit(solution)/shard_map/ppermute | solution.py:118
  7.1 4.1 %collective-permute-start.19 = (bf16[4,48,128]{2,1,0:T(8,128)(2,1)S(1)}, bf16[4,48,128]{2,1,0:T(8,128)(2,1)S(1)}, u32[]{:S(2)}, u32[]{:S(2)}) collective-permute-start(bf16[4,48,128]{2,1,0:T(8,128)(2,1)S(1)} %slice.51), channel_id=1, source_target_pairs={{0,64},{8,24},{16,80},{24,40},{32,96},{40,56},{48,112},{56,8},{64,... | collective-permute-start | bytes 147464 | tf_op jit(solution)/shard_map/ppermute | solution.py:119
  8.8 5.4 %collective-permute-start.20 = (bf16[4,48,128]{2,1,0:T(8,128)(2,1)S(1)}, bf16[4,48,128]{2,1,0:T(8,128)(2,1)S(1)}, u32[]{:S(2)}, u32[]{:S(2)}) collective-permute-start(bf16[4,48,128]{2,1,0:T(8,128)(2,1)S(1)} %slice.52), channel_id=1, source_target_pairs={{0,192},{8,56},{16,208},{24,8},{32,224},{40,24},{48,240},{56,40},{... | collective-permute-start | bytes 147464 | tf_op jit(solution)/shard_map/ppermute | solution.py:120
  14.2 7.9 %collective-permute-start.22 = (bf16[4,8,48,128]{3,2,1,0:T(8,128)(2,1)S(1)}, bf16[4,8,48,128]{3,2,1,0:T(8,128)(2,1)S(1)}, u32[]{:S(2)}, u32[]{:S(2)}) collective-permute-start(bf16[4,8,48,128]{3,2,1,0:T(8,128)(2,1)S(1)} %pad_maximum_fusion.1), channel_id=1, source_target_pairs={{0,16},{8,72},{16,32},{24,88},{32,48},{40,104},{48,0},{56,120},{64... | collective-permute-start | bytes 1179656 | tf_op jit(solution)/shard_map/ppermute | solution.py:117
  14.5 9.1 %collective-permute-start.21 = (bf16[4,8,48,128]{3,2,1,0:T(8,128)(2,1)S(1)}, bf16[4,8,48,128]{3,2,1,0:T(8,128)(2,1)S(1)}, u32[]{:S(2)}, u32[]{:S(2)}) collective-permute-start(bf16[4,8,48,128]{3,2,1,0:T(8,128)(2,1)S(1)} %pad_maximum_fusion.1), channel_id=1, source_target_pairs={{0,48},{8,200},{16,0},{24,216},{32,16},{40,232},{48,32},{56,248},{... | collective-permute-start | bytes 1179656 | tf_op jit(solution)/shard_map/ppermute | solution.py:118
  22.1 8.7 %copy-start.11 = (bf16[4,384,1,384]{3,1,2,0:T(8,128)(2,1)S(1)}, bf16[4,384,1,384]{3,1,2,0:T(8,128)(2,1)}, u32[]{:S(2)}) copy-start(bf16[4,384,1,384]{3,1,2,0:T(8,128)(2,1)} %param.9) | copy-start | bytes 3538948
  22.1 5.7 %collective-permute-start.23 = (bf16[2,8,48,128]{3,2,1,0:T(8,128)(2,1)S(1)}, bf16[2,8,48,128]{3,2,1,0:T(8,128)(2,1)S(1)}, u32[]{:S(2)}, u32[]{:S(2)}) collective-permute-start(bf16[2,8,48,128]{3,2,1,0:T(8,128)(2,1)S(1)} %slice.53), channel_id=1, source_target_pairs={{0,16},{8,72},{16,32},{24,88},{32,48},{40,104},{48,0},{56,120},{64... | collective-permute-start | bytes 589832 | tf_op jit(solution)/shard_map/ppermute | solution.py:119
  23.7 7.0 %collective-permute-start.24 = (bf16[2,8,48,128]{3,2,1,0:T(8,128)(2,1)S(1)}, bf16[2,8,48,128]{3,2,1,0:T(8,128)(2,1)S(1)}, u32[]{:S(2)}, u32[]{:S(2)}) collective-permute-start(bf16[2,8,48,128]{3,2,1,0:T(8,128)(2,1)S(1)} %slice.54), channel_id=1, source_target_pairs={{0,48},{8,200},{16,0},{24,216},{32,16},{40,232},{48,32},{56,248},{... | collective-permute-start | bytes 589832 | tf_op jit(solution)/shard_map/ppermute | solution.py:120
  24.4 19.2 %copy-start.13 = (s32[384]{0:T(512)S(1)}, s32[384]{0:T(512)}, u32[]{:S(2)}) copy-start(s32[384]{0:T(512)} %param.11) | copy-start | bytes 4612
  27.9 38.1 %copy-start.14 = (s32[32]{0:T(128)S(1)}, s32[32]{0:T(128)}, u32[]{:S(2)}) copy-start(s32[32]{0:T(128)} %occ_ref.1) | copy-start | bytes 388
  30.7 35.2 %collective-permute-start.25 = (bf16[16,8,48,128]{3,2,1,0:T(8,128)(2,1)S(1)}, bf16[16,8,48,128]{3,2,1,0:T(8,128)(2,1)S(1)}, u32[]{:S(2)}, u32[]{:S(2)}) collective-permute-start(bf16[16,8,48,128]{3,2,1,0:T(8,128)(2,1)S(1)} %constant_dynamic-update-slice_fusion.8.own_ref), channel_id=1, source_target_pairs={{0,8},{8,0},{16,24},{24,16},{32,40},{40,32},{48,56},{56,48},{64,72... | collective-permute-start | bytes 4718600 | tf_op jit(solution)/shard_map/ppermute | solution.py:127
  31.2 8.0 %collective-permute-start.26 = (bf16[4,64,384]{2,1,0:T(8,128)(2,1)S(1)}, bf16[4,64,384]{2,1,0:T(8,128)(2,1)S(1)}, u32[]{:S(2)}, u32[]{:S(2)}) collective-permute-start(bf16[4,64,384]{2,1,0:T(8,128)(2,1)S(1)} %pack_w.2.refs_0_), channel_id=1, source_target_pairs={{0,1},{1,2},{2,3},{3,4},{4,5},{5,6},{6,7},{7,0},{8,9},{9,10},{10,1... | collective-permute-start | bytes 589832 | tf_op jit(solution)/shard_map/ppermute | solution.py:103
  34.4 9.2 %collective-permute-start.27 = (bf16[4,64,384]{2,1,0:T(8,128)(2,1)S(1)}, bf16[4,64,384]{2,1,0:T(8,128)(2,1)}, u32[]{:S(2)}, u32[]{:S(2)}) collective-permute-start(bf16[4,64,384]{2,1,0:T(8,128)(2,1)S(1)} %pack_w.2.refs_0_), channel_id=1, source_target_pairs={{0,7},{1,0},{2,1},{3,2},{4,3},{5,4},{6,5},{7,6},{8,15},{9,8},{10,9... | collective-permute-start | bytes 589832 | tf_op jit(solution)/shard_map/ppermute | solution.py:104
  39.2 7.7 %collective-permute-start.28 = (bf16[4,64,384]{2,1,0:T(8,128)(2,1)S(1)}, bf16[4,64,384]{2,1,0:T(8,128)(2,1)}, u32[]{:S(2)}, u32[]{:S(2)}) collective-permute-start(bf16[4,64,384]{2,1,0:T(8,128)(2,1)S(1)} %collective-permute-done.26.refs_1_), channel_id=1, source_target_pairs={{0,1},{1,2},{2,3},{3,4},{4,5},{5,6},{6,7},{7,0},{8,9},{9,10},{10,1... | collective-permute-start | bytes 589832 | tf_op jit(solution)/shard_map/ppermute | solution.py:103
  42.9 0.7 copy-start.8
  43.5 7.8 %collective-permute-start.29 = (bf16[4,64,384]{2,1,0:T(8,128)(2,1)}, bf16[4,64,384]{2,1,0:T(8,128)(2,1)}, u32[]{:S(2)}, u32[]{:S(2)}) collective-permute-start(bf16[4,64,384]{2,1,0:T(8,128)(2,1)} %collective-permute-done.27.refs_2_), channel_id=1, source_target_pairs={{0,7},{1,0},{2,1},{3,2},{4,3},{5,4},{6,5},{7,6},{8,15},{9,8},{10,9... | collective-permute-start | bytes 589832 | tf_op jit(solution)/shard_map/ppermute | solution.py:104
  46.9 7.3 %collective-permute-start.30 = (bf16[4,64,384]{2,1,0:T(8,128)(2,1)}, bf16[4,64,384]{2,1,0:T(8,128)(2,1)S(1)}, u32[]{:S(2)}, u32[]{:S(2)}) collective-permute-start(bf16[4,64,384]{2,1,0:T(8,128)(2,1)} %collective-permute-done.28.refs_3_), channel_id=1, source_target_pairs={{0,1},{1,2},{2,3},{3,4},{4,5},{5,6},{6,7},{7,0},{8,9},{9,10},{10,1... | collective-permute-start | bytes 589832 | tf_op jit(solution)/shard_map/ppermute | solution.py:103
  51.3 7.1 %collective-permute-start.31 = (bf16[4,64,384]{2,1,0:T(8,128)(2,1)}, bf16[4,64,384]{2,1,0:T(8,128)(2,1)S(1)}, u32[]{:S(2)}, u32[]{:S(2)}) collective-permute-start(bf16[4,64,384]{2,1,0:T(8,128)(2,1)} %collective-permute-done.29.refs_4_), channel_id=1, source_target_pairs={{0,7},{1,0},{2,1},{3,2},{4,3},{5,4},{6,5},{7,6},{8,15},{9,8},{10,9... | collective-permute-start | bytes 589832 | tf_op jit(solution)/shard_map/ppermute | solution.py:104
  54.9 6.1 %collective-permute-start.32 = (bf16[2,64,384]{2,1,0:T(8,128)(2,1)}, bf16[2,64,384]{2,1,0:T(8,128)(2,1)}, u32[]{:S(2)}, u32[]{:S(2)}) collective-permute-start(bf16[2,64,384]{2,1,0:T(8,128)(2,1)} %slice.55), channel_id=1, source_target_pairs={{0,1},{1,2},{2,3},{3,4},{4,5},{5,6},{6,7},{7,0},{8,9},{9,10},{10,1... | collective-permute-start | bytes 294920 | tf_op jit(solution)/shard_map/ppermute | solution.py:106
  59.1 0.7 copy-start.6
  59.8 6.1 %collective-permute-start.33 = (bf16[2,64,384]{2,1,0:T(8,128)(2,1)}, bf16[2,64,384]{2,1,0:T(8,128)(2,1)}, u32[]{:S(2)}, u32[]{:S(2)}) collective-permute-start(bf16[2,64,384]{2,1,0:T(8,128)(2,1)} %slice.56), channel_id=1, source_target_pairs={{0,7},{1,0},{2,1},{3,2},{4,3},{5,4},{6,5},{7,6},{8,15},{9,8},{10,9... | collective-permute-start | bytes 294920 | tf_op jit(solution)/shard_map/ppermute | solution.py:107
  65.9 0.9 %copy-start.7 = (bf16[4,64,384]{2,1,0:T(8,128)(2,1)S(1)}, bf16[4,64,384]{2,1,0:T(8,128)(2,1)}, u32[]{:S(2)}) copy-start(bf16[4,64,384]{2,1,0:T(8,128)(2,1)} %copy-done.6) | copy-start | bytes 589828
  66.9 0.9 %copy-start.9 = (bf16[4,64,384]{2,1,0:T(8,128)(2,1)S(1)}, bf16[4,64,384]{2,1,0:T(8,128)(2,1)}, u32[]{:S(2)}) copy-start(bf16[4,64,384]{2,1,0:T(8,128)(2,1)} %copy-done.8) | copy-start | bytes 589828

commit v2 on v0

v2 whole, which is shorter than its diff:
```python
import math

import jax
import jax.numpy as jnp
from jax import lax
from jax.experimental import pallas as pl
from jax.experimental.pallas import tpu as pltpu
from jax.sharding import PartitionSpec as P

BF = jnp.bfloat16
F32 = jnp.float32
CAP = 64
NX = NY = 4
NZ = 8


ODD_LINKS = [(z, (z + 1) % NZ if z % 2 else (z - 1) % NZ) for z in range(NZ)]
EVEN_LINKS = [(z, (z - 1) % NZ if z % 2 else (z + 1) % NZ) for z in range(NZ)]


def line(first, flip):
    pairs = []
    for x in range(NX):
        for y in range(NY):
            for c in range(2):
                along_x = (c == 0) == first
                to_x = x ^ flip if along_x else x
                to_y = y if along_x else y ^ flip
                pairs.append(((x * NY + y) * 2 + c, (to_x * NY + to_y) * 2 + c))
    return pairs


SWAP = [(d, d ^ 1) for d in range(2 * NX * NY)]


def pick_matrix(pos, base_ref):
    rows = lax.broadcasted_iota(jnp.int32, (CAP, pos.shape[1]), 0) + base_ref[0]
    return (rows == pos).astype(F32).astype(BF)


def pack_t_kernel(base_ref, labels_ref, t_ref, out_ref, pos_ref, fits_ref):
    labels = labels_ref[...]
    pos = lax.broadcasted_iota(jnp.int32, labels.shape, 1)
    for g in range(1, 8):
        first = jnp.sum((labels < g).astype(F32), axis=1, keepdims=True).astype(jnp.int32)
        pos -= jnp.where(labels == g, first, 0)
    pos_ref[...] = pos
    fits_ref[0] = jnp.max(pos) + 1
    pick = pick_matrix(pos, base_ref)
    none = jnp.zeros_like(pick)
    ni, na, v = t_ref.shape
    half = ni // 2
    low = t_ref[:half].reshape(half * na, v)
    high = t_ref[half:].reshape(half * na, v)
    dims = (((1,), (1,)), ((), ()))
    both = lax.dot_general(low, jnp.concatenate([pick, none], 0), dims, preferred_element_type=F32)
    both += lax.dot_general(high, jnp.concatenate([none, pick], 0), dims, preferred_element_type=F32)
    out_ref[0] = both.astype(BF).reshape(half, na, 2 * CAP)


def pack_w_kernel(base_ref, pos_ref, w_ref, keep_ref, give_ref):
    pick = pick_matrix(pos_ref[...], base_ref)
    core = lax.axis_index("tr") % 2
    for e in range(keep_ref.shape[1]):
        keep_ref[0, e] = jnp.dot(pick, w_ref[2 * e + core], preferred_element_type=F32).astype(BF)
        give_ref[0, e] = jnp.dot(pick, w_ref[2 * e + 1 - core], preferred_element_type=F32).astype(BF)


SMEM = pl.BlockSpec(memory_space=pltpu.SMEM)
VMEM = pl.BlockSpec(memory_space=pltpu.VMEM)
ANY = pl.BlockSpec(memory_space=pl.ANY)


def pack_t(labels_row, base, t):
    ni, na, v = t.shape
    return pl.pallas_call(
        pack_t_kernel,
        out_shape=(
            jax.ShapeDtypeStruct((1, ni // 2, na, 2 * CAP), BF),
            jax.ShapeDtypeStruct(labels_row.shape, jnp.int32),
            jax.ShapeDtypeStruct((1,), jnp.int32),
        ),
        in_specs=[SMEM, VMEM, VMEM],
        out_specs=(VMEM, VMEM, SMEM),
        compiler_params=pltpu.CompilerParams(vmem_limit_bytes=8 * 2**20),
        cost_estimate=pl.CostEstimate(flops=0, bytes_accessed=2 * 2**20, transcendentals=0),
        name="pack_t",
    )(base, labels_row, t)


def pack_w(pos, base, w):
    nk, v, _ = w.shape
    part = jax.ShapeDtypeStruct((1, nk // 2, CAP, v), BF)
    return pl.pallas_call(
        pack_w_kernel,
        out_shape=(part, part),
        in_specs=[SMEM, VMEM, VMEM],
        out_specs=(VMEM, VMEM),
        compiler_params=pltpu.CompilerParams(vmem_limit_bytes=8 * 2**20),
        cost_estimate=pl.CostEstimate(flops=0, bytes_accessed=4 * 2**20, transcendentals=0),
        name="pack_w",
    )(base, pos, w)


OFFSETS = (0, 1, -1, 2, -2, 3, -3, 4)


def join_kernel(*refs):
    out_ref = refs[-1]
    at = 0
    for ref in refs[:-1]:
        out_ref[at : at + ref.shape[0]] = ref[...]
        at += ref.shape[0]


def join(name, *parts):
    shape = (sum(p.shape[0] for p in parts), *parts[0].shape[1:])
    size = 2 * 4 * math.prod(shape)
    return pl.pallas_call(
        join_kernel,
        out_shape=jax.ShapeDtypeStruct(shape, parts[0].dtype),
        in_specs=[VMEM] * len(parts),
        out_specs=VMEM,
        compiler_params=pltpu.CompilerParams(vmem_limit_bytes=8 * 2**20),
        cost_estimate=pl.CostEstimate(flops=0, bytes_accessed=size, transcendentals=0),
        name=name,
    )(*parts)


def lines(piece, first):
    return [lax.ppermute(piece, "tr", line(first, flip)) for flip in (1, 2, 3)]


def gather(keep, give, t):
    rows = lines(t, True)
    d = join("join_w", keep, lax.ppermute(give, "tr", SWAP))
    a1 = lax.ppermute(d, "su", ODD_LINKS)
    b1 = lax.ppermute(d, "su", EVEN_LINKS)
    row = join("join_row", t, *rows)
    planes = lines(row, False)
    a2 = lax.ppermute(b1, "su", ODD_LINKS)
    b2 = lax.ppermute(a1, "su", EVEN_LINKS)
    a3 = lax.ppermute(b2, "su", ODD_LINKS)
    b3 = lax.ppermute(a2, "su", EVEN_LINKS)
    a4 = lax.ppermute(b3[:1], "su", ODD_LINKS)
    b4 = lax.ppermute(a3[1:], "su", EVEN_LINKS)
    a4, b4 = lax.optimization_barrier((a4, b4))
    return [row, *planes], [d, a1, b1, a2, b2, a3, b3], a4, b4


def first_kernel(*refs):
    t_refs, d_refs, (own_ref, other_ref, rest_ref, t_all, t_cat, d_cat, sems) = refs[:4], refs[4:-7], refs[-7:]
    copies = [pltpu.make_async_copy(t_ref, t_all.at[NX * n : NX * n + NX], sems.at[n]) for n, t_ref in enumerate(t_refs)]
    for copy in copies:
        copy.start()
    _, ne, cap, v = d_refs[0].shape
    half_i, na = t_all.shape[1:3]
    rows = half_i * na
    wide = ne * cap
    for n, d_ref in enumerate(d_refs):
        for j in range(2):
            d_cat[j, n * wide : (n + 1) * wide] = d_ref[j].reshape(wide, v)
    tr = lax.axis_index("tr")
    z = lax.axis_index("su")
    x, y, core = tr // (2 * NY), (tr // 2) % NY, tr % 2
    way = 1 - 2 * (z % 2)
    for copy in copies:
        copy.wait()
    for n, off in enumerate(OFFSETS):
        block = (z - off * way + NZ) % NZ
        pair = []
        for e in range(ne):
            chip = block * ne + e
            dx = jnp.bitwise_xor(chip // NY, x)
            dy = jnp.bitwise_xor(chip % NY, y)
            at = jnp.where(core == 0, dy * NX + dx, dx * NY + dy)
            pair.append(t_all[at].reshape(rows, 2 * CAP))
        for h in range(2):
            lanes = slice(h * CAP, (h + 1) * CAP)
            both = jnp.concatenate([pair[0][:, lanes], pair[1][:, lanes]], 1)
            if n < len(d_refs):
                t_cat[h, :, n * wide : (n + 1) * wide] = both
            else:
                rest_ref[h] = both
    for h in range(2):
        other_ref[h] = jnp.dot(t_cat[h], d_cat[1], preferred_element_type=F32)
        own_ref[h] = jnp.dot(t_cat[h], d_cat[0], preferred_element_type=F32)


def first_part(t_parts, d_parts):
    chips, half_i, na, lanes = t_parts[0].shape
    _, ne, cap, v = d_parts[0].shape
    rows = half_i * na
    wide = ne * cap
    depth = len(d_parts) * wide
    sums = jax.ShapeDtypeStruct((2, rows, v), F32)
    return pl.pallas_call(
        first_kernel,
        out_shape=(sums, sums, jax.ShapeDtypeStruct((2, rows, wide), BF)),
        in_specs=[ANY] * len(t_parts) + [VMEM] * len(d_parts),
        out_specs=(VMEM, VMEM, VMEM),
        scratch_shapes=[
            pltpu.VMEM((len(t_parts) * chips, half_i, na, lanes), BF),
            pltpu.VMEM((2, rows, depth), BF),
            pltpu.VMEM((2, depth, v), BF),
            pltpu.SemaphoreType.DMA((len(t_parts),)),
        ],
        compiler_params=pltpu.CompilerParams(vmem_limit_bytes=20 * 2**20),
        cost_estimate=pl.CostEstimate(flops=8 * rows * v * depth, bytes_accessed=8 * 2**20, transcendentals=0),
        name="first_part",
    )(*t_parts, *d_parts)


def block_sum(sums_ref, rest_ref, d_ref, h):
    _, ne, cap, v = d_ref.shape
    return sums_ref[h] + jnp.dot(rest_ref[h], d_ref[0].reshape(ne * cap, v), preferred_element_type=F32)


def other_kernel(other_ref, rest_ref, d_ref, out_ref):
    for h in range(2):
        out_ref[h] = block_sum(other_ref, rest_ref, d_ref, h)


def other_part(other, rest, d):
    return pl.pallas_call(
        other_kernel,
        out_shape=jax.ShapeDtypeStruct(other.shape, F32),
        in_specs=[VMEM] * 3,
        out_specs=VMEM,
        compiler_params=pltpu.CompilerParams(vmem_limit_bytes=8 * 2**20),
        name="other_part",
    )(other, rest, d)


def last_kernel(occ_ref, labels_ref, fits_ref, own_ref, got_ref, rest_ref, d_ref, out_ref, flag_ref):
    flag_ref[0] = (fits_ref[0] <= CAP).astype(jnp.int32)
    label_j = occ_ref[lax.axis_index("tr")]
    half_i = out_ref.shape[0] // 2
    na, v = out_ref.shape[1:]
    labels = labels_ref[...]
    place = lax.broadcasted_iota(jnp.int32, (na, v), 0) + lax.axis_index("su") * na
    here = lax.broadcasted_iota(jnp.int32, (na, v), 1) == place
    labels_a = jnp.sum(jnp.where(here, labels, 0).astype(F32), axis=1, keepdims=True).astype(jnp.int32)
    plane = jnp.bitwise_xor(labels_a, labels)
    for h in range(2):
        sums = block_sum(own_ref, rest_ref, d_ref, h) + got_ref[h]
        for u in range(half_i):
            i = h * half_i + u
            keep = plane == jnp.bitwise_xor(occ_ref[i], label_j)
            out_ref[i] = jnp.where(keep, sums[u * na : (u + 1) * na], 0.0).astype(BF)


def window_kernel(total_ref, own_ref, got_ref, rest_ref, d_ref, out_ref):
    for h in range(2):
        out_ref[h] = total_ref[h] + block_sum(own_ref, rest_ref, d_ref, h) + got_ref[h]


def body(amplitudes, integrals, occupied_irreps, virtual_irreps):
    ni, _, na, v = amplitudes.shape
    t = amplitudes.reshape(ni, na, v)
    w = integrals.reshape(integrals.shape[0], v, v)
    labels_row = virtual_irreps.reshape(1, v)

    def one_pass(base):
        base = jnp.full((1,), base, jnp.int32)
        packed, pos, width = pack_t(labels_row, base, t)
        keep, give = pack_w(pos, base, w)
        t_parts, d_parts, a4, b4 = gather(keep, give, packed)
        own, other, rest = first_part(t_parts, d_parts)
        got = lax.ppermute(other_part(other, rest, b4), "tr", SWAP)
        return own, got, rest, a4, width

    own, got, rest, a4, width = one_pass(0)
    fast, fits = pl.pallas_call(
        last_kernel,
        out_shape=(jax.ShapeDtypeStruct((ni, na, v), BF), jax.ShapeDtypeStruct((1,), jnp.int32)),
        in_specs=[SMEM, VMEM, SMEM] + [VMEM] * 4,
        out_specs=(VMEM, SMEM),
        compiler_params=pltpu.CompilerParams(vmem_limit_bytes=8 * 2**20),
        name="last_part",
    )(occupied_irreps, labels_row, width, own, got, rest, a4)

    def all_windows():
        def window(n, total):
            own, got, rest, a4, _ = one_pass(n * CAP)
            return pl.pallas_call(
                window_kernel,
                out_shape=jax.ShapeDtypeStruct(total.shape, F32),
                in_specs=[VMEM] * 5,
                out_specs=VMEM,
                compiler_params=pltpu.CompilerParams(vmem_limit_bytes=16 * 2**20),
                name="window_part",
            )(total, own, got, rest, a4)

        windows = (width[0] + CAP - 1) // CAP
        total = lax.fori_loop(0, windows, window, jnp.zeros(own.shape, F32))
        label_j = occupied_irreps[lax.axis_index("tr")]
        labels_a = lax.dynamic_slice_in_dim(virtual_irreps, lax.axis_index("su") * na, na, 0)
        parity = jnp.bitwise_xor(occupied_irreps[:ni, None, None], label_j)
        parity = jnp.bitwise_xor(parity, labels_a[None, :, None])
        keep = jnp.bitwise_xor(parity, virtual_irreps[None, None, :]) == 0
        return jnp.where(keep, total.reshape(ni, na, v).astype(BF), jnp.zeros((), BF))

    out = lax.cond(fits[0] == 1, lambda: fast, all_windows)
    return out.reshape(ni, 1, na, v)


def solution(mesh):
    return jax.shard_map(
        body,
        mesh=mesh,
        in_specs=(P(None, "tr", "su", None), P("su", None, "tr", None), P(), P()),
        out_specs=P(None, "tr", "su", None),
        check_vma=False,
    )
```

time: 225 us -> 51.1 us (0.23)
  waiting for transfers between devices: 191 us -> 16.6 us
  starting transfers between devices: 0.04 us -> 23.6 us
  matrix products: 17.3 us -> 0 us
  between operations: 13.4 us -> 0.85 us
  Pallas kernels: 0 us -> 8.9 us
    all_gather x2 -> x0, waiting for transfers between devices: 190 us -> none  [the longest x1 106 us: body(): lax.all_gather(integrals, 'su', axis=0, tiled=True)]
    ppermute x0 -> x16, starting transfers between devices: none -> 23.6 us  [the longest x6 8 us: lines(): return [lax.ppermute(piece, 'tr', line(first, flip)) for flip in (1, 2, 3)]]
    dot_general x1 -> x0, matrix products: 17.3 us -> none  [body(): jnp.einsum('ikac,kcjb->ijab', whole_amps, lax.all_gather(integrals, 'su',...]
    ppermute x0 -> x16, waiting for transfers between devices: none -> 16.6 us  [the longest x6 8.8 us: lines(): return [lax.ppermute(piece, 'tr', line(first, flip)) for flip in (1, 2, 3)]]
    pallas_call x0 -> x7, Pallas kernels: none -> 8.9 us  [the longest x1 2.73 us: first_part(): pl.pallas_call(first_kernel, out_shape=(sums, sums, jax.ShapeDtypeStruct(...]
  transfers between devices with their start and end apart: 2 -> 16, of which waited for: 2 -> 8; matrix products, arithmetic and copies ran while one was open for 1% -> 0% of each run, Pallas kernels for 0% -> 5%
where the time goes in v2:
time: 51.1 us; the launch traced here: 50.9 us
  starting transfers between devices  23.6 us (46%)
  waiting for transfers between devices  16.6 us (32%)
  Pallas kernels  8.9 us (17%)
  between operations  0.85 us (2%)
  local copies, waits for them, and re-layouts  0.71 us (1%)
    ppermute x6, waiting for transfers between devices, lines(): return [lax.ppermute(piece, 'tr', line(first, flip)) for flip in (1, 2, 3)]  8.8 us
    ppermute x6, starting transfers between devices, lines(): return [lax.ppermute(piece, 'tr', line(first, flip)) for flip in (1, 2, 3)]  8 us
    ppermute x1, starting transfers between devices, gather(): a1 = lax.ppermute(d, 'su', ODD_LINKS)  4.54 us
    ppermute x1, starting transfers between devices, one_pass(): got = lax.ppermute(other_part(other, rest, b4), 'tr', SWAP)  4.13 us
    ppermute x1, waiting for transfers between devices, gather(): b3 = lax.ppermute(a2, 'su', EVEN_LINKS)  3.48 us
    ppermute x1, starting transfers between devices, gather(): d = join('join_w', keep, lax.ppermute(give, 'tr', SWAP))  3.33 us
    pallas_call x1, Pallas kernels, first_part(): pl.pallas_call(first_kernel, out_shape=(sums, sums, jax.ShapeDtypeStruct(...  2.73 us
    ppermute x1, waiting for transfers between devices, one_pass(): got = lax.ppermute(other_part(other, rest, b4), 'tr', SWAP)  2.47 us
  transfers between devices with their start and end apart: 16, of which 8 were waited for; matrix products, arithmetic and copies ran while one was open for 0% of the time, Pallas kernels for 5%

profile of v2, /device:TPU:1, one launch (start us, length us, event | category | flops | bytes accessed | tf_op | source)
XLA Modules:
  0.0 50.9 jit_solution(6571775378274343338)
XLA Ops:
  0.0 0.7 %reshape.69.labels_ref = s32[1,384]{1,0:T(1,128)S(1)} reshape(s32[384]{0:T(512)} %param.11) | data formatting | bytes 3072 | tf_op jit(solution)/shard_map/reshape | solution.py:262
  0.7 1.9 %pack_t.2 = (bf16[1,8,48,128]{3,2,1,0:T(8,128)(2,1)S(1)}, s32[1,384]{1,0:T(1,128)S(1)}, s32[1]{0:T(128)}) custom-call(s32[1]{0:T(128)} %constant.49.clone.1.base_ref, s32[1,384]{1,0:T(1,128)S(1)} %reshape.69.labels_ref, bf16[16,48,384]{2,1,0:T(8,128)(2,1)} %bitcast.8.t_ref), custom_call_target="tpu_custom_call" | custom-call | bytes 2097152 | tf_op jit(solution)/shard_map/pack_t/pallas_call | solution.py:76
  2.6 1.6 %pack_w.2 = (bf16[1,2,64,384]{3,2,1,0:T(8,128)(2,1)S(1)}, bf16[1,2,64,384]{3,2,1,0:T(8,128)(2,1)S(1)}) custom-call(s32[1]{0:T(128)} %constant.49.clone.1.base_ref, s32[1,384]{1,0:T(1,128)S(1)} %get-tuple-element.85.pos_ref, bf16[4,384,384]{2,1,0:T(8,128)(2,1)} %bitcast.9.w_ref), custom_call_target="tpu_custom_call" | custom-call | bytes 4194304 | tf_op jit(solution)/shard_map/pack_w/pallas_call | solution.py:94
  4.2 3.3 %collective-permute-start.22 = (bf16[1,2,64,384]{3,2,1,0:T(8,128)(2,1)S(1)}, bf16[1,2,64,384]{3,2,1,0:T(8,128)(2,1)S(1)}, u32[]{:S(2)}, u32[]{:S(2)}) collective-permute-start(bf16[1,2,64,384]{3,2,1,0:T(8,128)(2,1)S(1)} %get-tuple-element.87), channel_id=1, source_target_pairs={{0,8},{8,0},{16,24},{24,16},{32,40},{40,32},{48,56},{56,48},{64,72... | collective-permute-start | bytes 294920 | tf_op jit(solution)/shard_map/ppermute | solution.py:136
  7.5 0.9 %collective-permute-done.22.refs_1_ = bf16[1,2,64,384]{3,2,1,0:T(8,128)(2,1)S(1)} collective-permute-done((bf16[1,2,64,384]{3,2,1,0:T(8,128)(2,1)S(1)}, bf16[1,2,64,384]{3,2,1,0:T(8,128)(2,1)S(1)}, u32[]{:S(2)}, u32[]{:S(2)}) %collective-permute-start.22) | collective-permute-done | bytes 98336 | tf_op jit(solution)/shard_map/ppermute | solution.py:136
  8.5 0.1 collective-permute-start.24
  8.6 4.5 %collective-permute-start.23 = (bf16[2,2,64,384]{3,2,1,0:T(8,128)(2,1)S(1)}, bf16[2,2,64,384]{3,2,1,0:T(8,128)(2,1)S(1)}, u32[]{:S(2)}, u32[]{:S(2)}) collective-permute-start(bf16[2,2,64,384]{3,2,1,0:T(8,128)(2,1)S(1)} %join_w.2.refs_4_), channel_id=1, source_target_pairs={{0,7},{1,2},{2,1},{3,4},{4,3},{5,6},{6,5},{7,0},{8,15},{9,10},{10,... | collective-permute-start | bytes 589832 | tf_op jit(solution)/shard_map/ppermute | solution.py:137
  13.1 1.3 %collective-permute-start.16 = (bf16[1,8,48,128]{3,2,1,0:T(8,128)(2,1)S(1)}, bf16[1,8,48,128]{3,2,1,0:T(8,128)(2,1)S(1)}, u32[]{:S(2)}, u32[]{:S(2)}) collective-permute-start(bf16[1,8,48,128]{3,2,1,0:T(8,128)(2,1)S(1)} %get-tuple-element.84.refs_0_), channel_id=1, source_target_pairs={{0,64},{8,24},{16,80},{24,8},{32,96},{40,56},{48,112},{56,40},{64,... | collective-permute-start | bytes 294920 | tf_op jit(solution)/shard_map/ppermute | solution.py:131
  14.4 2.6 %collective-permute-start.17 = (bf16[1,8,48,128]{3,2,1,0:T(8,128)(2,1)S(1)}, bf16[1,8,48,128]{3,2,1,0:T(8,128)(2,1)S(1)}, u32[]{:S(2)}, u32[]{:S(2)}) collective-permute-start(bf16[1,8,48,128]{3,2,1,0:T(8,128)(2,1)S(1)} %get-tuple-element.84.refs_0_), channel_id=1, source_target_pairs={{0,128},{8,40},{16,144},{24,56},{32,160},{40,8},{48,176},{56,24},{... | collective-permute-start | bytes 294920 | tf_op jit(solution)/shard_map/ppermute | solution.py:131
  17.1 0.0 collective-permute-start.18
  17.1 0.0 collective-permute-done.24.refs_6_
  17.1 1.5 %collective-permute-start.25 = (bf16[2,2,64,384]{3,2,1,0:T(8,128)(2,1)S(1)}, bf16[2,2,64,384]{3,2,1,0:T(8,128)(2,1)S(1)}, u32[]{:S(2)}, u32[]{:S(2)}) collective-permute-start(bf16[2,2,64,384]{3,2,1,0:T(8,128)(2,1)S(1)} %collective-permute-done.24.refs_6_), channel_id=1, source_target_pairs={{0,7},{1,2},{2,1},{3,4},{4,3},{5,6},{6,5},{7,0},{8,15},{9,10},{10,... | collective-permute-start | bytes 589832 | tf_op jit(solution)/shard_map/ppermute | solution.py:141
  18.6 0.0 collective-permute-done.16.refs_1_
  18.6 1.6 %collective-permute-done.17.refs_2_ = bf16[1,8,48,128]{3,2,1,0:T(8,128)(2,1)S(1)} collective-permute-done((bf16[1,8,48,128]{3,2,1,0:T(8,128)(2,1)S(1)}, bf16[1,8,48,128]{3,2,1,0:T(8,128)(2,1)S(1)}, u32[]{:S(2)}, u32[]{:S(2)}) %collective-permute-start.17) | collective-permute-done | bytes 98336 | tf_op jit(solution)/shard_map/ppermute | solution.py:131
  20.1 1.6 %collective-permute-done.18.refs_3_ = bf16[1,8,48,128]{3,2,1,0:T(8,128)(2,1)S(1)} collective-permute-done((bf16[1,8,48,128]{3,2,1,0:T(8,128)(2,1)S(1)}, bf16[1,8,48,128]{3,2,1,0:T(8,128)(2,1)S(1)}, u32[]{:S(2)}, u32[]{:S(2)}) %collective-permute-start.18) | collective-permute-done | bytes 98336 | tf_op jit(solution)/shard_map/ppermute | solution.py:131
  21.8 1.6 %collective-permute-start.19 = (bf16[4,8,48,128]{3,2,1,0:T(8,128)(2,1)S(1)}, bf16[4,8,48,128]{3,2,1,0:T(8,128)(2,1)S(1)}, u32[]{:S(2)}, u32[]{:S(2)}) collective-permute-start(bf16[4,8,48,128]{3,2,1,0:T(8,128)(2,1)S(1)} %join_row.2.refs_0_), channel_id=1, source_target_pairs={{0,16},{8,72},{16,0},{24,88},{32,48},{40,104},{48,32},{56,120},{64... | collective-permute-start | bytes 1179656 | tf_op jit(solution)/shard_map/ppermute | solution.py:131
  23.4 2.2 %collective-permute-start.20 = (bf16[4,8,48,128]{3,2,1,0:T(8,128)(2,1)S(1)}, bf16[4,8,48,128]{3,2,1,0:T(8,128)(2,1)S(1)}, u32[]{:S(2)}, u32[]{:S(2)}) collective-permute-start(bf16[4,8,48,128]{3,2,1,0:T(8,128)(2,1)S(1)} %join_row.2.refs_0_), channel_id=1, source_target_pairs={{0,32},{8,136},{16,48},{24,152},{32,0},{40,168},{48,16},{56,184},{... | collective-permute-start | bytes 1179656 | tf_op jit(solution)/shard_map/ppermute | solution.py:131
  25.5 0.3 collective-permute-start.21
  25.9 1.3 %collective-permute-start.27 = (bf16[2,2,64,384]{3,2,1,0:T(8,128)(2,1)S(1)}, bf16[2,2,64,384]{3,2,1,0:T(8,128)(2,1)S(1)}, u32[]{:S(2)}, u32[]{:S(2)}) collective-permute-start(bf16[2,2,64,384]{3,2,1,0:T(8,128)(2,1)S(1)} %collective-permute-done.26.refs_8_), channel_id=1, source_target_pairs={{0,7},{1,2},{2,1},{3,4},{4,3},{5,6},{6,5},{7,0},{8,15},{9,10},{10,... | collective-permute-start | bytes 589832 | tf_op jit(solution)/shard_map/ppermute | solution.py:143
  27.2 3.5 %collective-permute-done.28.refs_10_ = bf16[2,2,64,384]{3,2,1,0:T(8,128)(2,1)S(1)} collective-permute-done((bf16[2,2,64,384]{3,2,1,0:T(8,128)(2,1)S(1)}, bf16[2,2,64,384]{3,2,1,0:T(8,128)(2,1)S(1)}, u32[]{:S(2)}, u32[]{:S(2)}) %collective-permute-start.28) | collective-permute-done | bytes 196640 | tf_op jit(solution)/shard_map/ppermute | solution.py:144
  30.7 0.1 collective-permute-start.29
  30.8 0.9 %collective-permute-done.27.refs_9_ = bf16[2,2,64,384]{3,2,1,0:T(8,128)(2,1)S(1)} collective-permute-done((bf16[2,2,64,384]{3,2,1,0:T(8,128)(2,1)S(1)}, bf16[2,2,64,384]{3,2,1,0:T(8,128)(2,1)S(1)}, u32[]{:S(2)}, u32[]{:S(2)}) %collective-permute-start.27) | collective-permute-done | bytes 196640 | tf_op jit(solution)/shard_map/ppermute | solution.py:143
  31.7 0.5 %collective-permute-start.30 = (bf16[1,2,64,384]{3,2,1,0:T(8,128)(2,1)S(1)}, bf16[1,2,64,384]{3,2,1,0:T(8,128)(2,1)S(1)}, u32[]{:S(2)}, u32[]{:S(2)}) collective-permute-start(bf16[1,2,64,384]{3,2,1,0:T(8,128)(2,1)S(1)} %slice.20), channel_id=1, source_target_pairs={{0,1},{1,0},{2,3},{3,2},{4,5},{5,4},{6,7},{7,6},{8,9},{9,8},{10,11... | collective-permute-start | bytes 294920 | tf_op jit(solution)/shard_map/ppermute | solution.py:146
  32.2 3.0 %collective-permute-done.20.refs_2_ = bf16[4,8,48,128]{3,2,1,0:T(8,128)(2,1)S(1)} collective-permute-done((bf16[4,8,48,128]{3,2,1,0:T(8,128)(2,1)S(1)}, bf16[4,8,48,128]{3,2,1,0:T(8,128)(2,1)S(1)}, u32[]{:S(2)}, u32[]{:S(2)}) %collective-permute-start.20) | collective-permute-done | bytes 393248 | tf_op jit(solution)/shard_map/ppermute | solution.py:131
  35.2 2.6 %collective-permute-done.21.refs_3_ = bf16[4,8,48,128]{3,2,1,0:T(8,128)(2,1)S(1)} collective-permute-done((bf16[4,8,48,128]{3,2,1,0:T(8,128)(2,1)S(1)}, bf16[4,8,48,128]{3,2,1,0:T(8,128)(2,1)S(1)}, u32[]{:S(2)}, u32[]{:S(2)}) %collective-permute-start.21) | collective-permute-done | bytes 393248 | tf_op jit(solution)/shard_map/ppermute | solution.py:131
  37.9 2.7 %first_part.2 = (f32[2,384,384]{2,1,0:T(8,128)S(1)}, f32[2,384,384]{2,1,0:T(8,128)S(1)}, bf16[2,384,128]{2,1,0:T(8,128)(2,1)S(1)}) custom-call(bf16[4,8,48,128]{3,2,1,0:T(8,128)(2,1)S(1)} %join_row.2.refs_0_, bf16[4,8,48,128]{3,2,1,0:T(8,128)(2,1)S(1)} %collective-permute-done.19.refs_1_, bf16[4,8,48,128]{3,2,1,0:T(8,128)(2,1)S(1)} %collective-permute-done.20.refs_2_, ...), custom_call_target="tpu_custom_call" | custom-call | flops 1056964608 | bytes 8388608 | tf_op jit(solution)/shard_map/first_part/pallas_call | solution.py:197
  40.6 0.0 copy-start.6
  40.6 0.3 other_part.2
  40.9 4.1 %collective-permute-start.31 = (f32[2,384,384]{2,1,0:T(8,128)S(1)}, f32[2,384,384]{2,1,0:T(8,128)S(1)}, u32[]{:S(2)}, u32[]{:S(2)}) collective-permute-start(f32[2,384,384]{2,1,0:T(8,128)S(1)} %other_part.2), channel_id=1, source_target_pairs={{0,8},{8,0},{16,24},{24,16},{32,40},{40,32},{48,56},{56,48},{64,72... | collective-permute-start | bytes 3538952 | tf_op jit(solution)/shard_map/ppermute | solution.py:270
  45.1 2.5 %collective-permute-done.31.got_ref = f32[2,384,384]{2,1,0:T(8,128)S(1)} collective-permute-done((f32[2,384,384]{2,1,0:T(8,128)S(1)}, f32[2,384,384]{2,1,0:T(8,128)S(1)}, u32[]{:S(2)}, u32[]{:S(2)}) %collective-permute-start.31) | collective-permute-done | bytes 1179680 | tf_op jit(solution)/shard_map/ppermute | solution.py:270
  47.5 2.3 %last_part.1 = (bf16[16,48,384]{2,1,0:T(8,128)(2,1)}, s32[1]{0:T(128)}) custom-call(s32[32]{0:T(128)S(1)} %copy-done.6, s32[1,384]{1,0:T(1,128)S(1)} %reshape.69.labels_ref, s32[1]{0:T(128)} %get-tuple-element.83.fits_ref, f32[2,384,384]{2,1,0:T(8,128)S(1)} %get-tuple-element.88.own_ref, f32[2,384,384]{2,1,0:T(8,128)S(1)} %collective-permute-done.31.got_ref, ...), custom_call_target="tpu_custom_call" | custom-call | tf_op jit(solution)/shard_map/last_part/pallas_call | solution.py:274
  50.5 0.2 conditional.1
  (15 shorter events, 0.1 us)
Async XLA Ops:
  4.2 4.3 %collective-permute-start.22 = (bf16[1,2,64,384]{3,2,1,0:T(8,128)(2,1)S(1)}, bf16[1,2,64,384]{3,2,1,0:T(8,128)(2,1)S(1)}, u32[]{:S(2)}, u32[]{:S(2)}) collective-permute-start(bf16[1,2,64,384]{3,2,1,0:T(8,128)(2,1)S(1)} %get-tuple-element.87), channel_id=1, source_target_pairs={{0,8},{8,0},{16,24},{24,16},{32,40},{40,32},{48,56},{56,48},{64,72... | collective-permute-start | bytes 294920 | tf_op jit(solution)/shard_map/ppermute | solution.py:136
  8.5 8.6 %collective-permute-start.24 = (bf16[2,2,64,384]{3,2,1,0:T(8,128)(2,1)S(1)}, bf16[2,2,64,384]{3,2,1,0:T(8,128)(2,1)S(1)}, u32[]{:S(2)}, u32[]{:S(2)}) collective-permute-start(bf16[2,2,64,384]{3,2,1,0:T(8,128)(2,1)S(1)} %join_w.2.refs_4_), channel_id=1, source_target_pairs={{0,1},{1,0},{2,3},{3,2},{4,5},{5,4},{6,7},{7,6},{8,9},{9,8},{10,11... | collective-permute-start | bytes 589832 | tf_op jit(solution)/shard_map/ppermute | solution.py:138
  8.6 10.0 %collective-permute-start.23 = (bf16[2,2,64,384]{3,2,1,0:T(8,128)(2,1)S(1)}, bf16[2,2,64,384]{3,2,1,0:T(8,128)(2,1)S(1)}, u32[]{:S(2)}, u32[]{:S(2)}) collective-permute-start(bf16[2,2,64,384]{3,2,1,0:T(8,128)(2,1)S(1)} %join_w.2.refs_4_), channel_id=1, source_target_pairs={{0,7},{1,2},{2,1},{3,4},{4,3},{5,6},{6,5},{7,0},{8,15},{9,10},{10,... | collective-permute-start | bytes 589832 | tf_op jit(solution)/shard_map/ppermute | solution.py:137
  13.1 5.4 %collective-permute-start.16 = (bf16[1,8,48,128]{3,2,1,0:T(8,128)(2,1)S(1)}, bf16[1,8,48,128]{3,2,1,0:T(8,128)(2,1)S(1)}, u32[]{:S(2)}, u32[]{:S(2)}) collective-permute-start(bf16[1,8,48,128]{3,2,1,0:T(8,128)(2,1)S(1)} %get-tuple-element.84.refs_0_), channel_id=1, source_target_pairs={{0,64},{8,24},{16,80},{24,8},{32,96},{40,56},{48,112},{56,40},{64,... | collective-permute-start | bytes 294920 | tf_op jit(solution)/shard_map/ppermute | solution.py:131
  14.4 5.7 %collective-permute-start.17 = (bf16[1,8,48,128]{3,2,1,0:T(8,128)(2,1)S(1)}, bf16[1,8,48,128]{3,2,1,0:T(8,128)(2,1)S(1)}, u32[]{:S(2)}, u32[]{:S(2)}) collective-permute-start(bf16[1,8,48,128]{3,2,1,0:T(8,128)(2,1)S(1)} %get-tuple-element.84.refs_0_), channel_id=1, source_target_pairs={{0,128},{8,40},{16,144},{24,56},{32,160},{40,8},{48,176},{56,24},{... | collective-permute-start | bytes 294920 | tf_op jit(solution)/shard_map/ppermute | solution.py:131
  17.1 4.7 %collective-permute-start.18 = (bf16[1,8,48,128]{3,2,1,0:T(8,128)(2,1)S(1)}, bf16[1,8,48,128]{3,2,1,0:T(8,128)(2,1)S(1)}, u32[]{:S(2)}, u32[]{:S(2)}) collective-permute-start(bf16[1,8,48,128]{3,2,1,0:T(8,128)(2,1)S(1)} %get-tuple-element.84.refs_0_), channel_id=1, source_target_pairs={{0,192},{8,56},{16,208},{24,40},{32,224},{40,24},{48,240},{56,8},{... | collective-permute-start | bytes 294920 | tf_op jit(solution)/shard_map/ppermute | solution.py:131
  17.1 8.8 %collective-permute-start.25 = (bf16[2,2,64,384]{3,2,1,0:T(8,128)(2,1)S(1)}, bf16[2,2,64,384]{3,2,1,0:T(8,128)(2,1)S(1)}, u32[]{:S(2)}, u32[]{:S(2)}) collective-permute-start(bf16[2,2,64,384]{3,2,1,0:T(8,128)(2,1)S(1)} %collective-permute-done.24.refs_6_), channel_id=1, source_target_pairs={{0,7},{1,2},{2,1},{3,4},{4,3},{5,6},{6,5},{7,0},{8,15},{9,10},{10,... | collective-permute-start | bytes 589832 | tf_op jit(solution)/shard_map/ppermute | solution.py:141
  18.5 7.3 %collective-permute-start.26 = (bf16[2,2,64,384]{3,2,1,0:T(8,128)(2,1)S(1)}, bf16[2,2,64,384]{3,2,1,0:T(8,128)(2,1)S(1)}, u32[]{:S(2)}, u32[]{:S(2)}) collective-permute-start(bf16[2,2,64,384]{3,2,1,0:T(8,128)(2,1)S(1)} %collective-permute-done.23.refs_5_), channel_id=1, source_target_pairs={{0,1},{1,0},{2,3},{3,2},{4,5},{5,4},{6,7},{7,6},{8,9},{9,8},{10,11... | collective-permute-start | bytes 589832 | tf_op jit(solution)/shard_map/ppermute | solution.py:142
  21.8 10.5 %collective-permute-start.19 = (bf16[4,8,48,128]{3,2,1,0:T(8,128)(2,1)S(1)}, bf16[4,8,48,128]{3,2,1,0:T(8,128)(2,1)S(1)}, u32[]{:S(2)}, u32[]{:S(2)}) collective-permute-start(bf16[4,8,48,128]{3,2,1,0:T(8,128)(2,1)S(1)} %join_row.2.refs_0_), channel_id=1, source_target_pairs={{0,16},{8,72},{16,0},{24,88},{32,48},{40,104},{48,32},{56,120},{64... | collective-permute-start | bytes 1179656 | tf_op jit(solution)/shard_map/ppermute | solution.py:131
  23.4 11.9 %collective-permute-start.20 = (bf16[4,8,48,128]{3,2,1,0:T(8,128)(2,1)S(1)}, bf16[4,8,48,128]{3,2,1,0:T(8,128)(2,1)S(1)}, u32[]{:S(2)}, u32[]{:S(2)}) collective-permute-start(bf16[4,8,48,128]{3,2,1,0:T(8,128)(2,1)S(1)} %join_row.2.refs_0_), channel_id=1, source_target_pairs={{0,32},{8,136},{16,48},{24,152},{32,0},{40,168},{48,16},{56,184},{... | collective-permute-start | bytes 1179656 | tf_op jit(solution)/shard_map/ppermute | solution.py:131
  25.5 12.3 %collective-permute-start.21 = (bf16[4,8,48,128]{3,2,1,0:T(8,128)(2,1)S(1)}, bf16[4,8,48,128]{3,2,1,0:T(8,128)(2,1)S(1)}, u32[]{:S(2)}, u32[]{:S(2)}) collective-permute-start(bf16[4,8,48,128]{3,2,1,0:T(8,128)(2,1)S(1)} %join_row.2.refs_0_), channel_id=1, source_target_pairs={{0,48},{8,200},{16,32},{24,216},{32,16},{40,232},{48,0},{56,248},{... | collective-permute-start | bytes 1179656 | tf_op jit(solution)/shard_map/ppermute | solution.py:131
  25.8 4.8 %collective-permute-start.28 = (bf16[2,2,64,384]{3,2,1,0:T(8,128)(2,1)S(1)}, bf16[2,2,64,384]{3,2,1,0:T(8,128)(2,1)S(1)}, u32[]{:S(2)}, u32[]{:S(2)}) collective-permute-start(bf16[2,2,64,384]{3,2,1,0:T(8,128)(2,1)S(1)} %collective-permute-done.25.refs_7_), channel_id=1, source_target_pairs={{0,1},{1,0},{2,3},{3,2},{4,5},{5,4},{6,7},{7,6},{8,9},{9,8},{10,11... | collective-permute-start | bytes 589832 | tf_op jit(solution)/shard_map/ppermute | solution.py:144
  25.9 5.8 %collective-permute-start.27 = (bf16[2,2,64,384]{3,2,1,0:T(8,128)(2,1)S(1)}, bf16[2,2,64,384]{3,2,1,0:T(8,128)(2,1)S(1)}, u32[]{:S(2)}, u32[]{:S(2)}) collective-permute-start(bf16[2,2,64,384]{3,2,1,0:T(8,128)(2,1)S(1)} %collective-permute-done.26.refs_8_), channel_id=1, source_target_pairs={{0,7},{1,2},{2,1},{3,4},{4,3},{5,6},{6,5},{7,0},{8,15},{9,10},{10,... | collective-permute-start | bytes 589832 | tf_op jit(solution)/shard_map/ppermute | solution.py:143
  30.7 9.9 %collective-permute-start.29 = (bf16[1,2,64,384]{3,2,1,0:T(8,128)(2,1)S(1)}, bf16[1,2,64,384]{3,2,1,0:T(8,128)(2,1)S(1)}, u32[]{:S(2)}, u32[]{:S(2)}) collective-permute-start(bf16[1,2,64,384]{3,2,1,0:T(8,128)(2,1)S(1)} %slice.19), channel_id=1, source_target_pairs={{0,7},{1,2},{2,1},{3,4},{4,3},{5,6},{6,5},{7,0},{8,15},{9,10},{10,... | collective-permute-start | bytes 294920 | tf_op jit(solution)/shard_map/ppermute | solution.py:145
  31.7 8.9 %collective-permute-start.30 = (bf16[1,2,64,384]{3,2,1,0:T(8,128)(2,1)S(1)}, bf16[1,2,64,384]{3,2,1,0:T(8,128)(2,1)S(1)}, u32[]{:S(2)}, u32[]{:S(2)}) collective-permute-start(bf16[1,2,64,384]{3,2,1,0:T(8,128)(2,1)S(1)} %slice.20), channel_id=1, source_target_pairs={{0,1},{1,0},{2,3},{3,2},{4,5},{5,4},{6,7},{7,6},{8,9},{9,8},{10,11... | collective-permute-start | bytes 294920 | tf_op jit(solution)/shard_map/ppermute | solution.py:146
  40.6 6.9 %copy-start.6 = (s32[32]{0:T(128)S(1)}, s32[32]{0:T(128)}, u32[]{:S(2)}) copy-start(s32[32]{0:T(128)} %occ_ref.1) | copy-start | bytes 388
  40.9 6.6 %collective-permute-start.31 = (f32[2,384,384]{2,1,0:T(8,128)S(1)}, f32[2,384,384]{2,1,0:T(8,128)S(1)}, u32[]{:S(2)}, u32[]{:S(2)}) collective-permute-start(f32[2,384,384]{2,1,0:T(8,128)S(1)} %other_part.2), channel_id=1, source_target_pairs={{0,8},{8,0},{16,24},{24,16},{32,40},{40,32},{48,56},{56,48},{64,72... | collective-permute-start | bytes 3538952 | tf_op jit(solution)/shard_map/ppermute | solution.py:270
  47.5 2.9 %copy-start.5 = (s32[384]{0:T(512)S(1)}, s32[384]{0:T(512)}, u32[]{:S(2)}) copy-start(s32[384]{0:T(512)} %param.11) | copy-start | bytes 4612

commit v3 on v2

v3 whole, which is shorter than its diff:
```python
import functools
import math

import jax
import jax.numpy as jnp
from jax import lax
from jax.experimental import pallas as pl
from jax.experimental.pallas import tpu as pltpu
from jax.sharding import PartitionSpec as P

BF = jnp.bfloat16
F32 = jnp.float32
IW = 16
CAP = 64
NX = NY = 4
NZ = 8


ODD_LINKS = [(z, (z + 1) % NZ if z % 2 else (z - 1) % NZ) for z in range(NZ)]
EVEN_LINKS = [(z, (z - 1) % NZ if z % 2 else (z + 1) % NZ) for z in range(NZ)]


def line(first, flip):
    pairs = []
    for x in range(NX):
        for y in range(NY):
            for c in range(2):
                along_x = (c == 0) == first
                to_x = x ^ flip if along_x else x
                to_y = y if along_x else y ^ flip
                pairs.append(((x * NY + y) * 2 + c, (to_x * NY + to_y) * 2 + c))
    return pairs


EVEN_LINKS_CROSSED = [(d * NZ + z, (d ^ 1) * NZ + to) for d in range(2 * NX * NY) for z, to in EVEN_LINKS]
SWAP = [(d, d ^ 1) for d in range(2 * NX * NY)]


def pick_matrix(pos, base):
    rows = lax.broadcasted_iota(jnp.int32, (CAP, pos.shape[1]), 0) + base
    return (rows == pos).astype(F32).astype(BF)


def group_positions(labels):
    pos = lax.broadcasted_iota(jnp.int32, labels.shape, 1)
    for g in range(1, 8):
        first = jnp.sum((labels < g).astype(F32), axis=1, keepdims=True).astype(jnp.int32)
        pos -= jnp.where(labels == g, first, 0)
    return pos


def give_kernel(window, labels_ref, w_ref, give_ref, pos_ref, width_ref, l_all, w_all, sems):
    base = 0 if window is None else window[0] * CAP
    ne = give_ref.shape[1]
    other = 1 - lax.axis_index("tr") % 2
    fetch_l = pltpu.make_async_copy(labels_ref, l_all, sems.at[ne])
    fetch_w = [pltpu.make_async_copy(w_ref.at[2 * e + other], w_all.at[e], sems.at[e]) for e in range(ne)]
    fetch_l.start()
    for copy in fetch_w:
        copy.start()
    fetch_l.wait()
    pos = group_positions(l_all[...].reshape(1, l_all.shape[0]))
    pos_ref[...] = pos
    width_ref[...] = jnp.full(width_ref.shape, 1, jnp.int32) + jnp.max(pos, axis=1, keepdims=True)
    pick = pick_matrix(pos, base)
    for e in range(ne):
        fetch_w[e].wait()
        give_ref[0, e] = jnp.dot(pick, w_all[e], preferred_element_type=F32).astype(BF)


def keep_kernel(window, pos_ref, t_ref, w_ref, row_ref, keep_ref, t_all, w_all, sems):
    base = 0 if window is None else window[0] * CAP
    ne = keep_ref.shape[1]
    core = lax.axis_index("tr") % 2
    fetch_w = [pltpu.make_async_copy(w_ref.at[2 * e + core], w_all.at[e], sems.at[e]) for e in range(ne)]
    fetch_t = pltpu.make_async_copy(t_ref, t_all, sems.at[ne])
    for copy in fetch_w:
        copy.start()
    fetch_t.start()
    pick = pick_matrix(pos_ref[...], base)
    none = jnp.zeros_like(pick)
    for e in range(ne):
        fetch_w[e].wait()
        keep_ref[0, e] = jnp.dot(pick, w_all[e], preferred_element_type=F32).astype(BF)
    fetch_t.wait()
    ni, na, v = t_all.shape
    half = ni // 2
    low = t_all[:half].reshape(half * na, v)
    high = t_all[half:].reshape(half * na, v)
    dims = (((1,), (1,)), ((), ()))
    both = lax.dot_general(low, jnp.concatenate([pick, none], 0), dims, preferred_element_type=F32)
    both += lax.dot_general(high, jnp.concatenate([none, pick], 0), dims, preferred_element_type=F32)
    row_ref[0] = both.astype(BF).reshape(half, na, 2 * CAP)


def bits_kernel(occ_ref, labels_ref, bits_ref):
    na, v = bits_ref.shape
    labels = labels_ref[...].reshape(1, v)
    place = lax.broadcasted_iota(jnp.int32, (na, v), 0) + lax.axis_index("su") * na
    here = lax.broadcasted_iota(jnp.int32, (na, v), 1) == place
    labels_a = jnp.sum(jnp.where(here, labels, 0).astype(F32), axis=1, keepdims=True).astype(jnp.int32)
    plane = jnp.bitwise_xor(jnp.bitwise_xor(labels_a, labels), occ_ref[lax.axis_index("tr")])
    bits = jnp.zeros((na, v), jnp.int32)
    for i in range(IW):
        bits += jnp.where(plane == occ_ref[i], 1 << i, 0)
    bits_ref[...] = bits


SMEM = pl.BlockSpec(memory_space=pltpu.SMEM)
VMEM = pl.BlockSpec(memory_space=pltpu.VMEM)
ANY = pl.BlockSpec(memory_space=pl.ANY)


def windowed(kernel, window):
    if window is None:
        return functools.partial(kernel, None), [], []
    return kernel, [SMEM], [window]


def pack_give(window, labels, w):
    nk, v, _ = w.shape
    kernel, specs, args = windowed(give_kernel, window)
    return pl.pallas_call(
        kernel,
        out_shape=(
            jax.ShapeDtypeStruct((1, nk // 2, CAP, v), BF),
            jax.ShapeDtypeStruct((1, v), jnp.int32),
            jax.ShapeDtypeStruct((1, 128), jnp.int32),
        ),
        in_specs=specs + [ANY, ANY],
        out_specs=(VMEM, VMEM, VMEM),
        scratch_shapes=[
            pltpu.VMEM((v,), jnp.int32),
            pltpu.VMEM((nk // 2, v, v), BF),
            pltpu.SemaphoreType.DMA((nk // 2 + 1,)),
        ],
        compiler_params=pltpu.CompilerParams(vmem_limit_bytes=8 * 2**20),
        name="pack_give",
    )(*args, labels, w)


def pack_keep(window, pos, t, w):
    nk, v, _ = w.shape
    ni, na, _ = t.shape
    kernel, specs, args = windowed(keep_kernel, window)
    return pl.pallas_call(
        kernel,
        out_shape=(
            jax.ShapeDtypeStruct((1, ni // 2, na, 2 * CAP), BF),
            jax.ShapeDtypeStruct((1, nk // 2, CAP, v), BF),
        ),
        in_specs=specs + [VMEM, ANY, ANY],
        out_specs=(VMEM, VMEM),
        scratch_shapes=[
            pltpu.VMEM(t.shape, BF),
            pltpu.VMEM((nk // 2, v, v), BF),
            pltpu.SemaphoreType.DMA((nk // 2 + 1,)),
        ],
        compiler_params=pltpu.CompilerParams(vmem_limit_bytes=8 * 2**20),
        cost_estimate=pl.CostEstimate(flops=0, bytes_accessed=4 * 2**20, transcendentals=0),
        name="pack_keep",
    )(*args, pos, t, w)


def symmetric_bits(occupied, labels, na):
    return pl.pallas_call(
        bits_kernel,
        out_shape=jax.ShapeDtypeStruct((na, labels.shape[0]), jnp.int32),
        in_specs=[SMEM, VMEM],
        out_specs=VMEM,
        compiler_params=pltpu.CompilerParams(vmem_limit_bytes=4 * 2**20),
        name="bits",
    )(occupied, labels)


OFFSETS = (0, 1, -1, 2, -2, 3, -3, 4)


def join_kernel(*refs):
    out_ref = refs[-1]
    at = 0
    for ref in refs[:-1]:
        out_ref[at : at + ref.shape[0]] = ref[...]
        at += ref.shape[0]


def join(name, *parts):
    shape = (sum(p.shape[0] for p in parts), *parts[0].shape[1:])
    size = 2 * 4 * math.prod(shape)
    return pl.pallas_call(
        join_kernel,
        out_shape=jax.ShapeDtypeStruct(shape, parts[0].dtype),
        in_specs=[VMEM] * len(parts),
        out_specs=VMEM,
        compiler_params=pltpu.CompilerParams(vmem_limit_bytes=8 * 2**20),
        cost_estimate=pl.CostEstimate(flops=0, bytes_accessed=size, transcendentals=0),
        name=name,
    )(*parts)


def lines(piece, first):
    return [lax.ppermute(piece, "tr", line(first, flip)) for flip in (1, 2, 3)]


def gather(keep, got, t):
    rows = lines(t, True)
    d = join("join_w", keep, got)
    a1 = lax.ppermute(d, "su", ODD_LINKS)
    b1 = lax.ppermute(d, "su", EVEN_LINKS)
    row = join("join_row", t, *rows)
    planes = lines(row, False)
    a2 = lax.ppermute(b1, "su", ODD_LINKS)
    b2 = lax.ppermute(a1, "su", EVEN_LINKS)
    a3 = lax.ppermute(b2, "su", ODD_LINKS)
    b3 = lax.ppermute(a2, "su", EVEN_LINKS)
    a4 = lax.ppermute(b3[:1], "su", ODD_LINKS)
    b4 = lax.ppermute(a3[1:], ("tr", "su"), EVEN_LINKS_CROSSED)
    return [row, *planes], [d, a1, b1, a2, b2, a3, b3], a4, b4


def blocks(d_refs, j, d_cat):
    _, ne, cap, v = d_refs[0].shape
    wide = ne * cap
    for n, d_ref in enumerate(d_refs):
        d_cat[n * wide : (n + 1) * wide] = d_ref[j].reshape(wide, v)


def other_kernel(*refs):
    t_refs, d_refs, (other_ref, t_cat, rest_ref, t_all, d_cat, sems) = refs[:4], refs[4:-6], refs[-6:]
    copies = [pltpu.make_async_copy(t_ref, t_all.at[NX * n : NX * n + NX], sems.at[n]) for n, t_ref in enumerate(t_refs)]
    for copy in copies:
        copy.start()
    _, ne, cap, v = d_refs[0].shape
    half_i, na = t_all.shape[1:3]
    rows = half_i * na
    wide = ne * cap
    blocks(d_refs, 1, d_cat)
    tr = lax.axis_index("tr")
    z = lax.axis_index("su")
    x, y, core = tr // (2 * NY), (tr // 2) % NY, tr % 2
    way = 1 - 2 * (z % 2)
    for copy in copies:
        copy.wait()
    for n, off in enumerate(OFFSETS):
        block = (z - off * way + NZ) % NZ
        pair = []
        for e in range(ne):
            chip = block * ne + e
            dx = jnp.bitwise_xor(chip // NY, x)
            dy = jnp.bitwise_xor(chip % NY, y)
            at = jnp.where(core == 0, dy * NX + dx, dx * NY + dy)
            pair.append(t_all[at].reshape(rows, 2 * CAP))
        for h in range(2):
            lanes = slice(h * CAP, (h + 1) * CAP)
            both = jnp.concatenate([pair[0][:, lanes], pair[1][:, lanes]], 1)
            if n < len(d_refs):
                t_cat[h, :, n * wide : (n + 1) * wide] = both
            else:
                rest_ref[h] = both
    for h in range(2):
        other_ref[h] = jnp.dot(t_cat[h], d_cat[...], preferred_element_type=F32)


def other_part(t_parts, d_parts):
    chips, half_i, na, lanes = t_parts[0].shape
    _, ne, cap, v = d_parts[0].shape
    rows = half_i * na
    wide = ne * cap
    depth = len(d_parts) * wide
    return pl.pallas_call(
        other_kernel,
        out_shape=(
            jax.ShapeDtypeStruct((2, rows, v), F32),
            jax.ShapeDtypeStruct((2, rows, depth), BF),
            jax.ShapeDtypeStruct((2, rows, wide), BF),
        ),
        in_specs=[ANY] * len(t_parts) + [VMEM] * len(d_parts),
        out_specs=(VMEM, VMEM, VMEM),
        scratch_shapes=[
            pltpu.VMEM((len(t_parts) * chips, half_i, na, lanes), BF),
            pltpu.VMEM((depth, v), BF),
            pltpu.SemaphoreType.DMA((len(t_parts),)),
        ],
        compiler_params=pltpu.CompilerParams(vmem_limit_bytes=20 * 2**20),
        cost_estimate=pl.CostEstimate(flops=4 * rows * v * depth, bytes_accessed=6 * 2**20, transcendentals=0),
        name="other_part",
    )(*t_parts, *d_parts)


def own_kernel(t_cat, *refs):
    d_refs, (own_ref, d_cat) = refs[:-2], refs[-2:]
    blocks(d_refs, 0, d_cat)
    for h in range(2):
        own_ref[h] = jnp.dot(t_cat[h], d_cat[...], preferred_element_type=F32)


def own_part(t_cat, d_parts):
    _, rows, depth = t_cat.shape
    v = d_parts[0].shape[3]
    return pl.pallas_call(
        own_kernel,
        out_shape=jax.ShapeDtypeStruct((2, rows, v), F32),
        in_specs=[VMEM] * (1 + len(d_parts)),
        out_specs=VMEM,
        scratch_shapes=[pltpu.VMEM((depth, v), BF)],
        compiler_params=pltpu.CompilerParams(vmem_limit_bytes=12 * 2**20),
        cost_estimate=pl.CostEstimate(flops=4 * rows * v * depth, bytes_accessed=4 * 2**20, transcendentals=0),
        name="own_part",
    )(t_cat, *d_parts)


def total(h, own_ref, got_ref, rest_ref, rest_got_ref, a4_ref, b4_ref):
    _, ne, cap, v = a4_ref.shape
    left = jnp.concatenate([rest_ref[h], rest_got_ref[h]], 1)
    right = jnp.concatenate([a4_ref[0].reshape(ne * cap, v), b4_ref[0].reshape(ne * cap, v)], 0)
    return own_ref[h] + got_ref[h] + jnp.dot(left, right, preferred_element_type=F32)


def last_kernel(width_ref, bits_ref, *refs):
    parts, (out_ref, fits_ref) = refs[:-2], refs[-2:]
    fits_ref[0] = (width_ref[0, 0] <= CAP).astype(jnp.int32)
    half_i = out_ref.shape[0] // 2
    na = out_ref.shape[1]
    for h in range(2):
        sums = total(h, *parts)
        for u in range(half_i):
            i = h * half_i + u
            keep = jnp.bitwise_and(bits_ref[...], 1 << i) != 0
            out_ref[i] = jnp.where(keep, sums[u * na : (u + 1) * na], 0.0).astype(BF)


def window_kernel(before_ref, *refs):
    parts, out_ref = refs[:-1], refs[-1]
    for h in range(2):
        out_ref[h] = before_ref[h] + total(h, *parts)


def body(amplitudes, integrals, occupied_irreps, virtual_irreps):
    ni, _, na, v = amplitudes.shape
    t = amplitudes.reshape(ni, na, v)
    w = integrals.reshape(integrals.shape[0], v, v)

    def one_pass(window):
        give, pos, width = pack_give(window, virtual_irreps, w)
        got = lax.ppermute(give, "tr", SWAP)
        row, keep = pack_keep(window, pos, t, w)
        t_parts, d_parts, a4, b4 = gather(keep, got, row)
        other, t_cat, rest = other_part(t_parts, d_parts)
        other, a4, b4 = lax.optimization_barrier((other, a4, b4))
        got = lax.ppermute(other, "tr", SWAP)
        rest_got = lax.ppermute(rest, "tr", SWAP)
        own = own_part(t_cat, d_parts)
        return (own, got, rest, rest_got, a4, b4), width

    parts, width = one_pass(None)
    fast, fits = pl.pallas_call(
        last_kernel,
        out_shape=(jax.ShapeDtypeStruct((ni, na, v), BF), jax.ShapeDtypeStruct((1,), jnp.int32)),
        in_specs=[VMEM, VMEM] + [VMEM] * len(parts),
        out_specs=(VMEM, SMEM),
        compiler_params=pltpu.CompilerParams(vmem_limit_bytes=8 * 2**20),
        name="last_part",
    )(width, symmetric_bits(occupied_irreps, virtual_irreps, na), *parts)

    def all_windows():
        def window(n, before):
            parts, _ = one_pass(jnp.full((1,), n, jnp.int32))
            return pl.pallas_call(
                window_kernel,
                out_shape=jax.ShapeDtypeStruct(before.shape, F32),
                in_specs=[VMEM] * (1 + len(parts)),
                out_specs=VMEM,
                compiler_params=pltpu.CompilerParams(vmem_limit_bytes=16 * 2**20),
                name="window_part",
            )(before, *parts)

        windows = (width[0, 0] + CAP - 1) // CAP
        sums = lax.fori_loop(0, windows, window, jnp.zeros(parts[0].shape, F32))
        label_j = occupied_irreps[lax.axis_index("tr")]
        labels_a = lax.dynamic_slice_in_dim(virtual_irreps, lax.axis_index("su") * na, na, 0)
        parity = jnp.bitwise_xor(occupied_irreps[:ni, None, None], label_j)
        parity = jnp.bitwise_xor(parity, labels_a[None, :, None])
        keep = jnp.bitwise_xor(parity, virtual_irreps[None, None, :]) == 0
        return jnp.where(keep, sums.reshape(ni, na, v).astype(BF), jnp.zeros((), BF))

    out = lax.cond(fits[0] == 1, lambda: fast, all_windows)
    return out.reshape(ni, 1, na, v)


def solution(mesh):
    return jax.shard_map(
        body,
        mesh=mesh,
        in_specs=(P(None, "tr", "su", None), P("su", None, "tr", None), P(), P()),
        out_specs=P(None, "tr", "su", None),
        check_vma=False,
    )
```

time: 51.1 us -> 46.8 us (0.916)
  waiting for transfers between devices: 16.6 us -> 9.49 us
  starting transfers between devices: 23.6 us -> 27.9 us
  Pallas kernels: 8.9 us -> 8 us
  local copies, waits for them, and re-layouts: 0.71 us -> 0.04 us
    ppermute x6, waiting for transfers between devices: 8.8 us -> 3.91 us  [lines(): return [lax.ppermute(piece, 'tr', line(first, flip)) for flip in (1, 2, 3)]]
    ppermute x3 -> x4, starting transfers between devices: 8.01 us -> 12 us  [the longest x1 5.03 us: gather(): b4 = lax.ppermute(a3[1:], ('tr', 'su'), EVEN_LINKS_CROSSED)]
    ppermute x3 -> x4, waiting for transfers between devices: 3.42 us -> 1.19 us  [the longest x1 0.93 us: one_pass(): rest_got = lax.ppermute(rest, 'tr', SWAP)]
    pallas_call x1, Pallas kernels: 2.34 us -> 1.21 us  [body(): pl.pallas_call(last_kernel, out_shape=(jax.ShapeDtypeStruct((ni, na, v),...]
    reshape x1 -> x0, local copies, waits for them, and re-layouts: 0.68 us -> none  [body(): labels_row = virtual_irreps.reshape(1, v)]
    pallas_call x4 -> x5, Pallas kernels: 6.52 us -> 6.74 us  [the longest x1 1.9 us: other_part(): pl.pallas_call(other_kernel, out_shape=(jax.ShapeDtypeStruct((2, rows, v)...]
  transfers between devices with their start and end apart: 16 -> 17, of which waited for: 8 -> 7; matrix products, arithmetic and copies ran while one was open for 0% -> 0% of each run, Pallas kernels for 5% -> 11%
where the time goes in v3:
time: 46.8 us; the launch traced here: 46.6 us
  starting transfers between devices  27.9 us (60%)
  waiting for transfers between devices  9.49 us (20%)
  Pallas kernels  8 us (17%)
  between operations  0.93 us (2%)
    ppermute x6, starting transfers between devices, lines(): return [lax.ppermute(piece, 'tr', line(first, flip)) for flip in (1, 2, 3)]  8 us
    ppermute x1, starting transfers between devices, gather(): b4 = lax.ppermute(a3[1:], ('tr', 'su'), EVEN_LINKS_CROSSED)  5.03 us
    ppermute x1, starting transfers between devices, gather(): a1 = lax.ppermute(d, 'su', ODD_LINKS)  4.54 us
    ppermute x6, waiting for transfers between devices, lines(): return [lax.ppermute(piece, 'tr', line(first, flip)) for flip in (1, 2, 3)]  3.91 us
    ppermute x1, starting transfers between devices, one_pass(): got = lax.ppermute(other, 'tr', SWAP)  3.56 us
    ppermute x1, waiting for transfers between devices, gather(): b3 = lax.ppermute(a2, 'su', EVEN_LINKS)  3.48 us
    ppermute x1, starting transfers between devices, one_pass(): got = lax.ppermute(give, 'tr', SWAP)  3.33 us
    pallas_call x1, Pallas kernels, other_part(): pl.pallas_call(other_kernel, out_shape=(jax.ShapeDtypeStruct((2, rows, v)...  1.9 us
  transfers between devices with their start and end apart: 17, of which 7 were waited for; matrix products, arithmetic and copies ran while one was open for 0% of the time, Pallas kernels for 11%

profile of v3, /device:TPU:1, one launch (start us, length us, event | category | flops | bytes accessed | tf_op | source)
XLA Modules:
  0.0 46.6 jit_solution(12749707160821731112)
XLA Ops:
  0.0 1.4 %pack_give.2 = (bf16[1,2,64,384]{3,2,1,0:T(8,128)(2,1)S(1)}, s32[1,384]{1,0:T(1,128)S(1)}, s32[1,128]{1,0:T(1,128)S(1)}) custom-call(s32[384]{0:T(512)} %labels_ref.3, bf16[4,384,384]{2,1,0:T(8,128)(2,1)} %bitcast.8.w_ref), custom_call_target="tpu_custom_call" | custom-call | tf_op jit(solution)/shard_map/pack_give/pallas_call | solution.py:123
  1.5 3.3 %collective-permute-start.23 = (bf16[1,2,64,384]{3,2,1,0:T(8,128)(2,1)S(1)}, bf16[1,2,64,384]{3,2,1,0:T(8,128)(2,1)S(1)}, u32[]{:S(2)}, u32[]{:S(2)}) collective-permute-start(bf16[1,2,64,384]{3,2,1,0:T(8,128)(2,1)S(1)} %get-tuple-element.86), channel_id=1, source_target_pairs={{0,8},{8,0},{16,24},{24,16},{32,40},{40,32},{48,56},{56,48},{64,72... | collective-permute-start | bytes 294920 | tf_op jit(solution)/shard_map/ppermute | solution.py:345
  4.8 1.7 %pack_keep.2 = (bf16[1,8,48,128]{3,2,1,0:T(8,128)(2,1)S(1)}, bf16[1,2,64,384]{3,2,1,0:T(8,128)(2,1)S(1)}) custom-call(s32[1,384]{1,0:T(1,128)S(1)} %get-tuple-element.83.pos_ref, bf16[16,48,384]{2,1,0:T(8,128)(2,1)S(1)} %bitcast.15, bf16[4,384,384]{2,1,0:T(8,128)(2,1)} %bitcast.8.w_ref), custom_call_target="tpu_custom_call" | custom-call | bytes 4194304 | tf_op jit(solution)/shard_map/pack_keep/pallas_call | solution.py:146
  6.5 0.0 collective-permute-done.23.refs_1_
  6.5 0.1 collective-permute-start.25
  6.6 4.5 %collective-permute-start.24 = (bf16[2,2,64,384]{3,2,1,0:T(8,128)(2,1)S(1)}, bf16[2,2,64,384]{3,2,1,0:T(8,128)(2,1)S(1)}, u32[]{:S(2)}, u32[]{:S(2)}) collective-permute-start(bf16[2,2,64,384]{3,2,1,0:T(8,128)(2,1)S(1)} %join_w.2.refs_4_.refs_0_), channel_id=1, source_target_pairs={{0,7},{1,2},{2,1},{3,4},{4,3},{5,6},{6,5},{7,0},{8,15},{9,10},{10,... | collective-permute-start | bytes 589832 | tf_op jit(solution)/shard_map/ppermute | solution.py:208
  11.2 1.3 %collective-permute-start.17 = (bf16[1,8,48,128]{3,2,1,0:T(8,128)(2,1)S(1)}, bf16[1,8,48,128]{3,2,1,0:T(8,128)(2,1)S(1)}, u32[]{:S(2)}, u32[]{:S(2)}) collective-permute-start(bf16[1,8,48,128]{3,2,1,0:T(8,128)(2,1)S(1)} %get-tuple-element.84.refs_0_), channel_id=1, source_target_pairs={{0,64},{8,24},{16,80},{24,8},{32,96},{40,56},{48,112},{56,40},{64,... | collective-permute-start | bytes 294920 | tf_op jit(solution)/shard_map/ppermute | solution.py:202
  12.5 2.6 %collective-permute-start.18 = (bf16[1,8,48,128]{3,2,1,0:T(8,128)(2,1)S(1)}, bf16[1,8,48,128]{3,2,1,0:T(8,128)(2,1)S(1)}, u32[]{:S(2)}, u32[]{:S(2)}) collective-permute-start(bf16[1,8,48,128]{3,2,1,0:T(8,128)(2,1)S(1)} %get-tuple-element.84.refs_0_), channel_id=1, source_target_pairs={{0,128},{8,40},{16,144},{24,56},{32,160},{40,8},{48,176},{56,24},{... | collective-permute-start | bytes 294920 | tf_op jit(solution)/shard_map/ppermute | solution.py:202
  15.1 0.0 collective-permute-start.19
  15.1 1.9 %collective-permute-start.26 = (bf16[2,2,64,384]{3,2,1,0:T(8,128)(2,1)S(1)}, bf16[2,2,64,384]{3,2,1,0:T(8,128)(2,1)S(1)}, u32[]{:S(2)}, u32[]{:S(2)}) collective-permute-start(bf16[2,2,64,384]{3,2,1,0:T(8,128)(2,1)S(1)} %collective-permute-done.25.refs_6_.refs_2_), channel_id=1, source_target_pairs={{0,7},{1,2},{2,1},{3,4},{4,3},{5,6},{6,5},{7,0},{8,15},{9,10},{10,... | collective-permute-start | bytes 589832 | tf_op jit(solution)/shard_map/ppermute | solution.py:212
  17.0 1.5 %collective-permute-done.18.refs_2_ = bf16[1,8,48,128]{3,2,1,0:T(8,128)(2,1)S(1)} collective-permute-done((bf16[1,8,48,128]{3,2,1,0:T(8,128)(2,1)S(1)}, bf16[1,8,48,128]{3,2,1,0:T(8,128)(2,1)S(1)}, u32[]{:S(2)}, u32[]{:S(2)}) %collective-permute-start.18) | collective-permute-done | bytes 98336 | tf_op jit(solution)/shard_map/ppermute | solution.py:202
  18.4 1.3 %collective-permute-done.19.refs_3_ = bf16[1,8,48,128]{3,2,1,0:T(8,128)(2,1)S(1)} collective-permute-done((bf16[1,8,48,128]{3,2,1,0:T(8,128)(2,1)S(1)}, bf16[1,8,48,128]{3,2,1,0:T(8,128)(2,1)S(1)}, u32[]{:S(2)}, u32[]{:S(2)}) %collective-permute-start.19) | collective-permute-done | bytes 98336 | tf_op jit(solution)/shard_map/ppermute | solution.py:202
  19.8 1.6 %collective-permute-start.20 = (bf16[4,8,48,128]{3,2,1,0:T(8,128)(2,1)S(1)}, bf16[4,8,48,128]{3,2,1,0:T(8,128)(2,1)S(1)}, u32[]{:S(2)}, u32[]{:S(2)}) collective-permute-start(bf16[4,8,48,128]{3,2,1,0:T(8,128)(2,1)S(1)} %join_row.2.refs_0_), channel_id=1, source_target_pairs={{0,16},{8,72},{16,0},{24,88},{32,48},{40,104},{48,32},{56,120},{64... | collective-permute-start | bytes 1179656 | tf_op jit(solution)/shard_map/ppermute | solution.py:202
  21.4 2.2 %collective-permute-start.21 = (bf16[4,8,48,128]{3,2,1,0:T(8,128)(2,1)S(1)}, bf16[4,8,48,128]{3,2,1,0:T(8,128)(2,1)S(1)}, u32[]{:S(2)}, u32[]{:S(2)}) collective-permute-start(bf16[4,8,48,128]{3,2,1,0:T(8,128)(2,1)S(1)} %join_row.2.refs_0_), channel_id=1, source_target_pairs={{0,32},{8,136},{16,48},{24,152},{32,0},{40,168},{48,16},{56,184},{... | collective-permute-start | bytes 1179656 | tf_op jit(solution)/shard_map/ppermute | solution.py:202
  23.5 0.3 collective-permute-start.22
  23.9 1.3 %collective-permute-start.28 = (bf16[2,2,64,384]{3,2,1,0:T(8,128)(2,1)S(1)}, bf16[2,2,64,384]{3,2,1,0:T(8,128)(2,1)S(1)}, u32[]{:S(2)}, u32[]{:S(2)}) collective-permute-start(bf16[2,2,64,384]{3,2,1,0:T(8,128)(2,1)S(1)} %collective-permute-done.27.refs_8_.refs_4_), channel_id=1, source_target_pairs={{0,7},{1,2},{2,1},{3,4},{4,3},{5,6},{6,5},{7,0},{8,15},{9,10},{10,... | collective-permute-start | bytes 589832 | tf_op jit(solution)/shard_map/ppermute | solution.py:214
  25.2 3.5 %collective-permute-done.29.refs_10_.refs_6_ = bf16[2,2,64,384]{3,2,1,0:T(8,128)(2,1)S(1)} collective-permute-done((bf16[2,2,64,384]{3,2,1,0:T(8,128)(2,1)S(1)}, bf16[2,2,64,384]{3,2,1,0:T(8,128)(2,1)S(1)}, u32[]{:S(2)}, u32[]{:S(2)}) %collective-permute-start.29) | collective-permute-done | bytes 196640 | tf_op jit(solution)/shard_map/ppermute | solution.py:215
  28.7 0.1 collective-permute-start.30
  28.8 0.9 %collective-permute-done.28.refs_9_.refs_5_ = bf16[2,2,64,384]{3,2,1,0:T(8,128)(2,1)S(1)} collective-permute-done((bf16[2,2,64,384]{3,2,1,0:T(8,128)(2,1)S(1)}, bf16[2,2,64,384]{3,2,1,0:T(8,128)(2,1)S(1)}, u32[]{:S(2)}, u32[]{:S(2)}) %collective-permute-start.28) | collective-permute-done | bytes 196640 | tf_op jit(solution)/shard_map/ppermute | solution.py:214
  29.7 0.0 copy-start.12
  29.7 0.0 copy-start.13
  29.7 5.0 %collective-permute-start.31 = (bf16[1,2,64,384]{3,2,1,0:T(8,128)(2,1)S(1)}, bf16[1,2,64,384]{3,2,1,0:T(8,128)(2,1)S(1)}, u32[]{:S(2)}, u32[]{:S(2)}) collective-permute-start(bf16[1,2,64,384]{3,2,1,0:T(8,128)(2,1)S(1)} %slice.23), channel_id=1, source_target_pairs={{0,9},{1,8},{2,11},{3,10},{4,13},{5,12},{6,15},{7,14},{8,1},{9,0},... | collective-permute-start | bytes 294920 | tf_op jit(solution)/shard_map/ppermute | solution.py:217
  34.8 1.1 %collective-permute-done.22.refs_3_ = bf16[4,8,48,128]{3,2,1,0:T(8,128)(2,1)S(1)} collective-permute-done((bf16[4,8,48,128]{3,2,1,0:T(8,128)(2,1)S(1)}, bf16[4,8,48,128]{3,2,1,0:T(8,128)(2,1)S(1)}, u32[]{:S(2)}, u32[]{:S(2)}) %collective-permute-start.22) | collective-permute-done | bytes 393248 | tf_op jit(solution)/shard_map/ppermute | solution.py:202
  35.9 1.9 %other_part.2 = (f32[2,384,384]{2,1,0:T(8,128)S(1)}, bf16[2,384,896]{2,1,0:T(8,128)(2,1)S(1)}, bf16[2,384,128]{2,1,0:T(8,128)(2,1)S(1)}) custom-call(bf16[4,8,48,128]{3,2,1,0:T(8,128)(2,1)S(1)} %join_row.2.refs_0_, bf16[4,8,48,128]{3,2,1,0:T(8,128)(2,1)S(1)} %collective-permute-done.20.refs_1_, bf16[4,8,48,128]{3,2,1,0:T(8,128)(2,1)S(1)} %collective-permute-done.21.refs_2_, ...), custom_call_target="tpu_custom_call" | custom-call | flops 528482304 | bytes 6291456 | tf_op jit(solution)/shard_map/other_part/pallas_call | solution.py:270
  37.8 0.3 collective-permute-done.31.refs_5_
  38.1 3.6 %collective-permute-start.32 = (f32[2,384,384]{2,1,0:T(8,128)S(1)}, f32[2,384,384]{2,1,0:T(8,128)S(1)}, u32[]{:S(2)}, u32[]{:S(2)}) collective-permute-start(f32[2,384,384]{2,1,0:T(8,128)S(1)} %get-tuple-element.89), channel_id=1, source_target_pairs={{0,8},{8,0},{16,24},{24,16},{32,40},{40,32},{48,56},{56,48},{64,72... | collective-permute-start | bytes 3538952 | tf_op jit(solution)/shard_map/ppermute | solution.py:350
  41.6 0.1 collective-permute-start.33
  41.7 0.8 %bits.1.bits_ref = s32[48,384]{1,0:T(8,128)S(1)} custom-call(s32[32]{0:T(128)S(1)} %copy-done.13, s32[384]{0:T(512)S(1)} %copy-done.12), custom_call_target="tpu_custom_call" | custom-call | tf_op jit(solution)/shard_map/bits/pallas_call | solution.py:166
  42.5 1.0 %own_part.2.refs_0_ = f32[2,384,384]{2,1,0:T(8,128)S(1)} custom-call(bf16[2,384,896]{2,1,0:T(8,128)(2,1)S(1)} %get-tuple-element.87.t_cat, bf16[2,2,64,384]{3,2,1,0:T(8,128)(2,1)S(1)} %join_w.2.refs_4_.refs_0_, bf16[2,2,64,384]{3,2,1,0:T(8,128)(2,1)S(1)} %collective-permute-done.24.refs_5_.refs_1_, ...), custom_call_target="tpu_custom_call" | custom-call | flops 528482304 | bytes 4194304 | tf_op jit(solution)/shard_map/own_part/pallas_call | solution.py:300
  43.4 0.9 %collective-permute-done.33.refs_3_ = bf16[2,384,128]{2,1,0:T(8,128)(2,1)S(1)} collective-permute-done((bf16[2,384,128]{2,1,0:T(8,128)(2,1)S(1)}, bf16[2,384,128]{2,1,0:T(8,128)(2,1)S(1)}, u32[]{:S(2)}, u32[]{:S(2)}) %collective-permute-start.33) | collective-permute-done | bytes 196640 | tf_op jit(solution)/shard_map/ppermute | solution.py:351
  44.4 1.2 %last_part.1 = (bf16[16,48,384]{2,1,0:T(8,128)(2,1)}, s32[1]{0:T(128)}) custom-call(s32[1,128]{1,0:T(1,128)S(1)} %get-tuple-element.82.width_ref, s32[48,384]{1,0:T(8,128)S(1)} %bits.1.bits_ref, f32[2,384,384]{2,1,0:T(8,128)S(1)} %own_part.2.refs_0_, f32[2,384,384]{2,1,0:T(8,128)S(1)} %collective-permute-done.32.refs_1_, ...), custom_call_target="tpu_custom_call" | custom-call | tf_op jit(solution)/shard_map/last_part/pallas_call | solution.py:356
  46.2 0.2 conditional.1
  (19 shorter events, 0.1 us)
Async XLA Ops:
  0.0 4.8 %copy-start.9 = (bf16[16,1,48,384]{3,2,1,0:T(8,128)(2,1)S(1)}, bf16[16,1,48,384]{3,2,1,0:T(8,128)(2,1)}, u32[]{:S(2)}) copy-start(bf16[16,1,48,384]{3,2,1,0:T(8,128)(2,1)} %param.8) | copy-start | bytes 1769476
  1.5 5.0 %collective-permute-start.23 = (bf16[1,2,64,384]{3,2,1,0:T(8,128)(2,1)S(1)}, bf16[1,2,64,384]{3,2,1,0:T(8,128)(2,1)S(1)}, u32[]{:S(2)}, u32[]{:S(2)}) collective-permute-start(bf16[1,2,64,384]{3,2,1,0:T(8,128)(2,1)S(1)} %get-tuple-element.86), channel_id=1, source_target_pairs={{0,8},{8,0},{16,24},{24,16},{32,40},{40,32},{48,56},{56,48},{64,72... | collective-permute-start | bytes 294920 | tf_op jit(solution)/shard_map/ppermute | solution.py:345
  6.5 8.6 %collective-permute-start.25 = (bf16[2,2,64,384]{3,2,1,0:T(8,128)(2,1)S(1)}, bf16[2,2,64,384]{3,2,1,0:T(8,128)(2,1)S(1)}, u32[]{:S(2)}, u32[]{:S(2)}) collective-permute-start(bf16[2,2,64,384]{3,2,1,0:T(8,128)(2,1)S(1)} %join_w.2.refs_4_.refs_0_), channel_id=1, source_target_pairs={{0,1},{1,0},{2,3},{3,2},{4,5},{5,4},{6,7},{7,6},{8,9},{9,8},{10,11... | collective-permute-start | bytes 589832 | tf_op jit(solution)/shard_map/ppermute | solution.py:209
  6.6 10.3 %collective-permute-start.24 = (bf16[2,2,64,384]{3,2,1,0:T(8,128)(2,1)S(1)}, bf16[2,2,64,384]{3,2,1,0:T(8,128)(2,1)S(1)}, u32[]{:S(2)}, u32[]{:S(2)}) collective-permute-start(bf16[2,2,64,384]{3,2,1,0:T(8,128)(2,1)S(1)} %join_w.2.refs_4_.refs_0_), channel_id=1, source_target_pairs={{0,7},{1,2},{2,1},{3,4},{4,3},{5,6},{6,5},{7,0},{8,15},{9,10},{10,... | collective-permute-start | bytes 589832 | tf_op jit(solution)/shard_map/ppermute | solution.py:208
  11.2 5.8 %collective-permute-start.17 = (bf16[1,8,48,128]{3,2,1,0:T(8,128)(2,1)S(1)}, bf16[1,8,48,128]{3,2,1,0:T(8,128)(2,1)S(1)}, u32[]{:S(2)}, u32[]{:S(2)}) collective-permute-start(bf16[1,8,48,128]{3,2,1,0:T(8,128)(2,1)S(1)} %get-tuple-element.84.refs_0_), channel_id=1, source_target_pairs={{0,64},{8,24},{16,80},{24,8},{32,96},{40,56},{48,112},{56,40},{64,... | collective-permute-start | bytes 294920 | tf_op jit(solution)/shard_map/ppermute | solution.py:202
  12.5 6.0 %collective-permute-start.18 = (bf16[1,8,48,128]{3,2,1,0:T(8,128)(2,1)S(1)}, bf16[1,8,48,128]{3,2,1,0:T(8,128)(2,1)S(1)}, u32[]{:S(2)}, u32[]{:S(2)}) collective-permute-start(bf16[1,8,48,128]{3,2,1,0:T(8,128)(2,1)S(1)} %get-tuple-element.84.refs_0_), channel_id=1, source_target_pairs={{0,128},{8,40},{16,144},{24,56},{32,160},{40,8},{48,176},{56,24},{... | collective-permute-start | bytes 294920 | tf_op jit(solution)/shard_map/ppermute | solution.py:202
  15.1 4.7 %collective-permute-start.19 = (bf16[1,8,48,128]{3,2,1,0:T(8,128)(2,1)S(1)}, bf16[1,8,48,128]{3,2,1,0:T(8,128)(2,1)S(1)}, u32[]{:S(2)}, u32[]{:S(2)}) collective-permute-start(bf16[1,8,48,128]{3,2,1,0:T(8,128)(2,1)S(1)} %get-tuple-element.84.refs_0_), channel_id=1, source_target_pairs={{0,192},{8,56},{16,208},{24,40},{32,224},{40,24},{48,240},{56,8},{... | collective-permute-start | bytes 294920 | tf_op jit(solution)/shard_map/ppermute | solution.py:202
  15.1 8.8 %collective-permute-start.26 = (bf16[2,2,64,384]{3,2,1,0:T(8,128)(2,1)S(1)}, bf16[2,2,64,384]{3,2,1,0:T(8,128)(2,1)S(1)}, u32[]{:S(2)}, u32[]{:S(2)}) collective-permute-start(bf16[2,2,64,384]{3,2,1,0:T(8,128)(2,1)S(1)} %collective-permute-done.25.refs_6_.refs_2_), channel_id=1, source_target_pairs={{0,7},{1,2},{2,1},{3,4},{4,3},{5,6},{6,5},{7,0},{8,15},{9,10},{10,... | collective-permute-start | bytes 589832 | tf_op jit(solution)/shard_map/ppermute | solution.py:212
  17.0 6.9 %collective-permute-start.27 = (bf16[2,2,64,384]{3,2,1,0:T(8,128)(2,1)S(1)}, bf16[2,2,64,384]{3,2,1,0:T(8,128)(2,1)S(1)}, u32[]{:S(2)}, u32[]{:S(2)}) collective-permute-start(bf16[2,2,64,384]{3,2,1,0:T(8,128)(2,1)S(1)} %collective-permute-done.24.refs_5_.refs_1_), channel_id=1, source_target_pairs={{0,1},{1,0},{2,3},{3,2},{4,5},{5,4},{6,7},{7,6},{8,9},{9,8},{10,11... | collective-permute-start | bytes 589832 | tf_op jit(solution)/shard_map/ppermute | solution.py:213
  19.8 15.0 %collective-permute-start.20 = (bf16[4,8,48,128]{3,2,1,0:T(8,128)(2,1)S(1)}, bf16[4,8,48,128]{3,2,1,0:T(8,128)(2,1)S(1)}, u32[]{:S(2)}, u32[]{:S(2)}) collective-permute-start(bf16[4,8,48,128]{3,2,1,0:T(8,128)(2,1)S(1)} %join_row.2.refs_0_), channel_id=1, source_target_pairs={{0,16},{8,72},{16,0},{24,88},{32,48},{40,104},{48,32},{56,120},{64... | collective-permute-start | bytes 1179656 | tf_op jit(solution)/shard_map/ppermute | solution.py:202
  21.4 13.4 %collective-permute-start.21 = (bf16[4,8,48,128]{3,2,1,0:T(8,128)(2,1)S(1)}, bf16[4,8,48,128]{3,2,1,0:T(8,128)(2,1)S(1)}, u32[]{:S(2)}, u32[]{:S(2)}) collective-permute-start(bf16[4,8,48,128]{3,2,1,0:T(8,128)(2,1)S(1)} %join_row.2.refs_0_), channel_id=1, source_target_pairs={{0,32},{8,136},{16,48},{24,152},{32,0},{40,168},{48,16},{56,184},{... | collective-permute-start | bytes 1179656 | tf_op jit(solution)/shard_map/ppermute | solution.py:202
  23.5 12.3 %collective-permute-start.22 = (bf16[4,8,48,128]{3,2,1,0:T(8,128)(2,1)S(1)}, bf16[4,8,48,128]{3,2,1,0:T(8,128)(2,1)S(1)}, u32[]{:S(2)}, u32[]{:S(2)}) collective-permute-start(bf16[4,8,48,128]{3,2,1,0:T(8,128)(2,1)S(1)} %join_row.2.refs_0_), channel_id=1, source_target_pairs={{0,48},{8,200},{16,32},{24,216},{32,16},{40,232},{48,0},{56,248},{... | collective-permute-start | bytes 1179656 | tf_op jit(solution)/shard_map/ppermute | solution.py:202
  23.9 4.8 %collective-permute-start.29 = (bf16[2,2,64,384]{3,2,1,0:T(8,128)(2,1)S(1)}, bf16[2,2,64,384]{3,2,1,0:T(8,128)(2,1)S(1)}, u32[]{:S(2)}, u32[]{:S(2)}) collective-permute-start(bf16[2,2,64,384]{3,2,1,0:T(8,128)(2,1)S(1)} %collective-permute-done.26.refs_7_.refs_3_), channel_id=1, source_target_pairs={{0,1},{1,0},{2,3},{3,2},{4,5},{5,4},{6,7},{7,6},{8,9},{9,8},{10,11... | collective-permute-start | bytes 589832 | tf_op jit(solution)/shard_map/ppermute | solution.py:215
  23.9 5.8 %collective-permute-start.28 = (bf16[2,2,64,384]{3,2,1,0:T(8,128)(2,1)S(1)}, bf16[2,2,64,384]{3,2,1,0:T(8,128)(2,1)S(1)}, u32[]{:S(2)}, u32[]{:S(2)}) collective-permute-start(bf16[2,2,64,384]{3,2,1,0:T(8,128)(2,1)S(1)} %collective-permute-done.27.refs_8_.refs_4_), channel_id=1, source_target_pairs={{0,7},{1,2},{2,1},{3,4},{4,3},{5,6},{6,5},{7,0},{8,15},{9,10},{10,... | collective-permute-start | bytes 589832 | tf_op jit(solution)/shard_map/ppermute | solution.py:214
  28.7 9.1 %collective-permute-start.30 = (bf16[1,2,64,384]{3,2,1,0:T(8,128)(2,1)S(1)}, bf16[1,2,64,384]{3,2,1,0:T(8,128)(2,1)S(1)}, u32[]{:S(2)}, u32[]{:S(2)}) collective-permute-start(bf16[1,2,64,384]{3,2,1,0:T(8,128)(2,1)S(1)} %slice.22), channel_id=1, source_target_pairs={{0,7},{1,2},{2,1},{3,4},{4,3},{5,6},{6,5},{7,0},{8,15},{9,10},{10,... | collective-permute-start | bytes 294920 | tf_op jit(solution)/shard_map/ppermute | solution.py:216
  29.7 12.0 %copy-start.12 = (s32[384]{0:T(512)S(1)}, s32[384]{0:T(512)}, u32[]{:S(2)}) copy-start(s32[384]{0:T(512)} %labels_ref.3) | copy-start | bytes 4612
  29.7 12.0 %copy-start.13 = (s32[32]{0:T(128)S(1)}, s32[32]{0:T(128)}, u32[]{:S(2)}) copy-start(s32[32]{0:T(128)} %occ_ref.1) | copy-start | bytes 388
  29.7 8.3 %collective-permute-start.31 = (bf16[1,2,64,384]{3,2,1,0:T(8,128)(2,1)S(1)}, bf16[1,2,64,384]{3,2,1,0:T(8,128)(2,1)S(1)}, u32[]{:S(2)}, u32[]{:S(2)}) collective-permute-start(bf16[1,2,64,384]{3,2,1,0:T(8,128)(2,1)S(1)} %slice.23), channel_id=1, source_target_pairs={{0,9},{1,8},{2,11},{3,10},{4,13},{5,12},{6,15},{7,14},{8,1},{9,0},... | collective-permute-start | bytes 294920 | tf_op jit(solution)/shard_map/ppermute | solution.py:217
  38.1 6.3 %collective-permute-start.32 = (f32[2,384,384]{2,1,0:T(8,128)S(1)}, f32[2,384,384]{2,1,0:T(8,128)S(1)}, u32[]{:S(2)}, u32[]{:S(2)}) collective-permute-start(f32[2,384,384]{2,1,0:T(8,128)S(1)} %get-tuple-element.89), channel_id=1, source_target_pairs={{0,8},{8,0},{16,24},{24,16},{32,40},{40,32},{48,56},{56,48},{64,72... | collective-permute-start | bytes 3538952 | tf_op jit(solution)/shard_map/ppermute | solution.py:350
  41.6 2.8 %collective-permute-start.33 = (bf16[2,384,128]{2,1,0:T(8,128)(2,1)S(1)}, bf16[2,384,128]{2,1,0:T(8,128)(2,1)S(1)}, u32[]{:S(2)}, u32[]{:S(2)}) collective-permute-start(bf16[2,384,128]{2,1,0:T(8,128)(2,1)S(1)} %get-tuple-element.90.refs_2_), channel_id=1, source_target_pairs={{0,8},{8,0},{16,24},{24,16},{32,40},{40,32},{48,56},{56,48},{64,72... | collective-permute-start | bytes 589832 | tf_op jit(solution)/shard_map/ppermute | solution.py:351

commit v4 on v3

--- a/solution.py
+++ b/solution.py
@@ -93,17 +93,27 @@
     row_ref[0] = both.astype(BF).reshape(half, na, 2 * CAP)
 
 
-def bits_kernel(occ_ref, labels_ref, bits_ref):
+def prepare_kernel(occ_ref, labels_ref, pos_ref, bits_ref, pick_own_ref, pick_other_ref, spread_ref, expand_ref):
     na, v = bits_ref.shape
     labels = labels_ref[...].reshape(1, v)
+    pos = pos_ref[...]
+    tr = lax.axis_index("tr")
     place = lax.broadcasted_iota(jnp.int32, (na, v), 0) + lax.axis_index("su") * na
     here = lax.broadcasted_iota(jnp.int32, (na, v), 1) == place
     labels_a = jnp.sum(jnp.where(here, labels, 0).astype(F32), axis=1, keepdims=True).astype(jnp.int32)
-    plane = jnp.bitwise_xor(jnp.bitwise_xor(labels_a, labels), occ_ref[lax.axis_index("tr")])
+    plane = jnp.bitwise_xor(jnp.bitwise_xor(labels_a, labels), occ_ref[tr])
     bits = jnp.zeros((na, v), jnp.int32)
     for i in range(IW):
         bits += jnp.where(plane == occ_ref[i], 1 << i, 0)
     bits_ref[...] = bits
+    rows_a = jnp.broadcast_to(labels_a, pick_own_ref.shape[1:])
+    for i in range(IW):
+        for ref, j in ((pick_own_ref, tr), (pick_other_ref, jnp.bitwise_xor(tr, 1))):
+            ref[i] = jnp.right_shift(jnp.bitwise_xor(rows_a, jnp.bitwise_xor(occ_ref[i], occ_ref[j])), 1)
+    wide = lax.broadcasted_iota(jnp.int32, spread_ref.shape, 0) == labels * CAP + pos
+    spread_ref[...] = wide.astype(F32).astype(BF)
+    pair = lax.broadcasted_iota(jnp.int32, expand_ref.shape, 0) == jnp.bitwise_and(labels, 1) * CAP + pos
+    expand_ref[...] = pair.astype(F32).astype(BF)
 
 
 SMEM = pl.BlockSpec(memory_space=pltpu.SMEM)
@@ -162,15 +172,23 @@
     )(*args, pos, t, w)
 
 
-def symmetric_bits(occupied, labels, na):
-    return pl.pallas_call(
-        bits_kernel,
-        out_shape=jax.ShapeDtypeStruct((na, labels.shape[0]), jnp.int32),
-        in_specs=[SMEM, VMEM],
-        out_specs=VMEM,
-        compiler_params=pltpu.CompilerParams(vmem_limit_bytes=4 * 2**20),
-        name="bits",
-    )(occupied, labels)
+def prepare(occupied, labels, pos, na):
+    v = labels.shape[0]
+    pick = jax.ShapeDtypeStruct((IW, na, 2 * CAP), jnp.int32)
+    return pl.pallas_call(
+        prepare_kernel,
+        out_shape=(
+            jax.ShapeDtypeStruct((na, v), jnp.int32),
+            pick,
+            pick,
+            jax.ShapeDtypeStruct((8 * CAP, v), BF),
+            jax.ShapeDtypeStruct((2 * CAP, v), BF),
+        ),
+        in_specs=[SMEM, VMEM, VMEM],
+        out_specs=(VMEM,) * 5,
+        compiler_params=pltpu.CompilerParams(vmem_limit_bytes=8 * 2**20),
+        name="prepare",
+    )(occupied, labels, pos)
 
 
 OFFSETS = (0, 1, -1, 2, -2, 3, -3, 4)
@@ -316,17 +334,200 @@
     return own_ref[h] + got_ref[h] + jnp.dot(left, right, preferred_element_type=F32)
 
 
-def last_kernel(width_ref, bits_ref, *refs):
-    parts, (out_ref, fits_ref) = refs[:-2], refs[-2:]
-    fits_ref[0] = (width_ref[0, 0] <= CAP).astype(jnp.int32)
-    half_i = out_ref.shape[0] // 2
-    na = out_ref.shape[1]
+def spread_kernel(spread_ref, *refs):
+    d_refs, outs = refs[:-2], refs[-2:]
+    _, ne, cap, v = d_refs[0].shape
+    dims = (((1,), (1,)), ((), ()))
+    for j in range(2):
+        for n, d_ref in enumerate(d_refs):
+            block = d_ref[j].reshape(ne * cap, v)
+            wide = lax.dot_general(block, spread_ref[...], dims, preferred_element_type=F32)
+            outs[j][n * ne : (n + 1) * ne] = wide.astype(BF).reshape(ne, cap, -1)
+        outs[j][len(d_refs) * ne :] = jnp.zeros((ne, cap, spread_ref.shape[0]), BF)
+
+
+def spread_blocks(spread, d_parts):
+    _, ne, cap, v = d_parts[0].shape
+    out = jax.ShapeDtypeStruct((NZ * ne, cap, spread.shape[0]), BF)
+    return pl.pallas_call(
+        spread_kernel,
+        out_shape=(out, out),
+        in_specs=[VMEM] * (1 + len(d_parts)),
+        out_specs=(VMEM, VMEM),
+        compiler_params=pltpu.CompilerParams(vmem_limit_bytes=8 * 2**20),
+        cost_estimate=pl.CostEstimate(
+            flops=4 * NZ * ne * cap * v * spread.shape[0], bytes_accessed=4 * 2**20, transcendentals=0
+        ),
+        name="spread",
+    )(spread, *d_parts)
+
+
+def block_at(first, second):
+    tr = lax.axis_index("tr")
+    z = lax.axis_index("su")
+    x, y, core = tr // (2 * NY), (tr // 2) % NY, tr % 2
+    to_x = jnp.bitwise_xor(x, jnp.where(core == 0, first, second))
+    to_y = jnp.bitwise_xor(y, jnp.where(core == 0, second, first))
+    ahead = (z - (2 * to_x + to_y // 2)) * (1 - 2 * (z % 2))
+    hops = (ahead + 2 * NZ) % NZ
+    arrival = jnp.where(hops == 0, 0, jnp.where(hops <= NZ // 2, 2 * hops - 1, 2 * (NZ - hops)))
+    return 2 * arrival + to_y % 2
+
+
+def pair_lanes(one, two, h):
+    lanes = slice(h * CAP, (h + 1) * CAP)
+    return jnp.concatenate([one[:, lanes], two[:, lanes]], 1)
+
+
+def flat(piece):
+    return piece.reshape(piece.shape[0] * piece.shape[1], piece.shape[2])
+
+
+def early_kernel(*refs):
+    t_refs, (d_own, d_other, own_ref, other_ref, t_cat, d_cat) = refs[:-6], refs[-6:]
+    lanes = 2 * CAP
+    for second, t_ref in enumerate(t_refs):
+        for p in range(NX // 2):
+            one, two = flat(t_ref[2 * p]), flat(t_ref[2 * p + 1])
+            at = (second * (NX // 2) + p) * lanes
+            for h in range(2):
+                t_cat[h, :, at : at + lanes] = pair_lanes(one, two, h)
+            for u in range(2):
+                src = block_at(2 * p + u, second)
+                d_cat[0, at + u * CAP : at + (u + 1) * CAP] = d_own[src]
+                d_cat[1, at + u * CAP : at + (u + 1) * CAP] = d_other[src]
+    for j, ref in enumerate((own_ref, other_ref)):
+        for h in range(2):
+            ref[h] = jnp.dot(t_cat[h], d_cat[j], preferred_element_type=F32)
+
+
+def early_sums(t_parts, d_own, d_other):
+    chips, half_i, na, lanes = t_parts[0].shape
+    rows = half_i * na
+    depth = len(t_parts) * chips * CAP
+    wide = d_own.shape[2]
+    out = jax.ShapeDtypeStruct((2, rows, wide), F32)
+    return pl.pallas_call(
+        early_kernel,
+        out_shape=(out, out),
+        in_specs=[VMEM] * (len(t_parts) + 2),
+        out_specs=(VMEM, VMEM),
+        scratch_shapes=[pltpu.VMEM((2, rows, depth), BF), pltpu.VMEM((2, depth, wide), BF)],
+        compiler_params=pltpu.CompilerParams(vmem_limit_bytes=16 * 2**20),
+        cost_estimate=pl.CostEstimate(flops=8 * rows * wide * depth, bytes_accessed=6 * 2**20, transcendentals=0),
+        name="early_sums",
+    )(*t_parts, d_own, d_other)
+
+
+def keep_pair(sums, pick):
+    lanes = 2 * CAP
+    out = sums[:, :lanes]
+    for g in range(1, 4):
+        out = jnp.where(pick == g, sums[:, g * lanes : (g + 1) * lanes], out)
+    return out
+
+
+def late_blocks(d_ref, d_cat):
+    for first in range(NX):
+        d_cat[first * CAP : (first + 1) * CAP] = d_ref[block_at(first, NX - 1)]
+
+
+def other_pair_kernel(pick_ref, *refs):
+    t_refs, (sums_ref, d_ref, other_ref, late_ref, rest_ref, d_cat) = refs[:NX], refs[NX:]
+    last = t_refs[-1]
+    lanes = 2 * CAP
+    for p in range(NX // 2):
+        one, two = flat(last[2 * p]), flat(last[2 * p + 1])
+        for h in range(2):
+            late_ref[h, :, p * lanes : (p + 1) * lanes] = pair_lanes(one, two, h)
+    late_blocks(d_ref, d_cat)
+    ni, na = other_ref.shape[:2]
+    half_i = ni // 2
     for h in range(2):
-        sums = total(h, *parts)
+        sums = sums_ref[h] + jnp.dot(late_ref[h], d_cat[...], preferred_element_type=F32)
         for u in range(half_i):
             i = h * half_i + u
-            keep = jnp.bitwise_and(bits_ref[...], 1 << i) != 0
-            out_ref[i] = jnp.where(keep, sums[u * na : (u + 1) * na], 0.0).astype(BF)
+            other_ref[i] = keep_pair(sums[u * na : (u + 1) * na], pick_ref[i])
+    tr = lax.axis_index("tr")
+    far = (lax.axis_index("su") + NZ // 2) % NZ
+    x, y, core = tr // (2 * NY), (tr // 2) % NY, tr % 2
+    pair = []
+    for e in range(2):
+        dx = jnp.bitwise_xor(far // 2, x)
+        dy = jnp.bitwise_xor(2 * (far % 2) + e, y)
+        first = jnp.where(core == 0, dx, dy)
+        second = jnp.where(core == 0, dy, dx)
+        piece = t_refs[0][first]
+        for n in range(1, NX):
+            piece = jnp.where(second == n, t_refs[n][first], piece)
+        pair.append(flat(piece))
+    for h in range(2):
+        rest_ref[h] = pair_lanes(*pair, h)
+
+
+def other_pair(pick, t_parts, sums, d):
+    chips, half_i, na, lanes = t_parts[0].shape
+    rows = half_i * na
+    return pl.pallas_call(
+        other_pair_kernel,
+        out_shape=(
+            jax.ShapeDtypeStruct(pick.shape, F32),
+            jax.ShapeDtypeStruct((2, rows, chips * CAP), BF),
+            jax.ShapeDtypeStruct((2, rows, lanes), BF),
+        ),
+        in_specs=[VMEM] * (3 + len(t_parts)),
+        out_specs=(VMEM, VMEM, VMEM),
+        scratch_shapes=[pltpu.VMEM((chips * CAP, d.shape[2]), BF)],
+        compiler_params=pltpu.CompilerParams(vmem_limit_bytes=12 * 2**20),
+        cost_estimate=pl.CostEstimate(
+            flops=4 * rows * d.shape[2] * chips * CAP, bytes_accessed=6 * 2**20, transcendentals=0
+        ),
+        name="other_pair",
+    )(pick, *t_parts, sums, d)
+
+
+def own_pair_kernel(pick_ref, spread_ref, sums_ref, late_ref, d_ref, rest_ref, rest_got_ref, a4_ref, b4_ref, own_ref, d_cat):
+    _, ne, cap, v = a4_ref.shape
+    depth = late_ref.shape[2]
+    late_blocks(d_ref, d_cat)
+    dims = (((1,), (1,)), ((), ()))
+    for n, ref in enumerate((a4_ref, b4_ref)):
+        wide = lax.dot_general(ref[0].reshape(ne * cap, v), spread_ref[...], dims, preferred_element_type=F32)
+        d_cat[depth + n * ne * cap : depth + (n + 1) * ne * cap] = wide.astype(BF)
+    ni, na = own_ref.shape[:2]
+    half_i = ni // 2
+    for h in range(2):
+        left = jnp.concatenate([late_ref[h], rest_ref[h], rest_got_ref[h]], 1)
+        sums = sums_ref[h] + jnp.dot(left, d_cat[...], preferred_element_type=F32)
+        for u in range(half_i):
+            i = h * half_i + u
+            own_ref[i] = keep_pair(sums[u * na : (u + 1) * na], pick_ref[i])
+
+
+def own_pair(pick, spread, sums, late, d, rest, rest_got, a4, b4):
+    depth = late.shape[2] + 2 * rest.shape[2]
+    return pl.pallas_call(
+        own_pair_kernel,
+        out_shape=jax.ShapeDtypeStruct(pick.shape, F32),
+        in_specs=[VMEM] * 9,
+        out_specs=VMEM,
+        scratch_shapes=[pltpu.VMEM((depth, d.shape[2]), BF)],
+        compiler_params=pltpu.CompilerParams(vmem_limit_bytes=12 * 2**20),
+        cost_estimate=pl.CostEstimate(
+            flops=4 * late.shape[1] * d.shape[2] * depth, bytes_accessed=4 * 2**20, transcendentals=0
+        ),
+        name="own_pair",
+    )(pick, spread, sums, late, d, rest, rest_got, a4, b4)
+
+
+def last_kernel(width_ref, bits_ref, expand_ref, own_ref, got_ref, out_ref, fits_ref):
+    fits_ref[0] = (width_ref[0, 0] <= CAP).astype(jnp.int32)
+    ni, na, lanes = own_ref.shape
+    sums = (own_ref[...] + got_ref[...]).astype(BF).reshape(ni * na, lanes)
+    wide = jnp.dot(sums, expand_ref[...], preferred_element_type=F32)
+    for i in range(ni):
+        keep = jnp.bitwise_and(bits_ref[...], 1 << i) != 0
+        out_ref[i] = jnp.where(keep, wide[i * na : (i + 1) * na], 0.0).astype(BF)
 
 
 def window_kernel(before_ref, *refs):
@@ -344,27 +545,33 @@
         give, pos, width = pack_give(window, virtual_irreps, w)
         got = lax.ppermute(give, "tr", SWAP)
         row, keep = pack_keep(window, pos, t, w)
-        t_parts, d_parts, a4, b4 = gather(keep, got, row)
-        other, t_cat, rest = other_part(t_parts, d_parts)
-        other, a4, b4 = lax.optimization_barrier((other, a4, b4))
-        got = lax.ppermute(other, "tr", SWAP)
-        rest_got = lax.ppermute(rest, "tr", SWAP)
-        own = own_part(t_cat, d_parts)
-        return (own, got, rest, rest_got, a4, b4), width
-
-    parts, width = one_pass(None)
+        return *gather(keep, got, row), pos, width
+
+    t_parts, d_parts, a4, b4, pos, width = one_pass(None)
+    bits, pick_own, pick_other, spread, expand = prepare(occupied_irreps, virtual_irreps, pos, na)
+    d_own, d_other = spread_blocks(spread, d_parts)
+    sums_own, sums_other = early_sums(t_parts[:-1], d_own, d_other)
+    other, t_late, rest = other_pair(pick_other, t_parts, sums_other, d_other)
+    other, a4, b4 = lax.optimization_barrier((other, a4, b4))
+    got = lax.ppermute(other, "tr", SWAP)
+    rest_got = lax.ppermute(rest, "tr", SWAP)
+    own = own_pair(pick_own, spread, sums_own, t_late, d_own, rest, rest_got, a4, b4)
     fast, fits = pl.pallas_call(
         last_kernel,
         out_shape=(jax.ShapeDtypeStruct((ni, na, v), BF), jax.ShapeDtypeStruct((1,), jnp.int32)),
-        in_specs=[VMEM, VMEM] + [VMEM] * len(parts),
+        in_specs=[VMEM] * 5,
         out_specs=(VMEM, SMEM),
         compiler_params=pltpu.CompilerParams(vmem_limit_bytes=8 * 2**20),
         name="last_part",
-    )(width, symmetric_bits(occupied_irreps, virtual_irreps, na), *parts)
+    )(width, bits, expand, own, got)
 
     def all_windows():
         def window(n, before):
-            parts, _ = one_pass(jnp.full((1,), n, jnp.int32))
+            t_parts, d_parts, a4, b4, _, _ = one_pass(jnp.full((1,), n, jnp.int32))
+            other, t_cat, rest = other_part(t_parts, d_parts)
+            got = lax.ppermute(other, "tr", SWAP)
+            rest_got = lax.ppermute(rest, "tr", SWAP)
+            parts = (own_part(t_cat, d_parts), got, rest, rest_got, a4, b4)
             return pl.pallas_call(
                 window_kernel,
                 out_shape=jax.ShapeDtypeStruct(before.shape, F32),
@@ -375,7 +582,7 @@
             )(before, *parts)
 
         windows = (width[0, 0] + CAP - 1) // CAP
-        sums = lax.fori_loop(0, windows, window, jnp.zeros(parts[0].shape, F32))
+        sums = lax.fori_loop(0, windows, window, jnp.zeros((2, ni // 2 * na, v), F32))
         label_j = occupied_irreps[lax.axis_index("tr")]
         labels_a = lax.dynamic_slice_in_dim(virtual_irreps, lax.axis_index("su") * na, na, 0)
         parity = jnp.bitwise_xor(occupied_irreps[:ni, None, None], label_j)

time: 46.8 us -> 42.7 us (0.912)
  waiting for transfers between devices: 9.49 us -> 6.01 us
  starting transfers between devices: 27.9 us -> 25.5 us
  Pallas kernels: 8 us -> 9.75 us
    ppermute x2, starting transfers between devices: 3.66 us -> 0.59 us  [the longest x1 0.5 us: body(): rest_got = lax.ppermute(rest, 'tr', SWAP)]
    pallas_call x3 -> x5, Pallas kernels: 3.61 us -> 5.58 us  [the longest x1 1.82 us: spread_blocks(): pl.pallas_call(spread_kernel, out_shape=(out, out), in_specs=[VMEM] * (1...]
    ppermute x6, waiting for transfers between devices: 3.91 us -> 1.99 us  [lines(): return [lax.ppermute(piece, 'tr', line(first, flip)) for flip in (1, 2, 3)]]
    ppermute x1, waiting for transfers between devices: 3.48 us -> 2.34 us  [gather(): b3 = lax.ppermute(a2, 'su', EVEN_LINKS)]
    ppermute x1, starting transfers between devices: 0.09 us -> 1.12 us  [gather(): a4 = lax.ppermute(b3[:1], 'su', ODD_LINKS)]
    ppermute x6, starting transfers between devices: 8 us -> 7.01 us  [lines(): return [lax.ppermute(piece, 'tr', line(first, flip)) for flip in (1, 2, 3)]]
    ppermute x1, waiting for transfers between devices: 0.9 us -> 0.17 us  [gather(): a3 = lax.ppermute(b2, 'su', ODD_LINKS)]
    ppermute x2, waiting for transfers between devices: 0.93 us -> 1.5 us  [the longest x1 1.49 us: body(): rest_got = lax.ppermute(rest, 'tr', SWAP)]
  transfers between devices with their start and end apart: 17 -> 17, of which waited for: 7 -> 4; matrix products, arithmetic and copies ran while one was open for 0% -> 0% of each run, Pallas kernels for 11% -> 17%
where the time goes in v4:
time: 42.7 us; the launch traced here: 42.5 us
  starting transfers between devices  25.5 us (60%)
  Pallas kernels  9.75 us (23%)
  waiting for transfers between devices  6.01 us (14%)
  between operations  0.98 us (2%)
    ppermute x6, starting transfers between devices, lines(): return [lax.ppermute(piece, 'tr', line(first, flip)) for flip in (1, 2, 3)]  7.01 us
    ppermute x1, starting transfers between devices, gather(): b4 = lax.ppermute(a3[1:], ('tr', 'su'), EVEN_LINKS_CROSSED)  4.94 us
    ppermute x1, starting transfers between devices, gather(): a1 = lax.ppermute(d, 'su', ODD_LINKS)  4.56 us
    ppermute x1, starting transfers between devices, one_pass(): got = lax.ppermute(give, 'tr', SWAP)  3.33 us
    ppermute x1, starting transfers between devices, gather(): a2 = lax.ppermute(b1, 'su', ODD_LINKS)  2.4 us
    ppermute x1, waiting for transfers between devices, gather(): b3 = lax.ppermute(a2, 'su', EVEN_LINKS)  2.34 us
    ppermute x6, waiting for transfers between devices, lines(): return [lax.ppermute(piece, 'tr', line(first, flip)) for flip in (1, 2, 3)]  1.99 us
    pallas_call x1, Pallas kernels, spread_blocks(): pl.pallas_call(spread_kernel, out_shape=(out, out), in_specs=[VMEM] * (1...  1.82 us
  transfers between devices with their start and end apart: 17, of which 4 were waited for; matrix products, arithmetic and copies ran while one was open for 0% of the time, Pallas kernels for 17%

profile of v4, /device:TPU:1, one launch (start us, length us, event | category | flops | bytes accessed | tf_op | source)
XLA Modules:
  0.0 42.5 jit_solution(12365198935218773924)
XLA Ops:
  0.0 1.5 %pack_give.2 = (bf16[1,2,64,384]{3,2,1,0:T(8,128)(2,1)S(1)}, s32[1,384]{1,0:T(1,128)S(1)}, s32[1,128]{1,0:T(1,128)S(1)}) custom-call(s32[384]{0:T(512)} %labels_ref.3, bf16[4,384,384]{2,1,0:T(8,128)(2,1)} %bitcast.15), custom_call_target="tpu_custom_call" | custom-call | tf_op jit(solution)/shard_map/pack_give/pallas_call | solution.py:133
  1.5 3.3 %collective-permute-start.22 = (bf16[1,2,64,384]{3,2,1,0:T(8,128)(2,1)S(1)}, bf16[1,2,64,384]{3,2,1,0:T(8,128)(2,1)S(1)}, u32[]{:S(2)}, u32[]{:S(2)}) collective-permute-start(bf16[1,2,64,384]{3,2,1,0:T(8,128)(2,1)S(1)} %get-tuple-element.96), channel_id=1, source_target_pairs={{0,8},{8,0},{16,24},{24,16},{32,40},{40,32},{48,56},{56,48},{64,72... | collective-permute-start | bytes 294920 | tf_op jit(solution)/shard_map/ppermute | solution.py:546
  4.8 1.5 %pack_keep.2 = (bf16[1,8,48,128]{3,2,1,0:T(8,128)(2,1)S(1)}, bf16[1,2,64,384]{3,2,1,0:T(8,128)(2,1)S(1)}) custom-call(s32[1,384]{1,0:T(1,128)S(1)} %get-tuple-element.89.pos_ref, bf16[16,48,384]{2,1,0:T(8,128)(2,1)} %bitcast.9.t_ref, bf16[4,384,384]{2,1,0:T(8,128)(2,1)S(1)} %bitcast.16), custom_call_target="tpu_custom_call" | custom-call | bytes 4194304 | tf_op jit(solution)/shard_map/pack_keep/pallas_call | solution.py:156
  6.4 0.1 collective-permute-start.24
  6.5 4.6 %collective-permute-start.23 = (bf16[2,2,64,384]{3,2,1,0:T(8,128)(2,1)S(1)}, bf16[2,2,64,384]{3,2,1,0:T(8,128)(2,1)S(1)}, u32[]{:S(2)}, u32[]{:S(2)}) collective-permute-start(bf16[2,2,64,384]{3,2,1,0:T(8,128)(2,1)S(1)} %join_w.2.refs_0_), channel_id=1, source_target_pairs={{0,7},{1,2},{2,1},{3,4},{4,3},{5,6},{6,5},{7,0},{8,15},{9,10},{10,... | collective-permute-start | bytes 589832 | tf_op jit(solution)/shard_map/ppermute | solution.py:226
  11.0 2.7 %collective-permute-start.19 = (bf16[1,8,48,128]{3,2,1,0:T(8,128)(2,1)S(1)}, bf16[1,8,48,128]{3,2,1,0:T(8,128)(2,1)S(1)}, u32[]{:S(2)}, u32[]{:S(2)}) collective-permute-start(bf16[1,8,48,128]{3,2,1,0:T(8,128)(2,1)S(1)} %get-tuple-element.94.refs_0_), channel_id=1, source_target_pairs={{0,192},{8,56},{16,208},{24,40},{32,224},{40,24},{48,240},{56,8},{... | collective-permute-start | bytes 294920 | tf_op jit(solution)/shard_map/ppermute | solution.py:220
  13.8 0.4 collective-permute-start.18
  14.1 0.2 collective-permute-start.17
  14.4 2.4 %collective-permute-start.25 = (bf16[2,2,64,384]{3,2,1,0:T(8,128)(2,1)S(1)}, bf16[2,2,64,384]{3,2,1,0:T(8,128)(2,1)S(1)}, u32[]{:S(2)}, u32[]{:S(2)}) collective-permute-start(bf16[2,2,64,384]{3,2,1,0:T(8,128)(2,1)S(1)} %collective-permute-done.24.refs_2_), channel_id=1, source_target_pairs={{0,7},{1,2},{2,1},{3,4},{4,3},{5,6},{6,5},{7,0},{8,15},{9,10},{10,... | collective-permute-start | bytes 589832 | tf_op jit(solution)/shard_map/ppermute | solution.py:230
  16.8 2.0 %collective-permute-done.18.refs_2_ = bf16[1,8,48,128]{3,2,1,0:T(8,128)(2,1)S(1)} collective-permute-done((bf16[1,8,48,128]{3,2,1,0:T(8,128)(2,1)S(1)}, bf16[1,8,48,128]{3,2,1,0:T(8,128)(2,1)S(1)}, u32[]{:S(2)}, u32[]{:S(2)}) %collective-permute-start.18) | collective-permute-done | bytes 98336 | tf_op jit(solution)/shard_map/ppermute | solution.py:220
  18.7 0.0 collective-permute-done.17.refs_1_
  18.8 2.8 %collective-permute-start.21 = (bf16[4,8,48,128]{3,2,1,0:T(8,128)(2,1)S(1)}, bf16[4,8,48,128]{3,2,1,0:T(8,128)(2,1)S(1)}, u32[]{:S(2)}, u32[]{:S(2)}) collective-permute-start(bf16[4,8,48,128]{3,2,1,0:T(8,128)(2,1)S(1)} %join_row.2.refs_0_), channel_id=1, source_target_pairs={{0,32},{8,136},{16,48},{24,152},{32,0},{40,168},{48,16},{56,184},{... | collective-permute-start | bytes 1179656 | tf_op jit(solution)/shard_map/ppermute | solution.py:220
  21.6 0.3 collective-permute-start.20
  21.9 0.6 %collective-permute-start.29 = (bf16[4,8,48,128]{3,2,1,0:T(8,128)(2,1)S(1)}, bf16[4,8,48,128]{3,2,1,0:T(8,128)(2,1)S(1)}, u32[]{:S(2)}, u32[]{:S(2)}) collective-permute-start(bf16[4,8,48,128]{3,2,1,0:T(8,128)(2,1)S(1)} %join_row.2.refs_0_), channel_id=1, source_target_pairs={{0,48},{8,200},{16,32},{24,216},{32,16},{40,232},{48,0},{56,248},{... | collective-permute-start | bytes 1179656 | tf_op jit(solution)/shard_map/ppermute | solution.py:220
  22.5 0.0 collective-permute-done.25.refs_3_
  22.5 0.0 collective-permute-start.28
  22.5 0.0 collective-permute-done.26.refs_4_
  22.5 1.5 %collective-permute-start.27 = (bf16[2,2,64,384]{3,2,1,0:T(8,128)(2,1)S(1)}, bf16[2,2,64,384]{3,2,1,0:T(8,128)(2,1)S(1)}, u32[]{:S(2)}, u32[]{:S(2)}) collective-permute-start(bf16[2,2,64,384]{3,2,1,0:T(8,128)(2,1)S(1)} %collective-permute-done.26.refs_4_), channel_id=1, source_target_pairs={{0,7},{1,2},{2,1},{3,4},{4,3},{5,6},{6,5},{7,0},{8,15},{9,10},{10,... | collective-permute-start | bytes 589832 | tf_op jit(solution)/shard_map/ppermute | solution.py:232
  24.0 1.0 %prepare.1 = (s32[48,384]{1,0:T(8,128)S(1)}, s32[16,48,128]{2,1,0:T(8,128)S(1)}, s32[16,48,128]{2,1,0:T(8,128)S(1)}, bf16[512,384]{1,0:T(8,128)(2,1)S(1)}, bf16[128,384]{1,0:T(8,128)(2,1)S(1)}) custom-call(s32[32]{0:T(128)S(1)} %copy-done.8, s32[384]{0:T(512)S(1)} %copy-done.7, s32[1,384]{1,0:T(1,128)S(1)} %get-tuple-element.89.pos_ref), custom_call_target="tpu_custom_call" | custom-call | tf_op jit(solution)/shard_map/prepare/pallas_call | solution.py:178
  25.0 2.3 %collective-permute-done.28.refs_6_ = bf16[2,2,64,384]{3,2,1,0:T(8,128)(2,1)S(1)} collective-permute-done((bf16[2,2,64,384]{3,2,1,0:T(8,128)(2,1)S(1)}, bf16[2,2,64,384]{3,2,1,0:T(8,128)(2,1)S(1)}, u32[]{:S(2)}, u32[]{:S(2)}) %collective-permute-start.28) | collective-permute-done | bytes 196640 | tf_op jit(solution)/shard_map/ppermute | solution.py:233
  27.3 1.1 %collective-permute-start.31 = (bf16[1,2,64,384]{3,2,1,0:T(8,128)(2,1)S(1)}, bf16[1,2,64,384]{3,2,1,0:T(8,128)(2,1)S(1)}, u32[]{:S(2)}, u32[]{:S(2)}) collective-permute-start(bf16[1,2,64,384]{3,2,1,0:T(8,128)(2,1)S(1)} %slice.22), channel_id=1, source_target_pairs={{0,7},{1,2},{2,1},{3,4},{4,3},{5,6},{6,5},{7,0},{8,15},{9,10},{10,... | collective-permute-start | bytes 294920 | tf_op jit(solution)/shard_map/ppermute | solution.py:234
  28.4 0.2 collective-permute-done.27.refs_5_
  28.6 4.9 %collective-permute-start.32 = (bf16[1,2,64,384]{3,2,1,0:T(8,128)(2,1)S(1)}, bf16[1,2,64,384]{3,2,1,0:T(8,128)(2,1)S(1)}, u32[]{:S(2)}, u32[]{:S(2)}) collective-permute-start(bf16[1,2,64,384]{3,2,1,0:T(8,128)(2,1)S(1)} %slice.23), channel_id=1, source_target_pairs={{0,9},{1,8},{2,11},{3,10},{4,13},{5,12},{6,15},{7,14},{8,1},{9,0},... | collective-permute-start | bytes 294920 | tf_op jit(solution)/shard_map/ppermute | solution.py:235
  33.6 1.8 %spread.1 = (bf16[16,64,512]{2,1,0:T(8,128)(2,1)S(1)}, bf16[16,64,512]{2,1,0:T(8,128)(2,1)S(1)}) custom-call(bf16[512,384]{1,0:T(8,128)(2,1)S(1)} %get-tuple-element.93.spread_ref, bf16[2,2,64,384]{3,2,1,0:T(8,128)(2,1)S(1)} %join_w.2.refs_0_, bf16[2,2,64,384]{3,2,1,0:T(8,128)(2,1)S(1)} %collective-permute-done.23.refs_1_, ...), custom_call_target="tpu_custom_call" | custom-call | flops 805306368 | bytes 4194304 | tf_op jit(solution)/shard_map/spread/pallas_call | solution.py:352
  35.4 1.5 %early_sums.1 = (f32[2,384,512]{2,1,0:T(8,128)S(1)}, f32[2,384,512]{2,1,0:T(8,128)S(1)}) custom-call(bf16[4,8,48,128]{3,2,1,0:T(8,128)(2,1)S(1)} %join_row.2.refs_0_, bf16[4,8,48,128]{3,2,1,0:T(8,128)(2,1)S(1)} %collective-permute-done.20.refs_1_, bf16[4,8,48,128]{3,2,1,0:T(8,128)(2,1)S(1)} %collective-permute-done.21.refs_2_, ...), custom_call_target="tpu_custom_call" | custom-call | flops 1207959552 | bytes 6291456 | tf_op jit(solution)/shard_map/early_sums/pallas_call | solution.py:410
  36.9 0.5 %other_pair.1 = (f32[16,48,128]{2,1,0:T(8,128)S(1)}, bf16[2,384,256]{2,1,0:T(8,128)(2,1)S(1)}, bf16[2,384,128]{2,1,0:T(8,128)(2,1)S(1)}) custom-call(s32[16,48,128]{2,1,0:T(8,128)S(1)} %get-tuple-element.100.pick_ref, bf16[4,8,48,128]{3,2,1,0:T(8,128)(2,1)S(1)} %join_row.2.refs_0_, bf16[4,8,48,128]{3,2,1,0:T(8,128)(2,1)S(1)} %collective-permute-done.20.refs_1_, ...), custom_call_target="tpu_custom_call" | custom-call | flops 201326592 | bytes 6291456 | tf_op jit(solution)/shard_map/other_pair/pallas_call | solution.py:471
  37.4 0.1 collective-permute-start.33
  37.5 0.5 %collective-permute-start.30 = (bf16[2,384,128]{2,1,0:T(8,128)(2,1)S(1)}, bf16[2,384,128]{2,1,0:T(8,128)(2,1)S(1)}, u32[]{:S(2)}, u32[]{:S(2)}) collective-permute-start(bf16[2,384,128]{2,1,0:T(8,128)(2,1)S(1)} %get-tuple-element.103.rest_ref), channel_id=1, source_target_pairs={{0,8},{8,0},{16,24},{24,16},{32,40},{40,32},{48,56},{56,48},{64,72... | collective-permute-start | bytes 589832 | tf_op jit(solution)/shard_map/ppermute | solution.py:557
  38.0 1.5 %collective-permute-done.30.rest_got_ref = bf16[2,384,128]{2,1,0:T(8,128)(2,1)S(1)} collective-permute-done((bf16[2,384,128]{2,1,0:T(8,128)(2,1)S(1)}, bf16[2,384,128]{2,1,0:T(8,128)(2,1)S(1)}, u32[]{:S(2)}, u32[]{:S(2)}) %collective-permute-start.30) | collective-permute-done | bytes 196640 | tf_op jit(solution)/shard_map/ppermute | solution.py:557
  39.5 0.8 %own_pair.1.own_ref = f32[16,48,128]{2,1,0:T(8,128)S(1)} custom-call(s32[16,48,128]{2,1,0:T(8,128)S(1)} %get-tuple-element.92.pick_ref, bf16[512,384]{1,0:T(8,128)(2,1)S(1)} %get-tuple-element.93.spread_ref, f32[2,384,512]{2,1,0:T(8,128)S(1)} %get-tuple-element.99.sums_ref, bf16[2,384,256]{2,1,0:T(8,128)(2,1)S(1)} %get-tuple-element.102.late_ref, ...), custom_call_target="tpu_custom_call" | custom-call | flops 402653184 | bytes 4194304 | tf_op jit(solution)/shard_map/own_pair/pallas_call | solution.py:509
  40.3 1.1 %last_part.1 = (bf16[16,48,384]{2,1,0:T(8,128)(2,1)}, s32[1]{0:T(128)}) custom-call(s32[1,128]{1,0:T(1,128)S(1)} %get-tuple-element.88.width_ref, s32[48,384]{1,0:T(8,128)S(1)} %get-tuple-element.90.bits_ref, bf16[128,384]{1,0:T(8,128)(2,1)S(1)} %get-tuple-element.91.expand_ref, f32[16,48,128]{2,1,0:T(8,128)S(1)} %own_pair.1.own_ref, ...), custom_call_target="tpu_custom_call" | custom-call | tf_op jit(solution)/shard_map/last_part/pallas_call | solution.py:559
  42.1 0.3 conditional.1
  (21 shorter events, 0.1 us)
Async XLA Ops:
  0.0 4.8 %copy-start.4 = (bf16[4,384,1,384]{3,1,2,0:T(8,128)(2,1)S(1)}, bf16[4,384,1,384]{3,1,2,0:T(8,128)(2,1)}, u32[]{:S(2)}) copy-start(bf16[4,384,1,384]{3,1,2,0:T(8,128)(2,1)} %param.9) | copy-start | bytes 3538948
  1.5 4.9 %collective-permute-start.22 = (bf16[1,2,64,384]{3,2,1,0:T(8,128)(2,1)S(1)}, bf16[1,2,64,384]{3,2,1,0:T(8,128)(2,1)S(1)}, u32[]{:S(2)}, u32[]{:S(2)}) collective-permute-start(bf16[1,2,64,384]{3,2,1,0:T(8,128)(2,1)S(1)} %get-tuple-element.96), channel_id=1, source_target_pairs={{0,8},{8,0},{16,24},{24,16},{32,40},{40,32},{48,56},{56,48},{64,72... | collective-permute-start | bytes 294920 | tf_op jit(solution)/shard_map/ppermute | solution.py:546
  4.8 19.1 %copy-start.7 = (s32[384]{0:T(512)S(1)}, s32[384]{0:T(512)}, u32[]{:S(2)}) copy-start(s32[384]{0:T(512)} %labels_ref.3) | copy-start | bytes 4612
  4.8 19.1 %copy-start.8 = (s32[32]{0:T(128)S(1)}, s32[32]{0:T(128)}, u32[]{:S(2)}) copy-start(s32[32]{0:T(128)} %occ_ref.1) | copy-start | bytes 388
  6.4 8.0 %collective-permute-start.24 = (bf16[2,2,64,384]{3,2,1,0:T(8,128)(2,1)S(1)}, bf16[2,2,64,384]{3,2,1,0:T(8,128)(2,1)S(1)}, u32[]{:S(2)}, u32[]{:S(2)}) collective-permute-start(bf16[2,2,64,384]{3,2,1,0:T(8,128)(2,1)S(1)} %join_w.2.refs_0_), channel_id=1, source_target_pairs={{0,1},{1,0},{2,3},{3,2},{4,5},{5,4},{6,7},{7,6},{8,9},{9,8},{10,11... | collective-permute-start | bytes 589832 | tf_op jit(solution)/shard_map/ppermute | solution.py:227
  6.5 10.3 %collective-permute-start.23 = (bf16[2,2,64,384]{3,2,1,0:T(8,128)(2,1)S(1)}, bf16[2,2,64,384]{3,2,1,0:T(8,128)(2,1)S(1)}, u32[]{:S(2)}, u32[]{:S(2)}) collective-permute-start(bf16[2,2,64,384]{3,2,1,0:T(8,128)(2,1)S(1)} %join_w.2.refs_0_), channel_id=1, source_target_pairs={{0,7},{1,2},{2,1},{3,4},{4,3},{5,6},{6,5},{7,0},{8,15},{9,10},{10,... | collective-permute-start | bytes 589832 | tf_op jit(solution)/shard_map/ppermute | solution.py:226
  11.0 5.7 %collective-permute-start.19 = (bf16[1,8,48,128]{3,2,1,0:T(8,128)(2,1)S(1)}, bf16[1,8,48,128]{3,2,1,0:T(8,128)(2,1)S(1)}, u32[]{:S(2)}, u32[]{:S(2)}) collective-permute-start(bf16[1,8,48,128]{3,2,1,0:T(8,128)(2,1)S(1)} %get-tuple-element.94.refs_0_), channel_id=1, source_target_pairs={{0,192},{8,56},{16,208},{24,40},{32,224},{40,24},{48,240},{56,8},{... | collective-permute-start | bytes 294920 | tf_op jit(solution)/shard_map/ppermute | solution.py:220
  13.8 5.0 %collective-permute-start.18 = (bf16[1,8,48,128]{3,2,1,0:T(8,128)(2,1)S(1)}, bf16[1,8,48,128]{3,2,1,0:T(8,128)(2,1)S(1)}, u32[]{:S(2)}, u32[]{:S(2)}) collective-permute-start(bf16[1,8,48,128]{3,2,1,0:T(8,128)(2,1)S(1)} %get-tuple-element.94.refs_0_), channel_id=1, source_target_pairs={{0,128},{8,40},{16,144},{24,56},{32,160},{40,8},{48,176},{56,24},{... | collective-permute-start | bytes 294920 | tf_op jit(solution)/shard_map/ppermute | solution.py:220
  14.1 4.6 %collective-permute-start.17 = (bf16[1,8,48,128]{3,2,1,0:T(8,128)(2,1)S(1)}, bf16[1,8,48,128]{3,2,1,0:T(8,128)(2,1)S(1)}, u32[]{:S(2)}, u32[]{:S(2)}) collective-permute-start(bf16[1,8,48,128]{3,2,1,0:T(8,128)(2,1)S(1)} %get-tuple-element.94.refs_0_), channel_id=1, source_target_pairs={{0,64},{8,24},{16,80},{24,8},{32,96},{40,56},{48,112},{56,40},{64,... | collective-permute-start | bytes 294920 | tf_op jit(solution)/shard_map/ppermute | solution.py:220
  14.4 8.1 %collective-permute-start.25 = (bf16[2,2,64,384]{3,2,1,0:T(8,128)(2,1)S(1)}, bf16[2,2,64,384]{3,2,1,0:T(8,128)(2,1)S(1)}, u32[]{:S(2)}, u32[]{:S(2)}) collective-permute-start(bf16[2,2,64,384]{3,2,1,0:T(8,128)(2,1)S(1)} %collective-permute-done.24.refs_2_), channel_id=1, source_target_pairs={{0,7},{1,2},{2,1},{3,4},{4,3},{5,6},{6,5},{7,0},{8,15},{9,10},{10,... | collective-permute-start | bytes 589832 | tf_op jit(solution)/shard_map/ppermute | solution.py:230
  16.8 5.7 %collective-permute-start.26 = (bf16[2,2,64,384]{3,2,1,0:T(8,128)(2,1)S(1)}, bf16[2,2,64,384]{3,2,1,0:T(8,128)(2,1)S(1)}, u32[]{:S(2)}, u32[]{:S(2)}) collective-permute-start(bf16[2,2,64,384]{3,2,1,0:T(8,128)(2,1)S(1)} %collective-permute-done.23.refs_1_), channel_id=1, source_target_pairs={{0,1},{1,0},{2,3},{3,2},{4,5},{5,4},{6,7},{7,6},{8,9},{9,8},{10,11... | collective-permute-start | bytes 589832 | tf_op jit(solution)/shard_map/ppermute | solution.py:231
  18.8 16.6 %collective-permute-start.21 = (bf16[4,8,48,128]{3,2,1,0:T(8,128)(2,1)S(1)}, bf16[4,8,48,128]{3,2,1,0:T(8,128)(2,1)S(1)}, u32[]{:S(2)}, u32[]{:S(2)}) collective-permute-start(bf16[4,8,48,128]{3,2,1,0:T(8,128)(2,1)S(1)} %join_row.2.refs_0_), channel_id=1, source_target_pairs={{0,32},{8,136},{16,48},{24,152},{32,0},{40,168},{48,16},{56,184},{... | collective-permute-start | bytes 1179656 | tf_op jit(solution)/shard_map/ppermute | solution.py:220
  21.6 13.8 %collective-permute-start.20 = (bf16[4,8,48,128]{3,2,1,0:T(8,128)(2,1)S(1)}, bf16[4,8,48,128]{3,2,1,0:T(8,128)(2,1)S(1)}, u32[]{:S(2)}, u32[]{:S(2)}) collective-permute-start(bf16[4,8,48,128]{3,2,1,0:T(8,128)(2,1)S(1)} %join_row.2.refs_0_), channel_id=1, source_target_pairs={{0,16},{8,72},{16,0},{24,88},{32,48},{40,104},{48,32},{56,120},{64... | collective-permute-start | bytes 1179656 | tf_op jit(solution)/shard_map/ppermute | solution.py:220
  21.9 15.0 %collective-permute-start.29 = (bf16[4,8,48,128]{3,2,1,0:T(8,128)(2,1)S(1)}, bf16[4,8,48,128]{3,2,1,0:T(8,128)(2,1)S(1)}, u32[]{:S(2)}, u32[]{:S(2)}) collective-permute-start(bf16[4,8,48,128]{3,2,1,0:T(8,128)(2,1)S(1)} %join_row.2.refs_0_), channel_id=1, source_target_pairs={{0,48},{8,200},{16,32},{24,216},{32,16},{40,232},{48,0},{56,248},{... | collective-permute-start | bytes 1179656 | tf_op jit(solution)/shard_map/ppermute | solution.py:220
  22.5 4.8 %collective-permute-start.28 = (bf16[2,2,64,384]{3,2,1,0:T(8,128)(2,1)S(1)}, bf16[2,2,64,384]{3,2,1,0:T(8,128)(2,1)S(1)}, u32[]{:S(2)}, u32[]{:S(2)}) collective-permute-start(bf16[2,2,64,384]{3,2,1,0:T(8,128)(2,1)S(1)} %collective-permute-done.25.refs_3_), channel_id=1, source_target_pairs={{0,1},{1,0},{2,3},{3,2},{4,5},{5,4},{6,7},{7,6},{8,9},{9,8},{10,11... | collective-permute-start | bytes 589832 | tf_op jit(solution)/shard_map/ppermute | solution.py:233
  22.5 6.1 %collective-permute-start.27 = (bf16[2,2,64,384]{3,2,1,0:T(8,128)(2,1)S(1)}, bf16[2,2,64,384]{3,2,1,0:T(8,128)(2,1)S(1)}, u32[]{:S(2)}, u32[]{:S(2)}) collective-permute-start(bf16[2,2,64,384]{3,2,1,0:T(8,128)(2,1)S(1)} %collective-permute-done.26.refs_4_), channel_id=1, source_target_pairs={{0,7},{1,2},{2,1},{3,4},{4,3},{5,6},{6,5},{7,0},{8,15},{9,10},{10,... | collective-permute-start | bytes 589832 | tf_op jit(solution)/shard_map/ppermute | solution.py:232
  27.3 10.1 %collective-permute-start.31 = (bf16[1,2,64,384]{3,2,1,0:T(8,128)(2,1)S(1)}, bf16[1,2,64,384]{3,2,1,0:T(8,128)(2,1)S(1)}, u32[]{:S(2)}, u32[]{:S(2)}) collective-permute-start(bf16[1,2,64,384]{3,2,1,0:T(8,128)(2,1)S(1)} %slice.22), channel_id=1, source_target_pairs={{0,7},{1,2},{2,1},{3,4},{4,3},{5,6},{6,5},{7,0},{8,15},{9,10},{10,... | collective-permute-start | bytes 294920 | tf_op jit(solution)/shard_map/ppermute | solution.py:234
  28.6 8.8 %collective-permute-start.32 = (bf16[1,2,64,384]{3,2,1,0:T(8,128)(2,1)S(1)}, bf16[1,2,64,384]{3,2,1,0:T(8,128)(2,1)S(1)}, u32[]{:S(2)}, u32[]{:S(2)}) collective-permute-start(bf16[1,2,64,384]{3,2,1,0:T(8,128)(2,1)S(1)} %slice.23), channel_id=1, source_target_pairs={{0,9},{1,8},{2,11},{3,10},{4,13},{5,12},{6,15},{7,14},{8,1},{9,0},... | collective-permute-start | bytes 294920 | tf_op jit(solution)/shard_map/ppermute | solution.py:235
  37.4 2.9 %collective-permute-start.33 = (f32[16,48,128]{2,1,0:T(8,128)S(1)}, f32[16,48,128]{2,1,0:T(8,128)S(1)}, u32[]{:S(2)}, u32[]{:S(2)}) collective-permute-start(f32[16,48,128]{2,1,0:T(8,128)S(1)} %get-tuple-element.107), channel_id=1, source_target_pairs={{0,8},{8,0},{16,24},{24,16},{32,40},{40,32},{48,56},{56,48},{64,72... | collective-permute-start | bytes 1179656 | tf_op jit(solution)/shard_map/ppermute | solution.py:556
  37.5 2.0 %collective-permute-start.30 = (bf16[2,384,128]{2,1,0:T(8,128)(2,1)S(1)}, bf16[2,384,128]{2,1,0:T(8,128)(2,1)S(1)}, u32[]{:S(2)}, u32[]{:S(2)}) collective-permute-start(bf16[2,384,128]{2,1,0:T(8,128)(2,1)S(1)} %get-tuple-element.103.rest_ref), channel_id=1, source_target_pairs={{0,8},{8,0},{16,24},{24,16},{32,40},{40,32},{48,56},{56,48},{64,72... | collective-permute-start | bytes 589832 | tf_op jit(solution)/shard_map/ppermute | solution.py:557

commit v5 on v4

--- a/solution.py
+++ b/solution.py
@@ -32,7 +32,6 @@
     return pairs
 
 
-EVEN_LINKS_CROSSED = [(d * NZ + z, (d ^ 1) * NZ + to) for d in range(2 * NX * NY) for z, to in EVEN_LINKS]
 SWAP = [(d, d ^ 1) for d in range(2 * NX * NY)]
 
 
@@ -220,7 +219,7 @@
     return [lax.ppermute(piece, "tr", line(first, flip)) for flip in (1, 2, 3)]
 
 
-def gather(keep, got, t):
+def gather(keep, got, t, beside=lambda parts: ()):
     rows = lines(t, True)
     d = join("join_w", keep, got)
     a1 = lax.ppermute(d, "su", ODD_LINKS)
@@ -231,9 +230,10 @@
     b2 = lax.ppermute(a1, "su", EVEN_LINKS)
     a3 = lax.ppermute(b2, "su", ODD_LINKS)
     b3 = lax.ppermute(a2, "su", EVEN_LINKS)
+    extra, a3 = lax.optimization_barrier((beside([d, a1, b1, a2, b2]), a3))
     a4 = lax.ppermute(b3[:1], "su", ODD_LINKS)
-    b4 = lax.ppermute(a3[1:], ("tr", "su"), EVEN_LINKS_CROSSED)
-    return [row, *planes], [d, a1, b1, a2, b2, a3, b3], a4, b4
+    b4 = lax.ppermute(a3[1:], "su", EVEN_LINKS)
+    return [row, *planes], [d, a1, b1, a2, b2, a3, b3], a4, b4, extra
 
 
 def blocks(d_refs, j, d_cat):
@@ -327,39 +327,61 @@
     )(t_cat, *d_parts)
 
 
-def total(h, own_ref, got_ref, rest_ref, rest_got_ref, a4_ref, b4_ref):
-    _, ne, cap, v = a4_ref.shape
-    left = jnp.concatenate([rest_ref[h], rest_got_ref[h]], 1)
-    right = jnp.concatenate([a4_ref[0].reshape(ne * cap, v), b4_ref[0].reshape(ne * cap, v)], 0)
-    return own_ref[h] + got_ref[h] + jnp.dot(left, right, preferred_element_type=F32)
+def far_sum(h, sums_ref, rest_ref, d_ref):
+    _, ne, cap, v = d_ref.shape
+    return sums_ref[h] + jnp.dot(rest_ref[h], d_ref[0].reshape(ne * cap, v), preferred_element_type=F32)
+
+
+def far_kernel(sums_ref, rest_ref, d_ref, out_ref):
+    for h in range(2):
+        out_ref[h] = far_sum(h, sums_ref, rest_ref, d_ref)
+
+
+def far_part(sums, rest, d):
+    return pl.pallas_call(
+        far_kernel,
+        out_shape=jax.ShapeDtypeStruct(sums.shape, F32),
+        in_specs=[VMEM] * 3,
+        out_specs=VMEM,
+        compiler_params=pltpu.CompilerParams(vmem_limit_bytes=8 * 2**20),
+        name="far_part",
+    )(sums, rest, d)
 
 
 def spread_kernel(spread_ref, *refs):
-    d_refs, outs = refs[:-2], refs[-2:]
-    _, ne, cap, v = d_refs[0].shape
+    d_refs, (own_ref, other_ref, d_cat) = refs[:-3], refs[-3:]
     dims = (((1,), (1,)), ((), ()))
-    for j in range(2):
-        for n, d_ref in enumerate(d_refs):
-            block = d_ref[j].reshape(ne * cap, v)
-            wide = lax.dot_general(block, spread_ref[...], dims, preferred_element_type=F32)
-            outs[j][n * ne : (n + 1) * ne] = wide.astype(BF).reshape(ne, cap, -1)
-        outs[j][len(d_refs) * ne :] = jnp.zeros((ne, cap, spread_ref.shape[0]), BF)
+    for j, ref in enumerate((own_ref, other_ref)):
+        blocks(d_refs, j, d_cat)
+        wide = lax.dot_general(d_cat[...], spread_ref[...], dims, preferred_element_type=F32)
+        ref[...] = wide.astype(BF).reshape(ref.shape)
 
 
 def spread_blocks(spread, d_parts):
     _, ne, cap, v = d_parts[0].shape
-    out = jax.ShapeDtypeStruct((NZ * ne, cap, spread.shape[0]), BF)
+    count = len(d_parts) * ne
+    out = jax.ShapeDtypeStruct((count, cap, spread.shape[0]), BF)
     return pl.pallas_call(
         spread_kernel,
         out_shape=(out, out),
         in_specs=[VMEM] * (1 + len(d_parts)),
         out_specs=(VMEM, VMEM),
+        scratch_shapes=[pltpu.VMEM((count * cap, v), BF)],
         compiler_params=pltpu.CompilerParams(vmem_limit_bytes=8 * 2**20),
         cost_estimate=pl.CostEstimate(
-            flops=4 * NZ * ne * cap * v * spread.shape[0], bytes_accessed=4 * 2**20, transcendentals=0
+            flops=4 * count * cap * v * spread.shape[0], bytes_accessed=4 * 2**20, transcendentals=0
         ),
         name="spread",
     )(spread, *d_parts)
+
+
+def put_block(d_early, d_late, first, second, d_cat, at):
+    src = block_at(first, second)
+    early, late = d_early.shape[0], d_late.shape[0]
+    near = d_early[jnp.minimum(src, early - 1)]
+    far = d_late[jnp.clip(src - early, 0, late - 1)]
+    far = jnp.where(src < early + late, far, jnp.zeros_like(far))
+    d_cat[at : at + CAP] = jnp.where(src < early, near, far)
 
 
 def block_at(first, second):
@@ -384,7 +406,7 @@
 
 
 def early_kernel(*refs):
-    t_refs, (d_own, d_other, own_ref, other_ref, t_cat, d_cat) = refs[:-6], refs[-6:]
+    t_refs, (d_early, d_late, other_ref, t_cat, d_cat) = refs[:-5], refs[-5:]
     lanes = 2 * CAP
     for second, t_ref in enumerate(t_refs):
         for p in range(NX // 2):
@@ -393,30 +415,26 @@
             for h in range(2):
                 t_cat[h, :, at : at + lanes] = pair_lanes(one, two, h)
             for u in range(2):
-                src = block_at(2 * p + u, second)
-                d_cat[0, at + u * CAP : at + (u + 1) * CAP] = d_own[src]
-                d_cat[1, at + u * CAP : at + (u + 1) * CAP] = d_other[src]
-    for j, ref in enumerate((own_ref, other_ref)):
-        for h in range(2):
-            ref[h] = jnp.dot(t_cat[h], d_cat[j], preferred_element_type=F32)
-
-
-def early_sums(t_parts, d_own, d_other):
+                put_block(d_early, d_late, 2 * p + u, second, d_cat, at + u * CAP)
+    for h in range(2):
+        other_ref[h] = jnp.dot(t_cat[h], d_cat[...], preferred_element_type=F32)
+
+
+def early_sums(t_parts, d_other):
     chips, half_i, na, lanes = t_parts[0].shape
     rows = half_i * na
     depth = len(t_parts) * chips * CAP
-    wide = d_own.shape[2]
-    out = jax.ShapeDtypeStruct((2, rows, wide), F32)
+    wide = d_other[0].shape[2]
     return pl.pallas_call(
         early_kernel,
-        out_shape=(out, out),
+        out_shape=(jax.ShapeDtypeStruct((2, rows, wide), F32), jax.ShapeDtypeStruct((2, rows, depth), BF)),
         in_specs=[VMEM] * (len(t_parts) + 2),
         out_specs=(VMEM, VMEM),
-        scratch_shapes=[pltpu.VMEM((2, rows, depth), BF), pltpu.VMEM((2, depth, wide), BF)],
+        scratch_shapes=[pltpu.VMEM((depth, wide), BF)],
         compiler_params=pltpu.CompilerParams(vmem_limit_bytes=16 * 2**20),
-        cost_estimate=pl.CostEstimate(flops=8 * rows * wide * depth, bytes_accessed=6 * 2**20, transcendentals=0),
+        cost_estimate=pl.CostEstimate(flops=4 * rows * wide * depth, bytes_accessed=6 * 2**20, transcendentals=0),
         name="early_sums",
-    )(*t_parts, d_own, d_other)
+    )(*t_parts, *d_other)
 
 
 def keep_pair(sums, pick):
@@ -427,20 +445,16 @@
     return out
 
 
-def late_blocks(d_ref, d_cat):
-    for first in range(NX):
-        d_cat[first * CAP : (first + 1) * CAP] = d_ref[block_at(first, NX - 1)]
-
-
 def other_pair_kernel(pick_ref, *refs):
-    t_refs, (sums_ref, d_ref, other_ref, late_ref, rest_ref, d_cat) = refs[:NX], refs[NX:]
+    t_refs, (sums_ref, d_early, d_late, other_ref, late_ref, rest_ref, d_cat) = refs[:NX], refs[NX:]
     last = t_refs[-1]
     lanes = 2 * CAP
     for p in range(NX // 2):
         one, two = flat(last[2 * p]), flat(last[2 * p + 1])
         for h in range(2):
             late_ref[h, :, p * lanes : (p + 1) * lanes] = pair_lanes(one, two, h)
-    late_blocks(d_ref, d_cat)
+    for first in range(NX):
+        put_block(d_early, d_late, first, NX - 1, d_cat, first * CAP)
     ni, na = other_ref.shape[:2]
     half_i = ni // 2
     for h in range(2):
@@ -475,49 +489,80 @@
             jax.ShapeDtypeStruct((2, rows, chips * CAP), BF),
             jax.ShapeDtypeStruct((2, rows, lanes), BF),
         ),
-        in_specs=[VMEM] * (3 + len(t_parts)),
+        in_specs=[VMEM] * (4 + len(t_parts)),
         out_specs=(VMEM, VMEM, VMEM),
-        scratch_shapes=[pltpu.VMEM((chips * CAP, d.shape[2]), BF)],
+        scratch_shapes=[pltpu.VMEM((chips * CAP, sums.shape[2]), BF)],
         compiler_params=pltpu.CompilerParams(vmem_limit_bytes=12 * 2**20),
         cost_estimate=pl.CostEstimate(
-            flops=4 * rows * d.shape[2] * chips * CAP, bytes_accessed=6 * 2**20, transcendentals=0
+            flops=4 * rows * sums.shape[2] * chips * CAP, bytes_accessed=6 * 2**20, transcendentals=0
         ),
         name="other_pair",
-    )(pick, *t_parts, sums, d)
-
-
-def own_pair_kernel(pick_ref, spread_ref, sums_ref, late_ref, d_ref, rest_ref, rest_got_ref, a4_ref, b4_ref, own_ref, d_cat):
-    _, ne, cap, v = a4_ref.shape
-    depth = late_ref.shape[2]
-    late_blocks(d_ref, d_cat)
+    )(pick, *t_parts, sums, *d)
+
+
+def spread_far(d_ref, spread_ref):
+    _, ne, cap, v = d_ref.shape
     dims = (((1,), (1,)), ((), ()))
-    for n, ref in enumerate((a4_ref, b4_ref)):
-        wide = lax.dot_general(ref[0].reshape(ne * cap, v), spread_ref[...], dims, preferred_element_type=F32)
-        d_cat[depth + n * ne * cap : depth + (n + 1) * ne * cap] = wide.astype(BF)
+    wide = lax.dot_general(d_ref[0].reshape(ne * cap, v), spread_ref[...], dims, preferred_element_type=F32)
+    return wide.astype(BF)
+
+
+def far_pair_kernel(pick_ref, spread_ref, sums_ref, rest_ref, d_ref, out_ref):
+    right = spread_far(d_ref, spread_ref)
+    ni, na = out_ref.shape[:2]
+    half_i = ni // 2
+    for h in range(2):
+        sums = jnp.dot(rest_ref[h], right, preferred_element_type=F32)
+        for u in range(half_i):
+            i = h * half_i + u
+            out_ref[i] = sums_ref[i] + keep_pair(sums[u * na : (u + 1) * na], pick_ref[i])
+
+
+def far_pair(pick, spread, sums, rest, d):
+    return pl.pallas_call(
+        far_pair_kernel,
+        out_shape=jax.ShapeDtypeStruct(pick.shape, F32),
+        in_specs=[VMEM] * 5,
+        out_specs=VMEM,
+        compiler_params=pltpu.CompilerParams(vmem_limit_bytes=8 * 2**20),
+        name="far_pair",
+    )(pick, spread, sums, rest, d)
+
+
+def own_pair_kernel(
+    pick_ref, spread_ref, t_cat, late_ref, d_early, d_late, rest_ref, far_ref, own_ref, left_cat, d_cat
+):
+    at = 0
+    for ref in (t_cat, late_ref, rest_ref):
+        left_cat[:, :, at : at + ref.shape[2]] = ref[...]
+        at += ref.shape[2]
+    for second in range(NX):
+        for first in range(NX):
+            put_block(d_early, d_late, first, second, d_cat, (second * NX + first) * CAP)
+    d_cat[NX * NX * CAP :] = spread_far(far_ref, spread_ref)
     ni, na = own_ref.shape[:2]
     half_i = ni // 2
     for h in range(2):
-        left = jnp.concatenate([late_ref[h], rest_ref[h], rest_got_ref[h]], 1)
-        sums = sums_ref[h] + jnp.dot(left, d_cat[...], preferred_element_type=F32)
+        sums = jnp.dot(left_cat[h], d_cat[...], preferred_element_type=F32)
         for u in range(half_i):
             i = h * half_i + u
             own_ref[i] = keep_pair(sums[u * na : (u + 1) * na], pick_ref[i])
 
 
-def own_pair(pick, spread, sums, late, d, rest, rest_got, a4, b4):
-    depth = late.shape[2] + 2 * rest.shape[2]
+def own_pair(pick, spread, t_cat, late, d, rest, far):
+    rows = late.shape[1]
+    depth = t_cat.shape[2] + late.shape[2] + rest.shape[2]
+    wide = d[0].shape[2]
     return pl.pallas_call(
         own_pair_kernel,
         out_shape=jax.ShapeDtypeStruct(pick.shape, F32),
-        in_specs=[VMEM] * 9,
+        in_specs=[VMEM] * 8,
         out_specs=VMEM,
-        scratch_shapes=[pltpu.VMEM((depth, d.shape[2]), BF)],
+        scratch_shapes=[pltpu.VMEM((2, rows, depth), BF), pltpu.VMEM((depth, wide), BF)],
         compiler_params=pltpu.CompilerParams(vmem_limit_bytes=12 * 2**20),
-        cost_estimate=pl.CostEstimate(
-            flops=4 * late.shape[1] * d.shape[2] * depth, bytes_accessed=4 * 2**20, transcendentals=0
-        ),
+        cost_estimate=pl.CostEstimate(flops=4 * rows * wide * depth, bytes_accessed=4 * 2**20, transcendentals=0),
         name="own_pair",
-    )(pick, spread, sums, late, d, rest, rest_got, a4, b4)
+    )(pick, spread, t_cat, late, *d, rest, far)
 
 
 def last_kernel(width_ref, bits_ref, expand_ref, own_ref, got_ref, out_ref, fits_ref):
@@ -530,10 +575,9 @@
         out_ref[i] = jnp.where(keep, wide[i * na : (i + 1) * na], 0.0).astype(BF)
 
 
-def window_kernel(before_ref, *refs):
-    parts, out_ref = refs[:-1], refs[-1]
-    for h in range(2):
-        out_ref[h] = before_ref[h] + total(h, *parts)
+def window_kernel(before_ref, own_ref, got_ref, rest_ref, d_ref, out_ref):
+    for h in range(2):
+        out_ref[h] = before_ref[h] + far_sum(h, own_ref, rest_ref, d_ref) + got_ref[h]
 
 
 def body(amplitudes, integrals, occupied_irreps, virtual_irreps):
@@ -541,21 +585,22 @@
     t = amplitudes.reshape(ni, na, v)
     w = integrals.reshape(integrals.shape[0], v, v)
 
-    def one_pass(window):
+    def pack(window):
         give, pos, width = pack_give(window, virtual_irreps, w)
         got = lax.ppermute(give, "tr", SWAP)
         row, keep = pack_keep(window, pos, t, w)
-        return *gather(keep, got, row), pos, width
-
-    t_parts, d_parts, a4, b4, pos, width = one_pass(None)
+        return keep, got, row, pos, width
+
+    keep, got, row, pos, width = pack(None)
     bits, pick_own, pick_other, spread, expand = prepare(occupied_irreps, virtual_irreps, pos, na)
-    d_own, d_other = spread_blocks(spread, d_parts)
-    sums_own, sums_other = early_sums(t_parts[:-1], d_own, d_other)
+    t_parts, d_parts, a4, b4, d_two = gather(keep, got, row, functools.partial(spread_blocks, spread))
+    d_three = spread_blocks(spread, d_parts[5:])
+    d_own, d_other = zip(d_two, d_three)
+    sums_other, t_cat = early_sums(t_parts[:-1], d_other)
     other, t_late, rest = other_pair(pick_other, t_parts, sums_other, d_other)
     other, a4, b4 = lax.optimization_barrier((other, a4, b4))
-    got = lax.ppermute(other, "tr", SWAP)
-    rest_got = lax.ppermute(rest, "tr", SWAP)
-    own = own_pair(pick_own, spread, sums_own, t_late, d_own, rest, rest_got, a4, b4)
+    got = lax.ppermute(far_pair(pick_other, spread, other, rest, b4), "tr", SWAP)
+    own = own_pair(pick_own, spread, t_cat, t_late, d_own, rest, a4)
     fast, fits = pl.pallas_call(
         last_kernel,
         out_shape=(jax.ShapeDtypeStruct((ni, na, v), BF), jax.ShapeDtypeStruct((1,), jnp.int32)),
@@ -567,11 +612,11 @@
 
     def all_windows():
         def window(n, before):
-            t_parts, d_parts, a4, b4, _, _ = one_pass(jnp.full((1,), n, jnp.int32))
+            keep, got, row, _, _ = pack(jnp.full((1,), n, jnp.int32))
+            t_parts, d_parts, a4, b4, _ = gather(keep, got, row)
             other, t_cat, rest = other_part(t_parts, d_parts)
-            got = lax.ppermute(other, "tr", SWAP)
-            rest_got = lax.ppermute(rest, "tr", SWAP)
-            parts = (own_part(t_cat, d_parts), got, rest, rest_got, a4, b4)
+            got = lax.ppermute(far_part(other, rest, b4), "tr", SWAP)
+            parts = (own_part(t_cat, d_parts), got, rest, a4)
             return pl.pallas_call(
                 window_kernel,
                 out_shape=jax.ShapeDtypeStruct(before.shape, F32),

time: 42.7 us -> 41.1 us (0.963)
  starting transfers between devices: 25.5 us -> 24.2 us
    ppermute x6, waiting for transfers between devices: 1.99 us -> 4.07 us  [lines(): return [lax.ppermute(piece, 'tr', line(first, flip)) for flip in (1, 2, 3)]]
    ppermute x4 -> x3, waiting for transfers between devices: 1.5 us -> 0.01 us  [the longest x1 0.01 us: body(): lax.ppermute(far_pair(pick_other, spread, other, rest, b4), 'tr', SWAP)]
    ppermute x4 -> x3, starting transfers between devices: 8.86 us -> 7.59 us  [the longest x1 3.83 us: body(): lax.ppermute(far_pair(pick_other, spread, other, rest, b4), 'tr', SWAP)]
    ppermute x1, waiting for transfers between devices: 2.34 us -> 1.42 us  [gather(): b3 = lax.ppermute(a2, 'su', EVEN_LINKS)]
    pallas_call x1, Pallas kernels: 0.82 us -> 1.39 us  [own_pair(): pl.pallas_call(own_pair_kernel, out_shape=jax.ShapeDtypeStruct(pick.shape...]
    pallas_call x1 -> x2, Pallas kernels: 1.82 us -> 1.39 us  [spread_blocks(): pl.pallas_call(spread_kernel, out_shape=(out, out), in_specs=[VMEM] * (1...]
    pallas_call x1 -> x2, Pallas kernels: 1.46 us -> 1.59 us  [the longest x1 0.99 us: early_sums(): pl.pallas_call(early_kernel, out_shape=(jax.ShapeDtypeStruct((2, rows, wi...]
  transfers between devices with their start and end apart: 17 -> 16, of which waited for: 4 -> 4; matrix products, arithmetic and copies ran while one was open for 0% -> 0% of each run, Pallas kernels for 17% -> 17%
where the time goes in v5:
time: 41.1 us; the launch traced here: 41 us
  starting transfers between devices  24.2 us (59%)
  Pallas kernels  10 us (24%)
  waiting for transfers between devices  5.68 us (14%)
  between operations  1.01 us (2%)
    ppermute x6, starting transfers between devices, lines(): return [lax.ppermute(piece, 'tr', line(first, flip)) for flip in (1, 2, 3)]  7.01 us
    ppermute x1, starting transfers between devices, gather(): a1 = lax.ppermute(d, 'su', ODD_LINKS)  4.56 us
    ppermute x6, waiting for transfers between devices, lines(): return [lax.ppermute(piece, 'tr', line(first, flip)) for flip in (1, 2, 3)]  4.07 us
    ppermute x1, starting transfers between devices, body(): lax.ppermute(far_pair(pick_other, spread, other, rest, b4), 'tr', SWAP)  3.83 us
    ppermute x1, starting transfers between devices, pack(): got = lax.ppermute(give, 'tr', SWAP)  3.33 us
    ppermute x1, starting transfers between devices, gather(): a2 = lax.ppermute(b1, 'su', ODD_LINKS)  2.4 us
    pallas_call x1, Pallas kernels, pack_keep(): pl.pallas_call(kernel, out_shape=(jax.ShapeDtypeStruct((1, ni // 2, na, 2...  1.51 us
    pallas_call x1, Pallas kernels, pack_give(): pl.pallas_call(kernel, out_shape=(jax.ShapeDtypeStruct((1, nk // 2, CAP,...  1.48 us
  transfers between devices with their start and end apart: 16, of which 4 were waited for; matrix products, arithmetic and copies ran while one was open for 0% of the time, Pallas kernels for 17%

profile of v5, /device:TPU:1, one launch (start us, length us, event | category | flops | bytes accessed | tf_op | source)
XLA Modules:
  0.0 41.0 jit_solution(5575590602835457463)
XLA Ops:
  0.0 1.5 %pack_give.2 = (bf16[1,2,64,384]{3,2,1,0:T(8,128)(2,1)S(1)}, s32[1,384]{1,0:T(1,128)S(1)}, s32[1,128]{1,0:T(1,128)S(1)}) custom-call(s32[384]{0:T(512)} %labels_ref.3, bf16[4,384,384]{2,1,0:T(8,128)(2,1)} %bitcast.15), custom_call_target="tpu_custom_call" | custom-call | tf_op jit(solution)/shard_map/pack_give/pallas_call | solution.py:132
  1.5 3.3 %collective-permute-start.21 = (bf16[1,2,64,384]{3,2,1,0:T(8,128)(2,1)S(1)}, bf16[1,2,64,384]{3,2,1,0:T(8,128)(2,1)S(1)}, u32[]{:S(2)}, u32[]{:S(2)}) collective-permute-start(bf16[1,2,64,384]{3,2,1,0:T(8,128)(2,1)S(1)} %get-tuple-element.101), channel_id=1, source_target_pairs={{0,8},{8,0},{16,24},{24,16},{32,40},{40,32},{48,56},{56,48},{64,72... | collective-permute-start | bytes 294920 | tf_op jit(solution)/shard_map/ppermute | solution.py:590
  4.8 1.5 %pack_keep.2 = (bf16[1,8,48,128]{3,2,1,0:T(8,128)(2,1)S(1)}, bf16[1,2,64,384]{3,2,1,0:T(8,128)(2,1)S(1)}) custom-call(s32[1,384]{1,0:T(1,128)S(1)} %get-tuple-element.94.pos_ref, bf16[16,48,384]{2,1,0:T(8,128)(2,1)} %bitcast.9.t_ref, bf16[4,384,384]{2,1,0:T(8,128)(2,1)S(1)} %bitcast.16), custom_call_target="tpu_custom_call" | custom-call | bytes 4194304 | tf_op jit(solution)/shard_map/pack_keep/pallas_call | solution.py:155
  6.4 0.1 collective-permute-start.23
  6.5 4.6 %collective-permute-start.22 = (bf16[2,2,64,384]{3,2,1,0:T(8,128)(2,1)S(1)}, bf16[2,2,64,384]{3,2,1,0:T(8,128)(2,1)S(1)}, u32[]{:S(2)}, u32[]{:S(2)}) collective-permute-start(bf16[2,2,64,384]{3,2,1,0:T(8,128)(2,1)S(1)} %join_w.2.refs_0_), channel_id=1, source_target_pairs={{0,7},{1,2},{2,1},{3,4},{4,3},{5,6},{6,5},{7,0},{8,15},{9,10},{10,... | collective-permute-start | bytes 589832 | tf_op jit(solution)/shard_map/ppermute | solution.py:225
  11.0 2.7 %collective-permute-start.18 = (bf16[1,8,48,128]{3,2,1,0:T(8,128)(2,1)S(1)}, bf16[1,8,48,128]{3,2,1,0:T(8,128)(2,1)S(1)}, u32[]{:S(2)}, u32[]{:S(2)}) collective-permute-start(bf16[1,8,48,128]{3,2,1,0:T(8,128)(2,1)S(1)} %get-tuple-element.99.refs_0_), channel_id=1, source_target_pairs={{0,192},{8,56},{16,208},{24,40},{32,224},{40,24},{48,240},{56,8},{... | collective-permute-start | bytes 294920 | tf_op jit(solution)/shard_map/ppermute | solution.py:219
  13.8 0.4 collective-permute-start.17
  14.1 0.2 collective-permute-start.16
  14.4 0.0 collective-permute-done.23.refs_2_
  14.4 2.4 %collective-permute-start.24 = (bf16[2,2,64,384]{3,2,1,0:T(8,128)(2,1)S(1)}, bf16[2,2,64,384]{3,2,1,0:T(8,128)(2,1)S(1)}, u32[]{:S(2)}, u32[]{:S(2)}) collective-permute-start(bf16[2,2,64,384]{3,2,1,0:T(8,128)(2,1)S(1)} %collective-permute-done.23.refs_2_), channel_id=1, source_target_pairs={{0,7},{1,2},{2,1},{3,4},{4,3},{5,6},{6,5},{7,0},{8,15},{9,10},{10,... | collective-permute-start | bytes 589832 | tf_op jit(solution)/shard_map/ppermute | solution.py:229
  16.8 0.0 collective-permute-done.18.refs_3_
  16.8 2.0 %collective-permute-done.17.refs_2_ = bf16[1,8,48,128]{3,2,1,0:T(8,128)(2,1)S(1)} collective-permute-done((bf16[1,8,48,128]{3,2,1,0:T(8,128)(2,1)S(1)}, bf16[1,8,48,128]{3,2,1,0:T(8,128)(2,1)S(1)}, u32[]{:S(2)}, u32[]{:S(2)}) %collective-permute-start.17) | collective-permute-done | bytes 98336 | tf_op jit(solution)/shard_map/ppermute | solution.py:219
  18.7 0.0 collective-permute-done.16.refs_1_
  18.8 2.8 %collective-permute-start.20 = (bf16[4,8,48,128]{3,2,1,0:T(8,128)(2,1)S(1)}, bf16[4,8,48,128]{3,2,1,0:T(8,128)(2,1)S(1)}, u32[]{:S(2)}, u32[]{:S(2)}) collective-permute-start(bf16[4,8,48,128]{3,2,1,0:T(8,128)(2,1)S(1)} %join_row.2.refs_0_), channel_id=1, source_target_pairs={{0,32},{8,136},{16,48},{24,152},{32,0},{40,168},{48,16},{56,184},{... | collective-permute-start | bytes 1179656 | tf_op jit(solution)/shard_map/ppermute | solution.py:219
  21.6 0.3 collective-permute-start.19
  21.9 0.6 %collective-permute-start.28 = (bf16[4,8,48,128]{3,2,1,0:T(8,128)(2,1)S(1)}, bf16[4,8,48,128]{3,2,1,0:T(8,128)(2,1)S(1)}, u32[]{:S(2)}, u32[]{:S(2)}) collective-permute-start(bf16[4,8,48,128]{3,2,1,0:T(8,128)(2,1)S(1)} %join_row.2.refs_0_), channel_id=1, source_target_pairs={{0,48},{8,200},{16,32},{24,216},{32,16},{40,232},{48,0},{56,248},{... | collective-permute-start | bytes 1179656 | tf_op jit(solution)/shard_map/ppermute | solution.py:219
  22.5 0.0 collective-permute-done.24.refs_3_
  22.5 1.5 %collective-permute-start.26 = (bf16[2,2,64,384]{3,2,1,0:T(8,128)(2,1)S(1)}, bf16[2,2,64,384]{3,2,1,0:T(8,128)(2,1)S(1)}, u32[]{:S(2)}, u32[]{:S(2)}) collective-permute-start(bf16[2,2,64,384]{3,2,1,0:T(8,128)(2,1)S(1)} %collective-permute-done.25.refs_4_), channel_id=1, source_target_pairs={{0,7},{1,2},{2,1},{3,4},{4,3},{5,6},{6,5},{7,0},{8,15},{9,10},{10,... | collective-permute-start | bytes 589832 | tf_op jit(solution)/shard_map/ppermute | solution.py:231
  24.0 1.0 %prepare.1 = (s32[48,384]{1,0:T(8,128)S(1)}, s32[16,48,128]{2,1,0:T(8,128)S(1)}, s32[16,48,128]{2,1,0:T(8,128)S(1)}, bf16[512,384]{1,0:T(8,128)(2,1)S(1)}, bf16[128,384]{1,0:T(8,128)(2,1)S(1)}) custom-call(s32[32]{0:T(128)S(1)} %copy-done.10, s32[384]{0:T(512)S(1)} %copy-done.9, s32[1,384]{1,0:T(1,128)S(1)} %get-tuple-element.94.pos_ref), custom_call_target="tpu_custom_call" | custom-call | tf_op jit(solution)/shard_map/prepare/pallas_call | solution.py:177
  25.0 0.9 %spread.2 = (bf16[10,64,512]{2,1,0:T(8,128)(2,1)S(1)}, bf16[10,64,512]{2,1,0:T(8,128)(2,1)S(1)}) custom-call(bf16[512,384]{1,0:T(8,128)(2,1)S(1)} %get-tuple-element.98.spread_ref, bf16[2,2,64,384]{3,2,1,0:T(8,128)(2,1)S(1)} %join_w.2.refs_0_, bf16[2,2,64,384]{3,2,1,0:T(8,128)(2,1)S(1)} %collective-permute-done.22.refs_1_, ...), custom_call_target="tpu_custom_call" | custom-call | flops 503316480 | bytes 4194304 | tf_op jit(solution)/shard_map/spread/pallas_call | solution.py:364
  25.9 1.4 %collective-permute-done.27.refs_1_ = bf16[2,2,64,384]{3,2,1,0:T(8,128)(2,1)S(1)} collective-permute-done((bf16[2,2,64,384]{3,2,1,0:T(8,128)(2,1)S(1)}, bf16[2,2,64,384]{3,2,1,0:T(8,128)(2,1)S(1)}, u32[]{:S(2)}, u32[]{:S(2)}) %collective-permute-start.27) | collective-permute-done | bytes 196640 | tf_op jit(solution)/shard_map/ppermute | solution.py:232
  27.3 1.1 %collective-permute-start.29 = (bf16[1,2,64,384]{3,2,1,0:T(8,128)(2,1)S(1)}, bf16[1,2,64,384]{3,2,1,0:T(8,128)(2,1)S(1)}, u32[]{:S(2)}, u32[]{:S(2)}) collective-permute-start(bf16[1,2,64,384]{3,2,1,0:T(8,128)(2,1)S(1)} %slice.22), channel_id=1, source_target_pairs={{0,7},{1,2},{2,1},{3,4},{4,3},{5,6},{6,5},{7,0},{8,15},{9,10},{10,... | collective-permute-start | bytes 294920 | tf_op jit(solution)/shard_map/ppermute | solution.py:234
  28.4 0.2 collective-permute-done.26.refs_0_
  28.6 0.4 %collective-permute-start.30 = (bf16[1,2,64,384]{3,2,1,0:T(8,128)(2,1)S(1)}, bf16[1,2,64,384]{3,2,1,0:T(8,128)(2,1)S(1)}, u32[]{:S(2)}, u32[]{:S(2)}) collective-permute-start(bf16[1,2,64,384]{3,2,1,0:T(8,128)(2,1)S(1)} %slice.19), channel_id=1, source_target_pairs={{0,1},{1,0},{2,3},{3,2},{4,5},{5,4},{6,7},{7,6},{8,9},{9,8},{10,11... | collective-permute-start | bytes 294920 | tf_op jit(solution)/shard_map/ppermute | solution.py:235
  29.1 0.5 %spread.3 = (bf16[4,64,512]{2,1,0:T(8,128)(2,1)S(1)}, bf16[4,64,512]{2,1,0:T(8,128)(2,1)S(1)}) custom-call(bf16[512,384]{1,0:T(8,128)(2,1)S(1)} %get-tuple-element.98.spread_ref, bf16[2,2,64,384]{3,2,1,0:T(8,128)(2,1)S(1)} %collective-permute-done.26.refs_0_, bf16[2,2,64,384]{3,2,1,0:T(8,128)(2,1)S(1)} %collective-permute-done.27.refs_1_), custom_call_target="tpu_custom_call" | custom-call | flops 201326592 | bytes 4194304 | tf_op jit(solution)/shard_map/spread/pallas_call | solution.py:364
  29.6 2.1 %collective-permute-done.19.refs_1_ = bf16[4,8,48,128]{3,2,1,0:T(8,128)(2,1)S(1)} collective-permute-done((bf16[4,8,48,128]{3,2,1,0:T(8,128)(2,1)S(1)}, bf16[4,8,48,128]{3,2,1,0:T(8,128)(2,1)S(1)}, u32[]{:S(2)}, u32[]{:S(2)}) %collective-permute-start.19) | collective-permute-done | bytes 393248 | tf_op jit(solution)/shard_map/ppermute | solution.py:219
  31.6 1.0 %early_sums.1 = (f32[2,384,512]{2,1,0:T(8,128)S(1)}, bf16[2,384,768]{2,1,0:T(8,128)(2,1)S(1)}) custom-call(bf16[4,8,48,128]{3,2,1,0:T(8,128)(2,1)S(1)} %join_row.2.refs_0_, bf16[4,8,48,128]{3,2,1,0:T(8,128)(2,1)S(1)} %collective-permute-done.19.refs_1_, bf16[4,8,48,128]{3,2,1,0:T(8,128)(2,1)S(1)} %collective-permute-done.20.refs_2_, ...), custom_call_target="tpu_custom_call" | custom-call | flops 603979776 | bytes 6291456 | tf_op jit(solution)/shard_map/early_sums/pallas_call | solution.py:428
  32.6 0.5 %other_pair.1 = (f32[16,48,128]{2,1,0:T(8,128)S(1)}, bf16[2,384,256]{2,1,0:T(8,128)(2,1)S(1)}, bf16[2,384,128]{2,1,0:T(8,128)(2,1)S(1)}) custom-call(s32[16,48,128]{2,1,0:T(8,128)S(1)} %get-tuple-element.108.pick_ref, bf16[4,8,48,128]{3,2,1,0:T(8,128)(2,1)S(1)} %join_row.2.refs_0_, bf16[4,8,48,128]{3,2,1,0:T(8,128)(2,1)S(1)} %collective-permute-done.19.refs_1_, ...), custom_call_target="tpu_custom_call" | custom-call | flops 201326592 | bytes 6291456 | tf_op jit(solution)/shard_map/other_pair/pallas_call | solution.py:485
  33.2 0.6 %far_pair.1 = f32[16,48,128]{2,1,0:T(8,128)S(1)} custom-call(s32[16,48,128]{2,1,0:T(8,128)S(1)} %get-tuple-element.108.pick_ref, bf16[512,384]{1,0:T(8,128)(2,1)S(1)} %get-tuple-element.98.spread_ref, f32[16,48,128]{2,1,0:T(8,128)S(1)} %get-tuple-element.116.sums_ref, bf16[2,384,128]{2,1,0:T(8,128)(2,1)S(1)} %get-tuple-element.113.rest_ref, ...), custom_call_target="tpu_custom_call" | custom-call | tf_op jit(solution)/shard_map/far_pair/pallas_call | solution.py:522
  33.8 3.8 %collective-permute-start.31 = (f32[16,48,128]{2,1,0:T(8,128)S(1)}, f32[16,48,128]{2,1,0:T(8,128)S(1)}, u32[]{:S(2)}, u32[]{:S(2)}) collective-permute-start(f32[16,48,128]{2,1,0:T(8,128)S(1)} %far_pair.1), channel_id=1, source_target_pairs={{0,8},{8,0},{16,24},{24,16},{32,40},{40,32},{48,56},{56,48},{64,72... | collective-permute-start | bytes 1179656 | tf_op jit(solution)/shard_map/ppermute | solution.py:602
  37.6 1.4 %own_pair.1.own_ref = f32[16,48,128]{2,1,0:T(8,128)S(1)} custom-call(s32[16,48,128]{2,1,0:T(8,128)S(1)} %get-tuple-element.97.pick_ref, bf16[512,384]{1,0:T(8,128)(2,1)S(1)} %get-tuple-element.98.spread_ref, bf16[2,384,768]{2,1,0:T(8,128)(2,1)S(1)} %get-tuple-element.107.t_cat, bf16[2,384,256]{2,1,0:T(8,128)(2,1)S(1)} %get-tuple-element.110.late_ref, ...), custom_call_target="tpu_custom_call" | custom-call | flops 905969664 | bytes 4194304 | tf_op jit(solution)/shard_map/own_pair/pallas_call | solution.py:556
  39.0 1.1 %last_part.1 = (bf16[16,48,384]{2,1,0:T(8,128)(2,1)}, s32[1]{0:T(128)}) custom-call(s32[1,128]{1,0:T(1,128)S(1)} %get-tuple-element.93.width_ref, s32[48,384]{1,0:T(8,128)S(1)} %get-tuple-element.95.bits_ref, bf16[128,384]{1,0:T(8,128)(2,1)S(1)} %get-tuple-element.96.expand_ref, f32[16,48,128]{2,1,0:T(8,128)S(1)} %own_pair.1.own_ref, ...), custom_call_target="tpu_custom_call" | custom-call | tf_op jit(solution)/shard_map/last_part/pallas_call | solution.py:604
  (21 shorter events, 0.1 us)
Async XLA Ops:
  0.0 4.8 %copy-start.6 = (bf16[4,384,1,384]{3,1,2,0:T(8,128)(2,1)S(1)}, bf16[4,384,1,384]{3,1,2,0:T(8,128)(2,1)}, u32[]{:S(2)}) copy-start(bf16[4,384,1,384]{3,1,2,0:T(8,128)(2,1)} %param.9) | copy-start | bytes 3538948
  1.5 4.9 %collective-permute-start.21 = (bf16[1,2,64,384]{3,2,1,0:T(8,128)(2,1)S(1)}, bf16[1,2,64,384]{3,2,1,0:T(8,128)(2,1)S(1)}, u32[]{:S(2)}, u32[]{:S(2)}) collective-permute-start(bf16[1,2,64,384]{3,2,1,0:T(8,128)(2,1)S(1)} %get-tuple-element.101), channel_id=1, source_target_pairs={{0,8},{8,0},{16,24},{24,16},{32,40},{40,32},{48,56},{56,48},{64,72... | collective-permute-start | bytes 294920 | tf_op jit(solution)/shard_map/ppermute | solution.py:590
  4.8 19.1 %copy-start.9 = (s32[384]{0:T(512)S(1)}, s32[384]{0:T(512)}, u32[]{:S(2)}) copy-start(s32[384]{0:T(512)} %labels_ref.3) | copy-start | bytes 4612
  4.8 19.1 %copy-start.10 = (s32[32]{0:T(128)S(1)}, s32[32]{0:T(128)}, u32[]{:S(2)}) copy-start(s32[32]{0:T(128)} %occ_ref.1) | copy-start | bytes 388
  6.4 8.0 %collective-permute-start.23 = (bf16[2,2,64,384]{3,2,1,0:T(8,128)(2,1)S(1)}, bf16[2,2,64,384]{3,2,1,0:T(8,128)(2,1)S(1)}, u32[]{:S(2)}, u32[]{:S(2)}) collective-permute-start(bf16[2,2,64,384]{3,2,1,0:T(8,128)(2,1)S(1)} %join_w.2.refs_0_), channel_id=1, source_target_pairs={{0,1},{1,0},{2,3},{3,2},{4,5},{5,4},{6,7},{7,6},{8,9},{9,8},{10,11... | collective-permute-start | bytes 589832 | tf_op jit(solution)/shard_map/ppermute | solution.py:226
  6.5 10.3 %collective-permute-start.22 = (bf16[2,2,64,384]{3,2,1,0:T(8,128)(2,1)S(1)}, bf16[2,2,64,384]{3,2,1,0:T(8,128)(2,1)S(1)}, u32[]{:S(2)}, u32[]{:S(2)}) collective-permute-start(bf16[2,2,64,384]{3,2,1,0:T(8,128)(2,1)S(1)} %join_w.2.refs_0_), channel_id=1, source_target_pairs={{0,7},{1,2},{2,1},{3,4},{4,3},{5,6},{6,5},{7,0},{8,15},{9,10},{10,... | collective-permute-start | bytes 589832 | tf_op jit(solution)/shard_map/ppermute | solution.py:225
  11.0 5.7 %collective-permute-start.18 = (bf16[1,8,48,128]{3,2,1,0:T(8,128)(2,1)S(1)}, bf16[1,8,48,128]{3,2,1,0:T(8,128)(2,1)S(1)}, u32[]{:S(2)}, u32[]{:S(2)}) collective-permute-start(bf16[1,8,48,128]{3,2,1,0:T(8,128)(2,1)S(1)} %get-tuple-element.99.refs_0_), channel_id=1, source_target_pairs={{0,192},{8,56},{16,208},{24,40},{32,224},{40,24},{48,240},{56,8},{... | collective-permute-start | bytes 294920 | tf_op jit(solution)/shard_map/ppermute | solution.py:219
  13.8 5.0 %collective-permute-start.17 = (bf16[1,8,48,128]{3,2,1,0:T(8,128)(2,1)S(1)}, bf16[1,8,48,128]{3,2,1,0:T(8,128)(2,1)S(1)}, u32[]{:S(2)}, u32[]{:S(2)}) collective-permute-start(bf16[1,8,48,128]{3,2,1,0:T(8,128)(2,1)S(1)} %get-tuple-element.99.refs_0_), channel_id=1, source_target_pairs={{0,128},{8,40},{16,144},{24,56},{32,160},{40,8},{48,176},{56,24},{... | collective-permute-start | bytes 294920 | tf_op jit(solution)/shard_map/ppermute | solution.py:219
  14.1 4.6 %collective-permute-start.16 = (bf16[1,8,48,128]{3,2,1,0:T(8,128)(2,1)S(1)}, bf16[1,8,48,128]{3,2,1,0:T(8,128)(2,1)S(1)}, u32[]{:S(2)}, u32[]{:S(2)}) collective-permute-start(bf16[1,8,48,128]{3,2,1,0:T(8,128)(2,1)S(1)} %get-tuple-element.99.refs_0_), channel_id=1, source_target_pairs={{0,64},{8,24},{16,80},{24,8},{32,96},{40,56},{48,112},{56,40},{64,... | collective-permute-start | bytes 294920 | tf_op jit(solution)/shard_map/ppermute | solution.py:219
  14.4 8.1 %collective-permute-start.24 = (bf16[2,2,64,384]{3,2,1,0:T(8,128)(2,1)S(1)}, bf16[2,2,64,384]{3,2,1,0:T(8,128)(2,1)S(1)}, u32[]{:S(2)}, u32[]{:S(2)}) collective-permute-start(bf16[2,2,64,384]{3,2,1,0:T(8,128)(2,1)S(1)} %collective-permute-done.23.refs_2_), channel_id=1, source_target_pairs={{0,7},{1,2},{2,1},{3,4},{4,3},{5,6},{6,5},{7,0},{8,15},{9,10},{10,... | collective-permute-start | bytes 589832 | tf_op jit(solution)/shard_map/ppermute | solution.py:229
  16.8 5.7 %collective-permute-start.25 = (bf16[2,2,64,384]{3,2,1,0:T(8,128)(2,1)S(1)}, bf16[2,2,64,384]{3,2,1,0:T(8,128)(2,1)S(1)}, u32[]{:S(2)}, u32[]{:S(2)}) collective-permute-start(bf16[2,2,64,384]{3,2,1,0:T(8,128)(2,1)S(1)} %collective-permute-done.22.refs_1_), channel_id=1, source_target_pairs={{0,1},{1,0},{2,3},{3,2},{4,5},{5,4},{6,7},{7,6},{8,9},{9,8},{10,11... | collective-permute-start | bytes 589832 | tf_op jit(solution)/shard_map/ppermute | solution.py:230
  18.8 10.8 %collective-permute-start.20 = (bf16[4,8,48,128]{3,2,1,0:T(8,128)(2,1)S(1)}, bf16[4,8,48,128]{3,2,1,0:T(8,128)(2,1)S(1)}, u32[]{:S(2)}, u32[]{:S(2)}) collective-permute-start(bf16[4,8,48,128]{3,2,1,0:T(8,128)(2,1)S(1)} %join_row.2.refs_0_), channel_id=1, source_target_pairs={{0,32},{8,136},{16,48},{24,152},{32,0},{40,168},{48,16},{56,184},{... | collective-permute-start | bytes 1179656 | tf_op jit(solution)/shard_map/ppermute | solution.py:219
  21.6 10.0 %collective-permute-start.19 = (bf16[4,8,48,128]{3,2,1,0:T(8,128)(2,1)S(1)}, bf16[4,8,48,128]{3,2,1,0:T(8,128)(2,1)S(1)}, u32[]{:S(2)}, u32[]{:S(2)}) collective-permute-start(bf16[4,8,48,128]{3,2,1,0:T(8,128)(2,1)S(1)} %join_row.2.refs_0_), channel_id=1, source_target_pairs={{0,16},{8,72},{16,0},{24,88},{32,48},{40,104},{48,32},{56,120},{64... | collective-permute-start | bytes 1179656 | tf_op jit(solution)/shard_map/ppermute | solution.py:219
  21.9 10.7 %collective-permute-start.28 = (bf16[4,8,48,128]{3,2,1,0:T(8,128)(2,1)S(1)}, bf16[4,8,48,128]{3,2,1,0:T(8,128)(2,1)S(1)}, u32[]{:S(2)}, u32[]{:S(2)}) collective-permute-start(bf16[4,8,48,128]{3,2,1,0:T(8,128)(2,1)S(1)} %join_row.2.refs_0_), channel_id=1, source_target_pairs={{0,48},{8,200},{16,32},{24,216},{32,16},{40,232},{48,0},{56,248},{... | collective-permute-start | bytes 1179656 | tf_op jit(solution)/shard_map/ppermute | solution.py:219
  22.5 4.8 %collective-permute-start.27 = (bf16[2,2,64,384]{3,2,1,0:T(8,128)(2,1)S(1)}, bf16[2,2,64,384]{3,2,1,0:T(8,128)(2,1)S(1)}, u32[]{:S(2)}, u32[]{:S(2)}) collective-permute-start(bf16[2,2,64,384]{3,2,1,0:T(8,128)(2,1)S(1)} %collective-permute-done.24.refs_3_), channel_id=1, source_target_pairs={{0,1},{1,0},{2,3},{3,2},{4,5},{5,4},{6,7},{7,6},{8,9},{9,8},{10,11... | collective-permute-start | bytes 589832 | tf_op jit(solution)/shard_map/ppermute | solution.py:232
  22.5 6.1 %collective-permute-start.26 = (bf16[2,2,64,384]{3,2,1,0:T(8,128)(2,1)S(1)}, bf16[2,2,64,384]{3,2,1,0:T(8,128)(2,1)S(1)}, u32[]{:S(2)}, u32[]{:S(2)}) collective-permute-start(bf16[2,2,64,384]{3,2,1,0:T(8,128)(2,1)S(1)} %collective-permute-done.25.refs_4_), channel_id=1, source_target_pairs={{0,7},{1,2},{2,1},{3,4},{4,3},{5,6},{6,5},{7,0},{8,15},{9,10},{10,... | collective-permute-start | bytes 589832 | tf_op jit(solution)/shard_map/ppermute | solution.py:231
  27.3 5.8 %collective-permute-start.29 = (bf16[1,2,64,384]{3,2,1,0:T(8,128)(2,1)S(1)}, bf16[1,2,64,384]{3,2,1,0:T(8,128)(2,1)S(1)}, u32[]{:S(2)}, u32[]{:S(2)}) collective-permute-start(bf16[1,2,64,384]{3,2,1,0:T(8,128)(2,1)S(1)} %slice.22), channel_id=1, source_target_pairs={{0,7},{1,2},{2,1},{3,4},{4,3},{5,6},{6,5},{7,0},{8,15},{9,10},{10,... | collective-permute-start | bytes 294920 | tf_op jit(solution)/shard_map/ppermute | solution.py:234
  28.6 4.5 %collective-permute-start.30 = (bf16[1,2,64,384]{3,2,1,0:T(8,128)(2,1)S(1)}, bf16[1,2,64,384]{3,2,1,0:T(8,128)(2,1)S(1)}, u32[]{:S(2)}, u32[]{:S(2)}) collective-permute-start(bf16[1,2,64,384]{3,2,1,0:T(8,128)(2,1)S(1)} %slice.19), channel_id=1, source_target_pairs={{0,1},{1,0},{2,3},{3,2},{4,5},{5,4},{6,7},{7,6},{8,9},{9,8},{10,11... | collective-permute-start | bytes 294920 | tf_op jit(solution)/shard_map/ppermute | solution.py:235
  33.8 5.2 %collective-permute-start.31 = (f32[16,48,128]{2,1,0:T(8,128)S(1)}, f32[16,48,128]{2,1,0:T(8,128)S(1)}, u32[]{:S(2)}, u32[]{:S(2)}) collective-permute-start(f32[16,48,128]{2,1,0:T(8,128)S(1)} %far_pair.1), channel_id=1, source_target_pairs={{0,8},{8,0},{16,24},{24,16},{32,40},{40,32},{48,56},{56,48},{64,72... | collective-permute-start | bytes 1179656 | tf_op jit(solution)/shard_map/ppermute | solution.py:602

commit v6 on v5

--- a/solution.py
+++ b/solution.py
@@ -92,7 +92,9 @@
     row_ref[0] = both.astype(BF).reshape(half, na, 2 * CAP)
 
 
-def prepare_kernel(occ_ref, labels_ref, pos_ref, bits_ref, pick_own_ref, pick_other_ref, spread_ref, expand_ref):
+def prepare_kernel(
+    occ_ref, labels_ref, pos_ref, bits_ref, pick_own_ref, pick_other_ref, half_ref, spread_ref, expand_ref
+):
     na, v = bits_ref.shape
     labels = labels_ref[...].reshape(1, v)
     pos = pos_ref[...]
@@ -109,6 +111,10 @@
     for i in range(IW):
         for ref, j in ((pick_own_ref, tr), (pick_other_ref, jnp.bitwise_xor(tr, 1))):
             ref[i] = jnp.right_shift(jnp.bitwise_xor(rows_a, jnp.bitwise_xor(occ_ref[i], occ_ref[j])), 1)
+    upper = lax.broadcasted_iota(jnp.int32, rows_a.shape, 1) // CAP
+    for i in range(IW):
+        irrep = jnp.bitwise_xor(rows_a, jnp.bitwise_xor(occ_ref[i], occ_ref[tr]))
+        half_ref[i] = (jnp.bitwise_and(irrep, 1) == upper).astype(jnp.int32)
     wide = lax.broadcasted_iota(jnp.int32, spread_ref.shape, 0) == labels * CAP + pos
     spread_ref[...] = wide.astype(F32).astype(BF)
     pair = lax.broadcasted_iota(jnp.int32, expand_ref.shape, 0) == jnp.bitwise_and(labels, 1) * CAP + pos
@@ -180,11 +186,12 @@
             jax.ShapeDtypeStruct((na, v), jnp.int32),
             pick,
             pick,
+            pick,
             jax.ShapeDtypeStruct((8 * CAP, v), BF),
             jax.ShapeDtypeStruct((2 * CAP, v), BF),
         ),
         in_specs=[SMEM, VMEM, VMEM],
-        out_specs=(VMEM,) * 5,
+        out_specs=(VMEM,) * 6,
         compiler_params=pltpu.CompilerParams(vmem_limit_bytes=8 * 2**20),
         name="prepare",
     )(occupied, labels, pos)
@@ -565,10 +572,11 @@
     )(pick, spread, t_cat, late, *d, rest, far)
 
 
-def last_kernel(width_ref, bits_ref, expand_ref, own_ref, got_ref, out_ref, fits_ref):
+def last_kernel(width_ref, bits_ref, half_ref, expand_ref, own_ref, got_ref, out_ref, fits_ref):
     fits_ref[0] = (width_ref[0, 0] <= CAP).astype(jnp.int32)
     ni, na, lanes = own_ref.shape
-    sums = (own_ref[...] + got_ref[...]).astype(BF).reshape(ni * na, lanes)
+    sums = jnp.where(half_ref[...] != 0, own_ref[...] + got_ref[...], 0.0)
+    sums = sums.astype(BF).reshape(ni * na, lanes)
     wide = jnp.dot(sums, expand_ref[...], preferred_element_type=F32)
     for i in range(ni):
         keep = jnp.bitwise_and(bits_ref[...], 1 << i) != 0
@@ -592,7 +600,7 @@
         return keep, got, row, pos, width
 
     keep, got, row, pos, width = pack(None)
-    bits, pick_own, pick_other, spread, expand = prepare(occupied_irreps, virtual_irreps, pos, na)
+    bits, pick_own, pick_other, half, spread, expand = prepare(occupied_irreps, virtual_irreps, pos, na)
     t_parts, d_parts, a4, b4, d_two = gather(keep, got, row, functools.partial(spread_blocks, spread))
     d_three = spread_blocks(spread, d_parts[5:])
     d_own, d_other = zip(d_two, d_three)
@@ -604,11 +612,11 @@
     fast, fits = pl.pallas_call(
         last_kernel,
         out_shape=(jax.ShapeDtypeStruct((ni, na, v), BF), jax.ShapeDtypeStruct((1,), jnp.int32)),
-        in_specs=[VMEM] * 5,
+        in_specs=[VMEM] * 6,
         out_specs=(VMEM, SMEM),
         compiler_params=pltpu.CompilerParams(vmem_limit_bytes=8 * 2**20),
         name="last_part",
-    )(width, bits, expand, own, got)
+    )(width, bits, half, expand, own, got)
 
     def all_windows():
         def window(n, before):

time: 41.1 us -> 41.1 us (level)
  no operation moved by 1% of the time
where the time goes in v6:
time: 41.1 us; the launch traced here: 41 us
  starting transfers between devices  24.2 us (59%)
  Pallas kernels  10.1 us (25%)
  waiting for transfers between devices  5.63 us (14%)
  between operations  1.01 us (2%)
    ppermute x6, starting transfers between devices, lines(): return [lax.ppermute(piece, 'tr', line(first, flip)) for flip in (1, 2, 3)]  7.01 us
    ppermute x1, starting transfers between devices, gather(): a1 = lax.ppermute(d, 'su', ODD_LINKS)  4.56 us
    ppermute x6, waiting for transfers between devices, lines(): return [lax.ppermute(piece, 'tr', line(first, flip)) for flip in (1, 2, 3)]  4.07 us
    ppermute x1, starting transfers between devices, body(): lax.ppermute(far_pair(pick_other, spread, other, rest, b4), 'tr', SWAP)  3.83 us
    ppermute x1, starting transfers between devices, pack(): got = lax.ppermute(give, 'tr', SWAP)  3.33 us
    ppermute x1, starting transfers between devices, gather(): a2 = lax.ppermute(b1, 'su', ODD_LINKS)  2.4 us
    pallas_call x1, Pallas kernels, pack_keep(): pl.pallas_call(kernel, out_shape=(jax.ShapeDtypeStruct((1, ni // 2, na, 2...  1.51 us
    pallas_call x1, Pallas kernels, pack_give(): pl.pallas_call(kernel, out_shape=(jax.ShapeDtypeStruct((1, nk // 2, CAP,...  1.48 us
  transfers between devices with their start and end apart: 16, of which 4 were waited for; matrix products, arithmetic and copies ran while one was open for 0% of the time, Pallas kernels for 17%

profile of v6, /device:TPU:1, one launch (start us, length us, event | category | flops | bytes accessed | tf_op | source)
XLA Modules:
  0.0 41.0 jit_solution(10816014477176857904)
XLA Ops:
  0.0 1.5 %pack_give.2 = (bf16[1,2,64,384]{3,2,1,0:T(8,128)(2,1)S(1)}, s32[1,384]{1,0:T(1,128)S(1)}, s32[1,128]{1,0:T(1,128)S(1)}) custom-call(s32[384]{0:T(512)} %labels_ref.3, bf16[4,384,384]{2,1,0:T(8,128)(2,1)} %bitcast.15), custom_call_target="tpu_custom_call" | custom-call | tf_op jit(solution)/shard_map/pack_give/pallas_call | solution.py:138
  1.5 3.3 %collective-permute-start.21 = (bf16[1,2,64,384]{3,2,1,0:T(8,128)(2,1)S(1)}, bf16[1,2,64,384]{3,2,1,0:T(8,128)(2,1)S(1)}, u32[]{:S(2)}, u32[]{:S(2)}) collective-permute-start(bf16[1,2,64,384]{3,2,1,0:T(8,128)(2,1)S(1)} %get-tuple-element.103), channel_id=1, source_target_pairs={{0,8},{8,0},{16,24},{24,16},{32,40},{40,32},{48,56},{56,48},{64,72... | collective-permute-start | bytes 294920 | tf_op jit(solution)/shard_map/ppermute | solution.py:598
  4.8 1.5 %pack_keep.2 = (bf16[1,8,48,128]{3,2,1,0:T(8,128)(2,1)S(1)}, bf16[1,2,64,384]{3,2,1,0:T(8,128)(2,1)S(1)}) custom-call(s32[1,384]{1,0:T(1,128)S(1)} %get-tuple-element.95.pos_ref, bf16[16,48,384]{2,1,0:T(8,128)(2,1)} %bitcast.9.t_ref, bf16[4,384,384]{2,1,0:T(8,128)(2,1)S(1)} %bitcast.16), custom_call_target="tpu_custom_call" | custom-call | bytes 4194304 | tf_op jit(solution)/shard_map/pack_keep/pallas_call | solution.py:161
  6.3 0.0 collective-permute-done.21.refs_1_
  6.4 0.1 collective-permute-start.23
  6.5 4.6 %collective-permute-start.22 = (bf16[2,2,64,384]{3,2,1,0:T(8,128)(2,1)S(1)}, bf16[2,2,64,384]{3,2,1,0:T(8,128)(2,1)S(1)}, u32[]{:S(2)}, u32[]{:S(2)}) collective-permute-start(bf16[2,2,64,384]{3,2,1,0:T(8,128)(2,1)S(1)} %join_w.2.refs_0_), channel_id=1, source_target_pairs={{0,7},{1,2},{2,1},{3,4},{4,3},{5,6},{6,5},{7,0},{8,15},{9,10},{10,... | collective-permute-start | bytes 589832 | tf_op jit(solution)/shard_map/ppermute | solution.py:232
  11.0 2.7 %collective-permute-start.18 = (bf16[1,8,48,128]{3,2,1,0:T(8,128)(2,1)S(1)}, bf16[1,8,48,128]{3,2,1,0:T(8,128)(2,1)S(1)}, u32[]{:S(2)}, u32[]{:S(2)}) collective-permute-start(bf16[1,8,48,128]{3,2,1,0:T(8,128)(2,1)S(1)} %get-tuple-element.101.refs_0_), channel_id=1, source_target_pairs={{0,192},{8,56},{16,208},{24,40},{32,224},{40,24},{48,240},{56,8},{... | collective-permute-start | bytes 294920 | tf_op jit(solution)/shard_map/ppermute | solution.py:226
  13.8 0.4 collective-permute-start.17
  14.1 0.2 collective-permute-start.16
  14.4 0.0 collective-permute-done.23.refs_2_
  14.4 2.4 %collective-permute-start.24 = (bf16[2,2,64,384]{3,2,1,0:T(8,128)(2,1)S(1)}, bf16[2,2,64,384]{3,2,1,0:T(8,128)(2,1)S(1)}, u32[]{:S(2)}, u32[]{:S(2)}) collective-permute-start(bf16[2,2,64,384]{3,2,1,0:T(8,128)(2,1)S(1)} %collective-permute-done.23.refs_2_), channel_id=1, source_target_pairs={{0,7},{1,2},{2,1},{3,4},{4,3},{5,6},{6,5},{7,0},{8,15},{9,10},{10,... | collective-permute-start | bytes 589832 | tf_op jit(solution)/shard_map/ppermute | solution.py:236
  16.8 0.0 collective-permute-done.22.refs_1_
  16.8 0.0 collective-permute-start.25
  16.8 2.0 %collective-permute-done.17.refs_2_ = bf16[1,8,48,128]{3,2,1,0:T(8,128)(2,1)S(1)} collective-permute-done((bf16[1,8,48,128]{3,2,1,0:T(8,128)(2,1)S(1)}, bf16[1,8,48,128]{3,2,1,0:T(8,128)(2,1)S(1)}, u32[]{:S(2)}, u32[]{:S(2)}) %collective-permute-start.17) | collective-permute-done | bytes 98336 | tf_op jit(solution)/shard_map/ppermute | solution.py:226
  18.8 2.8 %collective-permute-start.20 = (bf16[4,8,48,128]{3,2,1,0:T(8,128)(2,1)S(1)}, bf16[4,8,48,128]{3,2,1,0:T(8,128)(2,1)S(1)}, u32[]{:S(2)}, u32[]{:S(2)}) collective-permute-start(bf16[4,8,48,128]{3,2,1,0:T(8,128)(2,1)S(1)} %join_row.2.refs_0_), channel_id=1, source_target_pairs={{0,32},{8,136},{16,48},{24,152},{32,0},{40,168},{48,16},{56,184},{... | collective-permute-start | bytes 1179656 | tf_op jit(solution)/shard_map/ppermute | solution.py:226
  21.6 0.3 collective-permute-start.19
  21.9 0.6 %collective-permute-start.28 = (bf16[4,8,48,128]{3,2,1,0:T(8,128)(2,1)S(1)}, bf16[4,8,48,128]{3,2,1,0:T(8,128)(2,1)S(1)}, u32[]{:S(2)}, u32[]{:S(2)}) collective-permute-start(bf16[4,8,48,128]{3,2,1,0:T(8,128)(2,1)S(1)} %join_row.2.refs_0_), channel_id=1, source_target_pairs={{0,48},{8,200},{16,32},{24,216},{32,16},{40,232},{48,0},{56,248},{... | collective-permute-start | bytes 1179656 | tf_op jit(solution)/shard_map/ppermute | solution.py:226
  22.5 1.5 %collective-permute-start.26 = (bf16[2,2,64,384]{3,2,1,0:T(8,128)(2,1)S(1)}, bf16[2,2,64,384]{3,2,1,0:T(8,128)(2,1)S(1)}, u32[]{:S(2)}, u32[]{:S(2)}) collective-permute-start(bf16[2,2,64,384]{3,2,1,0:T(8,128)(2,1)S(1)} %collective-permute-done.25.refs_4_), channel_id=1, source_target_pairs={{0,7},{1,2},{2,1},{3,4},{4,3},{5,6},{6,5},{7,0},{8,15},{9,10},{10,... | collective-permute-start | bytes 589832 | tf_op jit(solution)/shard_map/ppermute | solution.py:238
  24.0 1.1 %prepare.1 = (s32[48,384]{1,0:T(8,128)S(1)}, s32[16,48,128]{2,1,0:T(8,128)S(1)}, s32[16,48,128]{2,1,0:T(8,128)S(1)}, s32[16,48,128]{2,1,0:T(8,128)S(1)}, bf16[51...) custom-call(s32[32]{0:T(128)S(1)} %copy-done.10, s32[384]{0:T(512)S(1)} %copy-done.9, ...), custom_call_target="tpu_custom_call" | custom-call | tf_op jit(solution)/shard_map/prepare/pallas_call | solution.py:183
  25.0 0.9 %spread.2 = (bf16[10,64,512]{2,1,0:T(8,128)(2,1)S(1)}, bf16[10,64,512]{2,1,0:T(8,128)(2,1)S(1)}) custom-call(bf16[512,384]{1,0:T(8,128)(2,1)S(1)} %get-tuple-element.100.spread_ref, bf16[2,2,64,384]{3,2,1,0:T(8,128)(2,1)S(1)} %join_w.2.refs_0_, bf16[2,2,64,384]{3,2,1,0:T(8,128)(2,1)S(1)} %collective-permute-done.22.refs_1_, ...), custom_call_target="tpu_custom_call" | custom-call | flops 503316480 | bytes 4194304 | tf_op jit(solution)/shard_map/spread/pallas_call | solution.py:371
  25.9 1.4 %collective-permute-done.27.refs_1_ = bf16[2,2,64,384]{3,2,1,0:T(8,128)(2,1)S(1)} collective-permute-done((bf16[2,2,64,384]{3,2,1,0:T(8,128)(2,1)S(1)}, bf16[2,2,64,384]{3,2,1,0:T(8,128)(2,1)S(1)}, u32[]{:S(2)}, u32[]{:S(2)}) %collective-permute-start.27) | collective-permute-done | bytes 196640 | tf_op jit(solution)/shard_map/ppermute | solution.py:239
  27.3 1.1 %collective-permute-start.29 = (bf16[1,2,64,384]{3,2,1,0:T(8,128)(2,1)S(1)}, bf16[1,2,64,384]{3,2,1,0:T(8,128)(2,1)S(1)}, u32[]{:S(2)}, u32[]{:S(2)}) collective-permute-start(bf16[1,2,64,384]{3,2,1,0:T(8,128)(2,1)S(1)} %slice.22), channel_id=1, source_target_pairs={{0,7},{1,2},{2,1},{3,4},{4,3},{5,6},{6,5},{7,0},{8,15},{9,10},{10,... | collective-permute-start | bytes 294920 | tf_op jit(solution)/shard_map/ppermute | solution.py:241
  28.4 0.2 collective-permute-done.26.refs_0_
  28.6 0.4 %collective-permute-start.30 = (bf16[1,2,64,384]{3,2,1,0:T(8,128)(2,1)S(1)}, bf16[1,2,64,384]{3,2,1,0:T(8,128)(2,1)S(1)}, u32[]{:S(2)}, u32[]{:S(2)}) collective-permute-start(bf16[1,2,64,384]{3,2,1,0:T(8,128)(2,1)S(1)} %slice.19), channel_id=1, source_target_pairs={{0,1},{1,0},{2,3},{3,2},{4,5},{5,4},{6,7},{7,6},{8,9},{9,8},{10,11... | collective-permute-start | bytes 294920 | tf_op jit(solution)/shard_map/ppermute | solution.py:242
  29.1 0.5 %spread.3 = (bf16[4,64,512]{2,1,0:T(8,128)(2,1)S(1)}, bf16[4,64,512]{2,1,0:T(8,128)(2,1)S(1)}) custom-call(bf16[512,384]{1,0:T(8,128)(2,1)S(1)} %get-tuple-element.100.spread_ref, bf16[2,2,64,384]{3,2,1,0:T(8,128)(2,1)S(1)} %collective-permute-done.26.refs_0_, bf16[2,2,64,384]{3,2,1,0:T(8,128)(2,1)S(1)} %collective-permute-done.27.refs_1_), custom_call_target="tpu_custom_call" | custom-call | flops 201326592 | bytes 4194304 | tf_op jit(solution)/shard_map/spread/pallas_call | solution.py:371
  29.6 2.1 %collective-permute-done.19.refs_1_ = bf16[4,8,48,128]{3,2,1,0:T(8,128)(2,1)S(1)} collective-permute-done((bf16[4,8,48,128]{3,2,1,0:T(8,128)(2,1)S(1)}, bf16[4,8,48,128]{3,2,1,0:T(8,128)(2,1)S(1)}, u32[]{:S(2)}, u32[]{:S(2)}) %collective-permute-start.19) | collective-permute-done | bytes 393248 | tf_op jit(solution)/shard_map/ppermute | solution.py:226
  31.6 1.0 %early_sums.1 = (f32[2,384,512]{2,1,0:T(8,128)S(1)}, bf16[2,384,768]{2,1,0:T(8,128)(2,1)S(1)}) custom-call(bf16[4,8,48,128]{3,2,1,0:T(8,128)(2,1)S(1)} %join_row.2.refs_0_, bf16[4,8,48,128]{3,2,1,0:T(8,128)(2,1)S(1)} %collective-permute-done.19.refs_1_, bf16[4,8,48,128]{3,2,1,0:T(8,128)(2,1)S(1)} %collective-permute-done.20.refs_2_, ...), custom_call_target="tpu_custom_call" | custom-call | flops 603979776 | bytes 6291456 | tf_op jit(solution)/shard_map/early_sums/pallas_call | solution.py:435
  32.6 0.5 %other_pair.1 = (f32[16,48,128]{2,1,0:T(8,128)S(1)}, bf16[2,384,256]{2,1,0:T(8,128)(2,1)S(1)}, bf16[2,384,128]{2,1,0:T(8,128)(2,1)S(1)}) custom-call(s32[16,48,128]{2,1,0:T(8,128)S(1)} %get-tuple-element.110.pick_ref, bf16[4,8,48,128]{3,2,1,0:T(8,128)(2,1)S(1)} %join_row.2.refs_0_, bf16[4,8,48,128]{3,2,1,0:T(8,128)(2,1)S(1)} %collective-permute-done.19.refs_1_, ...), custom_call_target="tpu_custom_call" | custom-call | flops 201326592 | bytes 6291456 | tf_op jit(solution)/shard_map/other_pair/pallas_call | solution.py:492
  33.2 0.6 %far_pair.1 = f32[16,48,128]{2,1,0:T(8,128)S(1)} custom-call(s32[16,48,128]{2,1,0:T(8,128)S(1)} %get-tuple-element.110.pick_ref, bf16[512,384]{1,0:T(8,128)(2,1)S(1)} %get-tuple-element.100.spread_ref, f32[16,48,128]{2,1,0:T(8,128)S(1)} %get-tuple-element.118.sums_ref, bf16[2,384,128]{2,1,0:T(8,128)(2,1)S(1)} %get-tuple-element.115.rest_ref, ...), custom_call_target="tpu_custom_call" | custom-call | tf_op jit(solution)/shard_map/far_pair/pallas_call | solution.py:529
  33.8 3.8 %collective-permute-start.31 = (f32[16,48,128]{2,1,0:T(8,128)S(1)}, f32[16,48,128]{2,1,0:T(8,128)S(1)}, u32[]{:S(2)}, u32[]{:S(2)}) collective-permute-start(f32[16,48,128]{2,1,0:T(8,128)S(1)} %far_pair.1), channel_id=1, source_target_pairs={{0,8},{8,0},{16,24},{24,16},{32,40},{40,32},{48,56},{56,48},{64,72... | collective-permute-start | bytes 1179656 | tf_op jit(solution)/shard_map/ppermute | solution.py:610
  37.6 1.4 %own_pair.1.own_ref = f32[16,48,128]{2,1,0:T(8,128)S(1)} custom-call(s32[16,48,128]{2,1,0:T(8,128)S(1)} %get-tuple-element.99.pick_ref, bf16[512,384]{1,0:T(8,128)(2,1)S(1)} %get-tuple-element.100.spread_ref, bf16[2,384,768]{2,1,0:T(8,128)(2,1)S(1)} %get-tuple-element.109.t_cat, bf16[2,384,256]{2,1,0:T(8,128)(2,1)S(1)} %get-tuple-element.112.late_ref, ...), custom_call_target="tpu_custom_call" | custom-call | flops 905969664 | bytes 4194304 | tf_op jit(solution)/shard_map/own_pair/pallas_call | solution.py:563
  39.0 1.1 %last_part.1 = (bf16[16,48,384]{2,1,0:T(8,128)(2,1)}, s32[1]{0:T(128)}) custom-call(s32[1,128]{1,0:T(1,128)S(1)} %get-tuple-element.94.width_ref, s32[48,384]{1,0:T(8,128)S(1)} %get-tuple-element.96.bits_ref, s32[16,48,128]{2,1,0:T(8,128)S(1)} %get-tuple-element.97.half_ref, bf16[128,384]{1,0:T(8,128)(2,1)S(1)} %get-tuple-element.98.expand_ref, ...), custom_call_target="tpu_custom_call" | custom-call | tf_op jit(solution)/shard_map/last_part/pallas_call | solution.py:612
  (21 shorter events, 0.1 us)
Async XLA Ops:
  0.0 4.8 %copy-start.6 = (bf16[4,384,1,384]{3,1,2,0:T(8,128)(2,1)S(1)}, bf16[4,384,1,384]{3,1,2,0:T(8,128)(2,1)}, u32[]{:S(2)}) copy-start(bf16[4,384,1,384]{3,1,2,0:T(8,128)(2,1)} %param.9) | copy-start | bytes 3538948
  1.5 4.9 %collective-permute-start.21 = (bf16[1,2,64,384]{3,2,1,0:T(8,128)(2,1)S(1)}, bf16[1,2,64,384]{3,2,1,0:T(8,128)(2,1)S(1)}, u32[]{:S(2)}, u32[]{:S(2)}) collective-permute-start(bf16[1,2,64,384]{3,2,1,0:T(8,128)(2,1)S(1)} %get-tuple-element.103), channel_id=1, source_target_pairs={{0,8},{8,0},{16,24},{24,16},{32,40},{40,32},{48,56},{56,48},{64,72... | collective-permute-start | bytes 294920 | tf_op jit(solution)/shard_map/ppermute | solution.py:598
  4.8 19.1 %copy-start.9 = (s32[384]{0:T(512)S(1)}, s32[384]{0:T(512)}, u32[]{:S(2)}) copy-start(s32[384]{0:T(512)} %labels_ref.3) | copy-start | bytes 4612
  4.8 19.1 %copy-start.10 = (s32[32]{0:T(128)S(1)}, s32[32]{0:T(128)}, u32[]{:S(2)}) copy-start(s32[32]{0:T(128)} %occ_ref.1) | copy-start | bytes 388
  6.4 8.0 %collective-permute-start.23 = (bf16[2,2,64,384]{3,2,1,0:T(8,128)(2,1)S(1)}, bf16[2,2,64,384]{3,2,1,0:T(8,128)(2,1)S(1)}, u32[]{:S(2)}, u32[]{:S(2)}) collective-permute-start(bf16[2,2,64,384]{3,2,1,0:T(8,128)(2,1)S(1)} %join_w.2.refs_0_), channel_id=1, source_target_pairs={{0,1},{1,0},{2,3},{3,2},{4,5},{5,4},{6,7},{7,6},{8,9},{9,8},{10,11... | collective-permute-start | bytes 589832 | tf_op jit(solution)/shard_map/ppermute | solution.py:233
  6.5 10.3 %collective-permute-start.22 = (bf16[2,2,64,384]{3,2,1,0:T(8,128)(2,1)S(1)}, bf16[2,2,64,384]{3,2,1,0:T(8,128)(2,1)S(1)}, u32[]{:S(2)}, u32[]{:S(2)}) collective-permute-start(bf16[2,2,64,384]{3,2,1,0:T(8,128)(2,1)S(1)} %join_w.2.refs_0_), channel_id=1, source_target_pairs={{0,7},{1,2},{2,1},{3,4},{4,3},{5,6},{6,5},{7,0},{8,15},{9,10},{10,... | collective-permute-start | bytes 589832 | tf_op jit(solution)/shard_map/ppermute | solution.py:232
  11.0 5.7 %collective-permute-start.18 = (bf16[1,8,48,128]{3,2,1,0:T(8,128)(2,1)S(1)}, bf16[1,8,48,128]{3,2,1,0:T(8,128)(2,1)S(1)}, u32[]{:S(2)}, u32[]{:S(2)}) collective-permute-start(bf16[1,8,48,128]{3,2,1,0:T(8,128)(2,1)S(1)} %get-tuple-element.101.refs_0_), channel_id=1, source_target_pairs={{0,192},{8,56},{16,208},{24,40},{32,224},{40,24},{48,240},{56,8},{... | collective-permute-start | bytes 294920 | tf_op jit(solution)/shard_map/ppermute | solution.py:226
  13.8 5.0 %collective-permute-start.17 = (bf16[1,8,48,128]{3,2,1,0:T(8,128)(2,1)S(1)}, bf16[1,8,48,128]{3,2,1,0:T(8,128)(2,1)S(1)}, u32[]{:S(2)}, u32[]{:S(2)}) collective-permute-start(bf16[1,8,48,128]{3,2,1,0:T(8,128)(2,1)S(1)} %get-tuple-element.101.refs_0_), channel_id=1, source_target_pairs={{0,128},{8,40},{16,144},{24,56},{32,160},{40,8},{48,176},{56,24},{... | collective-permute-start | bytes 294920 | tf_op jit(solution)/shard_map/ppermute | solution.py:226
  14.1 4.6 %collective-permute-start.16 = (bf16[1,8,48,128]{3,2,1,0:T(8,128)(2,1)S(1)}, bf16[1,8,48,128]{3,2,1,0:T(8,128)(2,1)S(1)}, u32[]{:S(2)}, u32[]{:S(2)}) collective-permute-start(bf16[1,8,48,128]{3,2,1,0:T(8,128)(2,1)S(1)} %get-tuple-element.101.refs_0_), channel_id=1, source_target_pairs={{0,64},{8,24},{16,80},{24,8},{32,96},{40,56},{48,112},{56,40},{64,... | collective-permute-start | bytes 294920 | tf_op jit(solution)/shard_map/ppermute | solution.py:226
  14.4 8.1 %collective-permute-start.24 = (bf16[2,2,64,384]{3,2,1,0:T(8,128)(2,1)S(1)}, bf16[2,2,64,384]{3,2,1,0:T(8,128)(2,1)S(1)}, u32[]{:S(2)}, u32[]{:S(2)}) collective-permute-start(bf16[2,2,64,384]{3,2,1,0:T(8,128)(2,1)S(1)} %collective-permute-done.23.refs_2_), channel_id=1, source_target_pairs={{0,7},{1,2},{2,1},{3,4},{4,3},{5,6},{6,5},{7,0},{8,15},{9,10},{10,... | collective-permute-start | bytes 589832 | tf_op jit(solution)/shard_map/ppermute | solution.py:236
  16.8 5.7 %collective-permute-start.25 = (bf16[2,2,64,384]{3,2,1,0:T(8,128)(2,1)S(1)}, bf16[2,2,64,384]{3,2,1,0:T(8,128)(2,1)S(1)}, u32[]{:S(2)}, u32[]{:S(2)}) collective-permute-start(bf16[2,2,64,384]{3,2,1,0:T(8,128)(2,1)S(1)} %collective-permute-done.22.refs_1_), channel_id=1, source_target_pairs={{0,1},{1,0},{2,3},{3,2},{4,5},{5,4},{6,7},{7,6},{8,9},{9,8},{10,11... | collective-permute-start | bytes 589832 | tf_op jit(solution)/shard_map/ppermute | solution.py:237
  18.8 10.8 %collective-permute-start.20 = (bf16[4,8,48,128]{3,2,1,0:T(8,128)(2,1)S(1)}, bf16[4,8,48,128]{3,2,1,0:T(8,128)(2,1)S(1)}, u32[]{:S(2)}, u32[]{:S(2)}) collective-permute-start(bf16[4,8,48,128]{3,2,1,0:T(8,128)(2,1)S(1)} %join_row.2.refs_0_), channel_id=1, source_target_pairs={{0,32},{8,136},{16,48},{24,152},{32,0},{40,168},{48,16},{56,184},{... | collective-permute-start | bytes 1179656 | tf_op jit(solution)/shard_map/ppermute | solution.py:226
  21.6 10.0 %collective-permute-start.19 = (bf16[4,8,48,128]{3,2,1,0:T(8,128)(2,1)S(1)}, bf16[4,8,48,128]{3,2,1,0:T(8,128)(2,1)S(1)}, u32[]{:S(2)}, u32[]{:S(2)}) collective-permute-start(bf16[4,8,48,128]{3,2,1,0:T(8,128)(2,1)S(1)} %join_row.2.refs_0_), channel_id=1, source_target_pairs={{0,16},{8,72},{16,0},{24,88},{32,48},{40,104},{48,32},{56,120},{64... | collective-permute-start | bytes 1179656 | tf_op jit(solution)/shard_map/ppermute | solution.py:226
  21.9 10.7 %collective-permute-start.28 = (bf16[4,8,48,128]{3,2,1,0:T(8,128)(2,1)S(1)}, bf16[4,8,48,128]{3,2,1,0:T(8,128)(2,1)S(1)}, u32[]{:S(2)}, u32[]{:S(2)}) collective-permute-start(bf16[4,8,48,128]{3,2,1,0:T(8,128)(2,1)S(1)} %join_row.2.refs_0_), channel_id=1, source_target_pairs={{0,48},{8,200},{16,32},{24,216},{32,16},{40,232},{48,0},{56,248},{... | collective-permute-start | bytes 1179656 | tf_op jit(solution)/shard_map/ppermute | solution.py:226
  22.5 4.8 %collective-permute-start.27 = (bf16[2,2,64,384]{3,2,1,0:T(8,128)(2,1)S(1)}, bf16[2,2,64,384]{3,2,1,0:T(8,128)(2,1)S(1)}, u32[]{:S(2)}, u32[]{:S(2)}) collective-permute-start(bf16[2,2,64,384]{3,2,1,0:T(8,128)(2,1)S(1)} %collective-permute-done.24.refs_3_), channel_id=1, source_target_pairs={{0,1},{1,0},{2,3},{3,2},{4,5},{5,4},{6,7},{7,6},{8,9},{9,8},{10,11... | collective-permute-start | bytes 589832 | tf_op jit(solution)/shard_map/ppermute | solution.py:239
  22.5 6.1 %collective-permute-start.26 = (bf16[2,2,64,384]{3,2,1,0:T(8,128)(2,1)S(1)}, bf16[2,2,64,384]{3,2,1,0:T(8,128)(2,1)S(1)}, u32[]{:S(2)}, u32[]{:S(2)}) collective-permute-start(bf16[2,2,64,384]{3,2,1,0:T(8,128)(2,1)S(1)} %collective-permute-done.25.refs_4_), channel_id=1, source_target_pairs={{0,7},{1,2},{2,1},{3,4},{4,3},{5,6},{6,5},{7,0},{8,15},{9,10},{10,... | collective-permute-start | bytes 589832 | tf_op jit(solution)/shard_map/ppermute | solution.py:238
  27.3 5.8 %collective-permute-start.29 = (bf16[1,2,64,384]{3,2,1,0:T(8,128)(2,1)S(1)}, bf16[1,2,64,384]{3,2,1,0:T(8,128)(2,1)S(1)}, u32[]{:S(2)}, u32[]{:S(2)}) collective-permute-start(bf16[1,2,64,384]{3,2,1,0:T(8,128)(2,1)S(1)} %slice.22), channel_id=1, source_target_pairs={{0,7},{1,2},{2,1},{3,4},{4,3},{5,6},{6,5},{7,0},{8,15},{9,10},{10,... | collective-permute-start | bytes 294920 | tf_op jit(solution)/shard_map/ppermute | solution.py:241
  28.6 4.5 %collective-permute-start.30 = (bf16[1,2,64,384]{3,2,1,0:T(8,128)(2,1)S(1)}, bf16[1,2,64,384]{3,2,1,0:T(8,128)(2,1)S(1)}, u32[]{:S(2)}, u32[]{:S(2)}) collective-permute-start(bf16[1,2,64,384]{3,2,1,0:T(8,128)(2,1)S(1)} %slice.19), channel_id=1, source_target_pairs={{0,1},{1,0},{2,3},{3,2},{4,5},{5,4},{6,7},{7,6},{8,9},{9,8},{10,11... | collective-permute-start | bytes 294920 | tf_op jit(solution)/shard_map/ppermute | solution.py:242
  33.8 5.2 %collective-permute-start.31 = (f32[16,48,128]{2,1,0:T(8,128)S(1)}, f32[16,48,128]{2,1,0:T(8,128)S(1)}, u32[]{:S(2)}, u32[]{:S(2)}) collective-permute-start(f32[16,48,128]{2,1,0:T(8,128)S(1)} %far_pair.1), channel_id=1, source_target_pairs={{0,8},{8,0},{16,24},{24,16},{32,40},{40,32},{48,56},{56,48},{64,72... | collective-permute-start | bytes 1179656 | tf_op jit(solution)/shard_map/ppermute | solution.py:610

commit v7 on v6

--- a/solution.py
+++ b/solution.py
@@ -48,14 +48,16 @@
     return pos
 
 
-def give_kernel(window, labels_ref, w_ref, give_ref, pos_ref, width_ref, l_all, w_all, sems):
+def give_kernel(window, labels_ref, t_ref, w_ref, give_ref, pos_ref, width_ref, t_all, w_keep, l_all, w_all, sems):
     base = 0 if window is None else window[0] * CAP
     ne = give_ref.shape[1]
-    other = 1 - lax.axis_index("tr") % 2
-    fetch_l = pltpu.make_async_copy(labels_ref, l_all, sems.at[ne])
-    fetch_w = [pltpu.make_async_copy(w_ref.at[2 * e + other], w_all.at[e], sems.at[e]) for e in range(ne)]
+    core = lax.axis_index("tr") % 2
+    fetch_l = pltpu.make_async_copy(labels_ref, l_all, sems.at[0])
+    fetch_w = [pltpu.make_async_copy(w_ref.at[2 * e + 1 - core], w_all.at[e], sems.at[1 + e]) for e in range(ne)]
+    later = [pltpu.make_async_copy(w_ref.at[2 * e + core], w_keep.at[e], sems.at[1 + ne + e]) for e in range(ne)]
+    later.append(pltpu.make_async_copy(t_ref, t_all, sems.at[1 + 2 * ne]))
     fetch_l.start()
-    for copy in fetch_w:
+    for copy in fetch_w + later:
         copy.start()
     fetch_l.wait()
     pos = group_positions(l_all[...].reshape(1, l_all.shape[0]))
@@ -65,27 +67,20 @@
     for e in range(ne):
         fetch_w[e].wait()
         give_ref[0, e] = jnp.dot(pick, w_all[e], preferred_element_type=F32).astype(BF)
-
-
-def keep_kernel(window, pos_ref, t_ref, w_ref, row_ref, keep_ref, t_all, w_all, sems):
+    for copy in later:
+        copy.wait()
+
+
+def keep_kernel(window, pos_ref, t_ref, w_ref, row_ref, keep_ref):
     base = 0 if window is None else window[0] * CAP
-    ne = keep_ref.shape[1]
-    core = lax.axis_index("tr") % 2
-    fetch_w = [pltpu.make_async_copy(w_ref.at[2 * e + core], w_all.at[e], sems.at[e]) for e in range(ne)]
-    fetch_t = pltpu.make_async_copy(t_ref, t_all, sems.at[ne])
-    for copy in fetch_w:
-        copy.start()
-    fetch_t.start()
     pick = pick_matrix(pos_ref[...], base)
     none = jnp.zeros_like(pick)
-    for e in range(ne):
-        fetch_w[e].wait()
-        keep_ref[0, e] = jnp.dot(pick, w_all[e], preferred_element_type=F32).astype(BF)
-    fetch_t.wait()
-    ni, na, v = t_all.shape
+    for e in range(keep_ref.shape[1]):
+        keep_ref[0, e] = jnp.dot(pick, w_ref[e], preferred_element_type=F32).astype(BF)
+    ni, na, v = t_ref.shape
     half = ni // 2
-    low = t_all[:half].reshape(half * na, v)
-    high = t_all[half:].reshape(half * na, v)
+    low = t_ref[:half].reshape(half * na, v)
+    high = t_ref[half:].reshape(half * na, v)
     dims = (((1,), (1,)), ((), ()))
     both = lax.dot_general(low, jnp.concatenate([pick, none], 0), dims, preferred_element_type=F32)
     both += lax.dot_general(high, jnp.concatenate([none, pick], 0), dims, preferred_element_type=F32)
@@ -132,7 +127,7 @@
     return kernel, [SMEM], [window]
 
 
-def pack_give(window, labels, w):
+def pack_give(window, labels, t, w):
     nk, v, _ = w.shape
     kernel, specs, args = windowed(give_kernel, window)
     return pl.pallas_call(
@@ -141,17 +136,19 @@
             jax.ShapeDtypeStruct((1, nk // 2, CAP, v), BF),
             jax.ShapeDtypeStruct((1, v), jnp.int32),
             jax.ShapeDtypeStruct((1, 128), jnp.int32),
+            jax.ShapeDtypeStruct(t.shape, BF),
+            jax.ShapeDtypeStruct((nk // 2, v, v), BF),
         ),
-        in_specs=specs + [ANY, ANY],
-        out_specs=(VMEM, VMEM, VMEM),
+        in_specs=specs + [ANY] * 3,
+        out_specs=(VMEM,) * 5,
         scratch_shapes=[
             pltpu.VMEM((v,), jnp.int32),
             pltpu.VMEM((nk // 2, v, v), BF),
-            pltpu.SemaphoreType.DMA((nk // 2 + 1,)),
+            pltpu.SemaphoreType.DMA((nk + 2,)),
         ],
         compiler_params=pltpu.CompilerParams(vmem_limit_bytes=8 * 2**20),
         name="pack_give",
-    )(*args, labels, w)
+    )(*args, labels, t, w)
 
 
 def pack_keep(window, pos, t, w):
@@ -162,15 +159,10 @@
         kernel,
         out_shape=(
             jax.ShapeDtypeStruct((1, ni // 2, na, 2 * CAP), BF),
-            jax.ShapeDtypeStruct((1, nk // 2, CAP, v), BF),
+            jax.ShapeDtypeStruct((1, nk, CAP, v), BF),
         ),
-        in_specs=specs + [VMEM, ANY, ANY],
+        in_specs=specs + [VMEM] * 3,
         out_specs=(VMEM, VMEM),
-        scratch_shapes=[
-            pltpu.VMEM(t.shape, BF),
-            pltpu.VMEM((nk // 2, v, v), BF),
-            pltpu.SemaphoreType.DMA((nk // 2 + 1,)),
-        ],
         compiler_params=pltpu.CompilerParams(vmem_limit_bytes=8 * 2**20),
         cost_estimate=pl.CostEstimate(flops=0, bytes_accessed=4 * 2**20, transcendentals=0),
         name="pack_keep",
@@ -594,9 +586,9 @@
     w = integrals.reshape(integrals.shape[0], v, v)
 
     def pack(window):
-        give, pos, width = pack_give(window, virtual_irreps, w)
+        give, pos, width, t_here, w_here = pack_give(window, virtual_irreps, t, w)
         got = lax.ppermute(give, "tr", SWAP)
-        row, keep = pack_keep(window, pos, t, w)
+        row, keep = pack_keep(window, pos, t_here, w_here)
         return keep, got, row, pos, width
 
     keep, got, row, pos, width = pack(None)

time: 41.1 us -> 41 us (level)
  waiting for transfers between devices: 5.63 us -> 7.1 us
  Pallas kernels: 10.1 us -> 9.05 us
    pallas_call x1, Pallas kernels: 1.51 us -> 0.42 us  [pack_keep(): pl.pallas_call(kernel, out_shape=(jax.ShapeDtypeStruct((1, ni // 2, na, 2...]
    ppermute x1, starting transfers between devices: 1.12 us -> 0.47 us  [gather(): a4 = lax.ppermute(b3[:1], 'su', ODD_LINKS)]
    ppermute x1, waiting for transfers between devices: 0.17 us -> 0.82 us  [gather(): a3 = lax.ppermute(b2, 'su', ODD_LINKS)]
    ppermute x1, starting transfers between devices: 3.83 us -> 4.4 us  [body(): lax.ppermute(far_pair(pick_other, spread, other, rest, b4), 'tr', SWAP)]
    ppermute x1, waiting for transfers between devices: 0.01 us -> 0.52 us  [pack(): got = lax.ppermute(give, 'tr', SWAP)]
  transfers between devices with their start and end apart: 16 -> 16, of which waited for: 4 -> 5; matrix products, arithmetic and copies ran while one was open for 0% -> 0% of each run, Pallas kernels for 17% -> 14%
where the time goes in v7:
time: 41 us; the launch traced here: 40.9 us
  starting transfers between devices  23.8 us (58%)
  Pallas kernels  9.05 us (22%)
  waiting for transfers between devices  7.1 us (17%)
  between operations  0.88 us (2%)
    ppermute x6, starting transfers between devices, lines(): return [lax.ppermute(piece, 'tr', line(first, flip)) for flip in (1, 2, 3)]  7.01 us
    ppermute x1, starting transfers between devices, gather(): a1 = lax.ppermute(d, 'su', ODD_LINKS)  4.55 us
    ppermute x1, starting transfers between devices, body(): lax.ppermute(far_pair(pick_other, spread, other, rest, b4), 'tr', SWAP)  4.4 us
    ppermute x6, waiting for transfers between devices, lines(): return [lax.ppermute(piece, 'tr', line(first, flip)) for flip in (1, 2, 3)]  4.4 us
    ppermute x1, starting transfers between devices, pack(): got = lax.ppermute(give, 'tr', SWAP)  3.33 us
    ppermute x1, starting transfers between devices, gather(): a2 = lax.ppermute(b1, 'su', ODD_LINKS)  2.08 us
    pallas_call x1, Pallas kernels, pack_give(): pl.pallas_call(kernel, out_shape=(jax.ShapeDtypeStruct((1, nk // 2, CAP,...  1.49 us
    ppermute x1, starting transfers between devices, gather(): a3 = lax.ppermute(b2, 'su', ODD_LINKS)  1.45 us
  transfers between devices with their start and end apart: 16, of which 5 were waited for; matrix products, arithmetic and copies ran while one was open for 0% of the time, Pallas kernels for 14%

profile of v7, /device:TPU:1, one launch (start us, length us, event | category | flops | bytes accessed | tf_op | source)
XLA Modules:
  0.0 40.9 jit_solution(12455212297626615306)
XLA Ops:
  0.0 1.5 %pack_give.2 = (bf16[1,2,64,384]{3,2,1,0:T(8,128)(2,1)S(1)}, s32[1,384]{1,0:T(1,128)S(1)}, s32[1,128]{1,0:T(1,128)S(1)}, bf16[16,48,384]{2,1,0:T(8,128)(2,1)S(1)}, bf16[2,384,384]{2,1,0:T(8,128)(2,1)S(1)}) custom-call(s32[384]{0:T(512)} %labels_ref.3, bf16[16,48,384]{2,1,0:T(8,128)(2,1)} %bitcast.15, bf16[4,384,384]{2,1,0:T(8,128)(2,1)} %bitcast.9.w_ref), custom_call_target="tpu_custom_call" | custom-call | tf_op jit(solution)/shard_map/pack_give/pallas_call | solution.py:133
  1.5 3.3 %collective-permute-start.21 = (bf16[1,2,64,384]{3,2,1,0:T(8,128)(2,1)S(1)}, bf16[1,2,64,384]{3,2,1,0:T(8,128)(2,1)S(1)}, u32[]{:S(2)}, u32[]{:S(2)}) collective-permute-start(bf16[1,2,64,384]{3,2,1,0:T(8,128)(2,1)S(1)} %get-tuple-element.109), channel_id=1, source_target_pairs={{0,8},{8,0},{16,24},{24,16},{32,40},{40,32},{48,56},{56,48},{64,72... | collective-permute-start | bytes 294920 | tf_op jit(solution)/shard_map/ppermute | solution.py:590
  4.8 0.4 %pack_keep.2 = (bf16[1,8,48,128]{3,2,1,0:T(8,128)(2,1)S(1)}, bf16[1,2,64,384]{3,2,1,0:T(8,128)(2,1)S(1)}) custom-call(s32[1,384]{1,0:T(1,128)S(1)} %get-tuple-element.99.pos_ref, bf16[16,48,384]{2,1,0:T(8,128)(2,1)S(1)} %get-tuple-element.105.t_ref, bf16[2,384,384]{2,1,0:T(8,128)(2,1)S(1)} %get-tuple-element.106.w_ref), custom_call_target="tpu_custom_call" | custom-call | bytes 4194304 | tf_op jit(solution)/shard_map/pack_keep/pallas_call | solution.py:158
  5.2 0.5 %collective-permute-done.21.refs_1_ = bf16[1,2,64,384]{3,2,1,0:T(8,128)(2,1)S(1)} collective-permute-done((bf16[1,2,64,384]{3,2,1,0:T(8,128)(2,1)S(1)}, bf16[1,2,64,384]{3,2,1,0:T(8,128)(2,1)S(1)}, u32[]{:S(2)}, u32[]{:S(2)}) %collective-permute-start.21) | collective-permute-done | bytes 98336 | tf_op jit(solution)/shard_map/ppermute | solution.py:590
  5.8 0.1 collective-permute-start.23
  5.9 4.6 %collective-permute-start.22 = (bf16[2,2,64,384]{3,2,1,0:T(8,128)(2,1)S(1)}, bf16[2,2,64,384]{3,2,1,0:T(8,128)(2,1)S(1)}, u32[]{:S(2)}, u32[]{:S(2)}) collective-permute-start(bf16[2,2,64,384]{3,2,1,0:T(8,128)(2,1)S(1)} %join_w.2.refs_0_), channel_id=1, source_target_pairs={{0,7},{1,2},{2,1},{3,4},{4,3},{5,6},{6,5},{7,0},{8,15},{9,10},{10,... | collective-permute-start | bytes 589832 | tf_op jit(solution)/shard_map/ppermute | solution.py:224
  10.4 2.7 %collective-permute-start.18 = (bf16[1,8,48,128]{3,2,1,0:T(8,128)(2,1)S(1)}, bf16[1,8,48,128]{3,2,1,0:T(8,128)(2,1)S(1)}, u32[]{:S(2)}, u32[]{:S(2)}) collective-permute-start(bf16[1,8,48,128]{3,2,1,0:T(8,128)(2,1)S(1)} %get-tuple-element.107.refs_0_), channel_id=1, source_target_pairs={{0,192},{8,56},{16,208},{24,40},{32,224},{40,24},{48,240},{56,8},{... | collective-permute-start | bytes 294920 | tf_op jit(solution)/shard_map/ppermute | solution.py:218
  13.2 0.3 collective-permute-start.17
  13.5 0.2 collective-permute-start.16
  13.8 2.1 %collective-permute-start.24 = (bf16[2,2,64,384]{3,2,1,0:T(8,128)(2,1)S(1)}, bf16[2,2,64,384]{3,2,1,0:T(8,128)(2,1)S(1)}, u32[]{:S(2)}, u32[]{:S(2)}) collective-permute-start(bf16[2,2,64,384]{3,2,1,0:T(8,128)(2,1)S(1)} %collective-permute-done.23.refs_2_), channel_id=1, source_target_pairs={{0,7},{1,2},{2,1},{3,4},{4,3},{5,6},{6,5},{7,0},{8,15},{9,10},{10,... | collective-permute-start | bytes 589832 | tf_op jit(solution)/shard_map/ppermute | solution.py:228
  15.8 0.0 collective-permute-done.22.refs_1_
  15.9 0.0 collective-permute-start.25
  15.9 0.0 collective-permute-done.18.refs_3_
  15.9 2.3 %collective-permute-done.17.refs_2_ = bf16[1,8,48,128]{3,2,1,0:T(8,128)(2,1)S(1)} collective-permute-done((bf16[1,8,48,128]{3,2,1,0:T(8,128)(2,1)S(1)}, bf16[1,8,48,128]{3,2,1,0:T(8,128)(2,1)S(1)}, u32[]{:S(2)}, u32[]{:S(2)}) %collective-permute-start.17) | collective-permute-done | bytes 98336 | tf_op jit(solution)/shard_map/ppermute | solution.py:218
  18.2 2.8 %collective-permute-start.20 = (bf16[4,8,48,128]{3,2,1,0:T(8,128)(2,1)S(1)}, bf16[4,8,48,128]{3,2,1,0:T(8,128)(2,1)S(1)}, u32[]{:S(2)}, u32[]{:S(2)}) collective-permute-start(bf16[4,8,48,128]{3,2,1,0:T(8,128)(2,1)S(1)} %join_row.2.refs_0_), channel_id=1, source_target_pairs={{0,32},{8,136},{16,48},{24,152},{32,0},{40,168},{48,16},{56,184},{... | collective-permute-start | bytes 1179656 | tf_op jit(solution)/shard_map/ppermute | solution.py:218
  21.0 0.3 collective-permute-start.19
  21.3 0.6 %collective-permute-start.28 = (bf16[4,8,48,128]{3,2,1,0:T(8,128)(2,1)S(1)}, bf16[4,8,48,128]{3,2,1,0:T(8,128)(2,1)S(1)}, u32[]{:S(2)}, u32[]{:S(2)}) collective-permute-start(bf16[4,8,48,128]{3,2,1,0:T(8,128)(2,1)S(1)} %join_row.2.refs_0_), channel_id=1, source_target_pairs={{0,48},{8,200},{16,32},{24,216},{32,16},{40,232},{48,0},{56,248},{... | collective-permute-start | bytes 1179656 | tf_op jit(solution)/shard_map/ppermute | solution.py:218
  21.9 1.5 %collective-permute-start.26 = (bf16[2,2,64,384]{3,2,1,0:T(8,128)(2,1)S(1)}, bf16[2,2,64,384]{3,2,1,0:T(8,128)(2,1)S(1)}, u32[]{:S(2)}, u32[]{:S(2)}) collective-permute-start(bf16[2,2,64,384]{3,2,1,0:T(8,128)(2,1)S(1)} %collective-permute-done.25.refs_4_), channel_id=1, source_target_pairs={{0,7},{1,2},{2,1},{3,4},{4,3},{5,6},{6,5},{7,0},{8,15},{9,10},{10,... | collective-permute-start | bytes 589832 | tf_op jit(solution)/shard_map/ppermute | solution.py:230
  23.3 1.1 %prepare.1 = (s32[48,384]{1,0:T(8,128)S(1)}, s32[16,48,128]{2,1,0:T(8,128)S(1)}, s32[16,48,128]{2,1,0:T(8,128)S(1)}, s32[16,48,128]{2,1,0:T(8,128)S(1)}, bf16[51...) custom-call(s32[32]{0:T(128)S(1)} %copy-done.7, s32[384]{0:T(512)S(1)} %copy-done.6, ...), custom_call_target="tpu_custom_call" | custom-call | tf_op jit(solution)/shard_map/prepare/pallas_call | solution.py:175
  24.4 0.9 %spread.2 = (bf16[10,64,512]{2,1,0:T(8,128)(2,1)S(1)}, bf16[10,64,512]{2,1,0:T(8,128)(2,1)S(1)}) custom-call(bf16[512,384]{1,0:T(8,128)(2,1)S(1)} %get-tuple-element.104.spread_ref, bf16[2,2,64,384]{3,2,1,0:T(8,128)(2,1)S(1)} %join_w.2.refs_0_, bf16[2,2,64,384]{3,2,1,0:T(8,128)(2,1)S(1)} %collective-permute-done.22.refs_1_, ...), custom_call_target="tpu_custom_call" | custom-call | flops 503316480 | bytes 4194304 | tf_op jit(solution)/shard_map/spread/pallas_call | solution.py:363
  25.4 1.3 %collective-permute-done.27.refs_1_ = bf16[2,2,64,384]{3,2,1,0:T(8,128)(2,1)S(1)} collective-permute-done((bf16[2,2,64,384]{3,2,1,0:T(8,128)(2,1)S(1)}, bf16[2,2,64,384]{3,2,1,0:T(8,128)(2,1)S(1)}, u32[]{:S(2)}, u32[]{:S(2)}) %collective-permute-start.27) | collective-permute-done | bytes 196640 | tf_op jit(solution)/shard_map/ppermute | solution.py:231
  26.7 0.5 %collective-permute-start.29 = (bf16[1,2,64,384]{3,2,1,0:T(8,128)(2,1)S(1)}, bf16[1,2,64,384]{3,2,1,0:T(8,128)(2,1)S(1)}, u32[]{:S(2)}, u32[]{:S(2)}) collective-permute-start(bf16[1,2,64,384]{3,2,1,0:T(8,128)(2,1)S(1)} %slice.22), channel_id=1, source_target_pairs={{0,7},{1,2},{2,1},{3,4},{4,3},{5,6},{6,5},{7,0},{8,15},{9,10},{10,... | collective-permute-start | bytes 294920 | tf_op jit(solution)/shard_map/ppermute | solution.py:233
  27.2 0.8 %collective-permute-done.26.refs_0_ = bf16[2,2,64,384]{3,2,1,0:T(8,128)(2,1)S(1)} collective-permute-done((bf16[2,2,64,384]{3,2,1,0:T(8,128)(2,1)S(1)}, bf16[2,2,64,384]{3,2,1,0:T(8,128)(2,1)S(1)}, u32[]{:S(2)}, u32[]{:S(2)}) %collective-permute-start.26) | collective-permute-done | bytes 196640 | tf_op jit(solution)/shard_map/ppermute | solution.py:230
  28.0 0.4 %collective-permute-start.30 = (bf16[1,2,64,384]{3,2,1,0:T(8,128)(2,1)S(1)}, bf16[1,2,64,384]{3,2,1,0:T(8,128)(2,1)S(1)}, u32[]{:S(2)}, u32[]{:S(2)}) collective-permute-start(bf16[1,2,64,384]{3,2,1,0:T(8,128)(2,1)S(1)} %slice.19), channel_id=1, source_target_pairs={{0,1},{1,0},{2,3},{3,2},{4,5},{5,4},{6,7},{7,6},{8,9},{9,8},{10,11... | collective-permute-start | bytes 294920 | tf_op jit(solution)/shard_map/ppermute | solution.py:234
  28.5 0.5 %spread.3 = (bf16[4,64,512]{2,1,0:T(8,128)(2,1)S(1)}, bf16[4,64,512]{2,1,0:T(8,128)(2,1)S(1)}) custom-call(bf16[512,384]{1,0:T(8,128)(2,1)S(1)} %get-tuple-element.104.spread_ref, bf16[2,2,64,384]{3,2,1,0:T(8,128)(2,1)S(1)} %collective-permute-done.26.refs_0_, bf16[2,2,64,384]{3,2,1,0:T(8,128)(2,1)S(1)} %collective-permute-done.27.refs_1_), custom_call_target="tpu_custom_call" | custom-call | flops 201326592 | bytes 4194304 | tf_op jit(solution)/shard_map/spread/pallas_call | solution.py:363
  28.9 2.1 %collective-permute-done.19.refs_1_ = bf16[4,8,48,128]{3,2,1,0:T(8,128)(2,1)S(1)} collective-permute-done((bf16[4,8,48,128]{3,2,1,0:T(8,128)(2,1)S(1)}, bf16[4,8,48,128]{3,2,1,0:T(8,128)(2,1)S(1)}, u32[]{:S(2)}, u32[]{:S(2)}) %collective-permute-start.19) | collective-permute-done | bytes 393248 | tf_op jit(solution)/shard_map/ppermute | solution.py:218
  31.0 1.0 %early_sums.1 = (f32[2,384,512]{2,1,0:T(8,128)S(1)}, bf16[2,384,768]{2,1,0:T(8,128)(2,1)S(1)}) custom-call(bf16[4,8,48,128]{3,2,1,0:T(8,128)(2,1)S(1)} %join_row.2.refs_0_, bf16[4,8,48,128]{3,2,1,0:T(8,128)(2,1)S(1)} %collective-permute-done.19.refs_1_, bf16[4,8,48,128]{3,2,1,0:T(8,128)(2,1)S(1)} %collective-permute-done.20.refs_2_, ...), custom_call_target="tpu_custom_call" | custom-call | flops 603979776 | bytes 6291456 | tf_op jit(solution)/shard_map/early_sums/pallas_call | solution.py:427
  32.1 0.5 %other_pair.1 = (f32[16,48,128]{2,1,0:T(8,128)S(1)}, bf16[2,384,256]{2,1,0:T(8,128)(2,1)S(1)}, bf16[2,384,128]{2,1,0:T(8,128)(2,1)S(1)}) custom-call(s32[16,48,128]{2,1,0:T(8,128)S(1)} %get-tuple-element.116.pick_ref, bf16[4,8,48,128]{3,2,1,0:T(8,128)(2,1)S(1)} %join_row.2.refs_0_, bf16[4,8,48,128]{3,2,1,0:T(8,128)(2,1)S(1)} %collective-permute-done.19.refs_1_, ...), custom_call_target="tpu_custom_call" | custom-call | flops 201326592 | bytes 6291456 | tf_op jit(solution)/shard_map/other_pair/pallas_call | solution.py:484
  32.6 0.6 %far_pair.1 = f32[16,48,128]{2,1,0:T(8,128)S(1)} custom-call(s32[16,48,128]{2,1,0:T(8,128)S(1)} %get-tuple-element.116.pick_ref, bf16[512,384]{1,0:T(8,128)(2,1)S(1)} %get-tuple-element.104.spread_ref, f32[16,48,128]{2,1,0:T(8,128)S(1)} %get-tuple-element.124.sums_ref, bf16[2,384,128]{2,1,0:T(8,128)(2,1)S(1)} %get-tuple-element.121.rest_ref, ...), custom_call_target="tpu_custom_call" | custom-call | tf_op jit(solution)/shard_map/far_pair/pallas_call | solution.py:521
  33.2 4.4 %collective-permute-start.31 = (f32[16,48,128]{2,1,0:T(8,128)S(1)}, f32[16,48,128]{2,1,0:T(8,128)S(1)}, u32[]{:S(2)}, u32[]{:S(2)}) collective-permute-start(f32[16,48,128]{2,1,0:T(8,128)S(1)} %far_pair.1), channel_id=1, source_target_pairs={{0,8},{8,0},{16,24},{24,16},{32,40},{40,32},{48,56},{56,48},{64,72... | collective-permute-start | bytes 1179656 | tf_op jit(solution)/shard_map/ppermute | solution.py:602
  37.6 1.4 %own_pair.1.own_ref = f32[16,48,128]{2,1,0:T(8,128)S(1)} custom-call(s32[16,48,128]{2,1,0:T(8,128)S(1)} %get-tuple-element.103.pick_ref, bf16[512,384]{1,0:T(8,128)(2,1)S(1)} %get-tuple-element.104.spread_ref, bf16[2,384,768]{2,1,0:T(8,128)(2,1)S(1)} %get-tuple-element.115.t_cat, bf16[2,384,256]{2,1,0:T(8,128)(2,1)S(1)} %get-tuple-element.118.late_ref, ...), custom_call_target="tpu_custom_call" | custom-call | flops 905969664 | bytes 4194304 | tf_op jit(solution)/shard_map/own_pair/pallas_call | solution.py:555
  39.0 1.1 %last_part.1 = (bf16[16,48,384]{2,1,0:T(8,128)(2,1)}, s32[1]{0:T(128)}) custom-call(s32[1,128]{1,0:T(1,128)S(1)} %get-tuple-element.98.width_ref, s32[48,384]{1,0:T(8,128)S(1)} %get-tuple-element.100.bits_ref, s32[16,48,128]{2,1,0:T(8,128)S(1)} %get-tuple-element.101.half_ref, bf16[128,384]{1,0:T(8,128)(2,1)S(1)} %get-tuple-element.102.expand_ref, ...), custom_call_target="tpu_custom_call" | custom-call | tf_op jit(solution)/shard_map/last_part/pallas_call | solution.py:604
  (19 shorter events, 0.1 us)
Async XLA Ops:
  1.5 4.3 %collective-permute-start.21 = (bf16[1,2,64,384]{3,2,1,0:T(8,128)(2,1)S(1)}, bf16[1,2,64,384]{3,2,1,0:T(8,128)(2,1)S(1)}, u32[]{:S(2)}, u32[]{:S(2)}) collective-permute-start(bf16[1,2,64,384]{3,2,1,0:T(8,128)(2,1)S(1)} %get-tuple-element.109), channel_id=1, source_target_pairs={{0,8},{8,0},{16,24},{24,16},{32,40},{40,32},{48,56},{56,48},{64,72... | collective-permute-start | bytes 294920 | tf_op jit(solution)/shard_map/ppermute | solution.py:590
  4.8 18.5 %copy-start.6 = (s32[384]{0:T(512)S(1)}, s32[384]{0:T(512)}, u32[]{:S(2)}) copy-start(s32[384]{0:T(512)} %labels_ref.3) | copy-start | bytes 4612
  4.8 18.5 %copy-start.7 = (s32[32]{0:T(128)S(1)}, s32[32]{0:T(128)}, u32[]{:S(2)}) copy-start(s32[32]{0:T(128)} %occ_ref.1) | copy-start | bytes 388
  5.8 8.0 %collective-permute-start.23 = (bf16[2,2,64,384]{3,2,1,0:T(8,128)(2,1)S(1)}, bf16[2,2,64,384]{3,2,1,0:T(8,128)(2,1)S(1)}, u32[]{:S(2)}, u32[]{:S(2)}) collective-permute-start(bf16[2,2,64,384]{3,2,1,0:T(8,128)(2,1)S(1)} %join_w.2.refs_0_), channel_id=1, source_target_pairs={{0,1},{1,0},{2,3},{3,2},{4,5},{5,4},{6,7},{7,6},{8,9},{9,8},{10,11... | collective-permute-start | bytes 589832 | tf_op jit(solution)/shard_map/ppermute | solution.py:225
  5.9 10.0 %collective-permute-start.22 = (bf16[2,2,64,384]{3,2,1,0:T(8,128)(2,1)S(1)}, bf16[2,2,64,384]{3,2,1,0:T(8,128)(2,1)S(1)}, u32[]{:S(2)}, u32[]{:S(2)}) collective-permute-start(bf16[2,2,64,384]{3,2,1,0:T(8,128)(2,1)S(1)} %join_w.2.refs_0_), channel_id=1, source_target_pairs={{0,7},{1,2},{2,1},{3,4},{4,3},{5,6},{6,5},{7,0},{8,15},{9,10},{10,... | collective-permute-start | bytes 589832 | tf_op jit(solution)/shard_map/ppermute | solution.py:224
  10.4 5.4 %collective-permute-start.18 = (bf16[1,8,48,128]{3,2,1,0:T(8,128)(2,1)S(1)}, bf16[1,8,48,128]{3,2,1,0:T(8,128)(2,1)S(1)}, u32[]{:S(2)}, u32[]{:S(2)}) collective-permute-start(bf16[1,8,48,128]{3,2,1,0:T(8,128)(2,1)S(1)} %get-tuple-element.107.refs_0_), channel_id=1, source_target_pairs={{0,192},{8,56},{16,208},{24,40},{32,224},{40,24},{48,240},{56,8},{... | collective-permute-start | bytes 294920 | tf_op jit(solution)/shard_map/ppermute | solution.py:218
  13.2 5.0 %collective-permute-start.17 = (bf16[1,8,48,128]{3,2,1,0:T(8,128)(2,1)S(1)}, bf16[1,8,48,128]{3,2,1,0:T(8,128)(2,1)S(1)}, u32[]{:S(2)}, u32[]{:S(2)}) collective-permute-start(bf16[1,8,48,128]{3,2,1,0:T(8,128)(2,1)S(1)} %get-tuple-element.107.refs_0_), channel_id=1, source_target_pairs={{0,128},{8,40},{16,144},{24,56},{32,160},{40,8},{48,176},{56,24},{... | collective-permute-start | bytes 294920 | tf_op jit(solution)/shard_map/ppermute | solution.py:218
  13.5 4.6 %collective-permute-start.16 = (bf16[1,8,48,128]{3,2,1,0:T(8,128)(2,1)S(1)}, bf16[1,8,48,128]{3,2,1,0:T(8,128)(2,1)S(1)}, u32[]{:S(2)}, u32[]{:S(2)}) collective-permute-start(bf16[1,8,48,128]{3,2,1,0:T(8,128)(2,1)S(1)} %get-tuple-element.107.refs_0_), channel_id=1, source_target_pairs={{0,64},{8,24},{16,80},{24,8},{32,96},{40,56},{48,112},{56,40},{64,... | collective-permute-start | bytes 294920 | tf_op jit(solution)/shard_map/ppermute | solution.py:218
  13.8 8.1 %collective-permute-start.24 = (bf16[2,2,64,384]{3,2,1,0:T(8,128)(2,1)S(1)}, bf16[2,2,64,384]{3,2,1,0:T(8,128)(2,1)S(1)}, u32[]{:S(2)}, u32[]{:S(2)}) collective-permute-start(bf16[2,2,64,384]{3,2,1,0:T(8,128)(2,1)S(1)} %collective-permute-done.23.refs_2_), channel_id=1, source_target_pairs={{0,7},{1,2},{2,1},{3,4},{4,3},{5,6},{6,5},{7,0},{8,15},{9,10},{10,... | collective-permute-start | bytes 589832 | tf_op jit(solution)/shard_map/ppermute | solution.py:228
  15.9 6.0 %collective-permute-start.25 = (bf16[2,2,64,384]{3,2,1,0:T(8,128)(2,1)S(1)}, bf16[2,2,64,384]{3,2,1,0:T(8,128)(2,1)S(1)}, u32[]{:S(2)}, u32[]{:S(2)}) collective-permute-start(bf16[2,2,64,384]{3,2,1,0:T(8,128)(2,1)S(1)} %collective-permute-done.22.refs_1_), channel_id=1, source_target_pairs={{0,1},{1,0},{2,3},{3,2},{4,5},{5,4},{6,7},{7,6},{8,9},{9,8},{10,11... | collective-permute-start | bytes 589832 | tf_op jit(solution)/shard_map/ppermute | solution.py:229
  18.2 10.8 %collective-permute-start.20 = (bf16[4,8,48,128]{3,2,1,0:T(8,128)(2,1)S(1)}, bf16[4,8,48,128]{3,2,1,0:T(8,128)(2,1)S(1)}, u32[]{:S(2)}, u32[]{:S(2)}) collective-permute-start(bf16[4,8,48,128]{3,2,1,0:T(8,128)(2,1)S(1)} %join_row.2.refs_0_), channel_id=1, source_target_pairs={{0,32},{8,136},{16,48},{24,152},{32,0},{40,168},{48,16},{56,184},{... | collective-permute-start | bytes 1179656 | tf_op jit(solution)/shard_map/ppermute | solution.py:218
  21.0 10.0 %collective-permute-start.19 = (bf16[4,8,48,128]{3,2,1,0:T(8,128)(2,1)S(1)}, bf16[4,8,48,128]{3,2,1,0:T(8,128)(2,1)S(1)}, u32[]{:S(2)}, u32[]{:S(2)}) collective-permute-start(bf16[4,8,48,128]{3,2,1,0:T(8,128)(2,1)S(1)} %join_row.2.refs_0_), channel_id=1, source_target_pairs={{0,16},{8,72},{16,0},{24,88},{32,48},{40,104},{48,32},{56,120},{64... | collective-permute-start | bytes 1179656 | tf_op jit(solution)/shard_map/ppermute | solution.py:218
  21.3 10.7 %collective-permute-start.28 = (bf16[4,8,48,128]{3,2,1,0:T(8,128)(2,1)S(1)}, bf16[4,8,48,128]{3,2,1,0:T(8,128)(2,1)S(1)}, u32[]{:S(2)}, u32[]{:S(2)}) collective-permute-start(bf16[4,8,48,128]{3,2,1,0:T(8,128)(2,1)S(1)} %join_row.2.refs_0_), channel_id=1, source_target_pairs={{0,48},{8,200},{16,32},{24,216},{32,16},{40,232},{48,0},{56,248},{... | collective-permute-start | bytes 1179656 | tf_op jit(solution)/shard_map/ppermute | solution.py:218
  21.9 4.8 %collective-permute-start.27 = (bf16[2,2,64,384]{3,2,1,0:T(8,128)(2,1)S(1)}, bf16[2,2,64,384]{3,2,1,0:T(8,128)(2,1)S(1)}, u32[]{:S(2)}, u32[]{:S(2)}) collective-permute-start(bf16[2,2,64,384]{3,2,1,0:T(8,128)(2,1)S(1)} %collective-permute-done.24.refs_3_), channel_id=1, source_target_pairs={{0,1},{1,0},{2,3},{3,2},{4,5},{5,4},{6,7},{7,6},{8,9},{9,8},{10,11... | collective-permute-start | bytes 589832 | tf_op jit(solution)/shard_map/ppermute | solution.py:231
  21.9 6.1 %collective-permute-start.26 = (bf16[2,2,64,384]{3,2,1,0:T(8,128)(2,1)S(1)}, bf16[2,2,64,384]{3,2,1,0:T(8,128)(2,1)S(1)}, u32[]{:S(2)}, u32[]{:S(2)}) collective-permute-start(bf16[2,2,64,384]{3,2,1,0:T(8,128)(2,1)S(1)} %collective-permute-done.25.refs_4_), channel_id=1, source_target_pairs={{0,7},{1,2},{2,1},{3,4},{4,3},{5,6},{6,5},{7,0},{8,15},{9,10},{10,... | collective-permute-start | bytes 589832 | tf_op jit(solution)/shard_map/ppermute | solution.py:230
  26.7 5.9 %collective-permute-start.29 = (bf16[1,2,64,384]{3,2,1,0:T(8,128)(2,1)S(1)}, bf16[1,2,64,384]{3,2,1,0:T(8,128)(2,1)S(1)}, u32[]{:S(2)}, u32[]{:S(2)}) collective-permute-start(bf16[1,2,64,384]{3,2,1,0:T(8,128)(2,1)S(1)} %slice.22), channel_id=1, source_target_pairs={{0,7},{1,2},{2,1},{3,4},{4,3},{5,6},{6,5},{7,0},{8,15},{9,10},{10,... | collective-permute-start | bytes 294920 | tf_op jit(solution)/shard_map/ppermute | solution.py:233
  28.0 4.6 %collective-permute-start.30 = (bf16[1,2,64,384]{3,2,1,0:T(8,128)(2,1)S(1)}, bf16[1,2,64,384]{3,2,1,0:T(8,128)(2,1)S(1)}, u32[]{:S(2)}, u32[]{:S(2)}) collective-permute-start(bf16[1,2,64,384]{3,2,1,0:T(8,128)(2,1)S(1)} %slice.19), channel_id=1, source_target_pairs={{0,1},{1,0},{2,3},{3,2},{4,5},{5,4},{6,7},{7,6},{8,9},{9,8},{10,11... | collective-permute-start | bytes 294920 | tf_op jit(solution)/shard_map/ppermute | solution.py:234
  33.2 5.8 %collective-permute-start.31 = (f32[16,48,128]{2,1,0:T(8,128)S(1)}, f32[16,48,128]{2,1,0:T(8,128)S(1)}, u32[]{:S(2)}, u32[]{:S(2)}) collective-permute-start(f32[16,48,128]{2,1,0:T(8,128)S(1)} %far_pair.1), channel_id=1, source_target_pairs={{0,8},{8,0},{16,24},{24,16},{32,40},{40,32},{48,56},{56,48},{64,72... | collective-permute-start | bytes 1179656 | tf_op jit(solution)/shard_map/ppermute | solution.py:602

commit v8 on v7

--- a/solution.py
+++ b/solution.py
@@ -415,8 +415,8 @@
                 t_cat[h, :, at : at + lanes] = pair_lanes(one, two, h)
             for u in range(2):
                 put_block(d_early, d_late, 2 * p + u, second, d_cat, at + u * CAP)
-    for h in range(2):
-        other_ref[h] = jnp.dot(t_cat[h], d_cat[...], preferred_element_type=F32)
+    left = t_cat[...].reshape(2 * t_cat.shape[1], t_cat.shape[2])
+    other_ref[...] = jnp.dot(left, d_cat[...], preferred_element_type=F32).reshape(other_ref.shape)
 
 
 def early_sums(t_parts, d_other):
@@ -509,12 +509,10 @@
 def far_pair_kernel(pick_ref, spread_ref, sums_ref, rest_ref, d_ref, out_ref):
     right = spread_far(d_ref, spread_ref)
     ni, na = out_ref.shape[:2]
-    half_i = ni // 2
-    for h in range(2):
-        sums = jnp.dot(rest_ref[h], right, preferred_element_type=F32)
-        for u in range(half_i):
-            i = h * half_i + u
-            out_ref[i] = sums_ref[i] + keep_pair(sums[u * na : (u + 1) * na], pick_ref[i])
+    left = rest_ref[...].reshape(ni * na, rest_ref.shape[2])
+    sums = jnp.dot(left, right, preferred_element_type=F32)
+    for i in range(ni):
+        out_ref[i] = sums_ref[i] + keep_pair(sums[i * na : (i + 1) * na], pick_ref[i])
 
 
 def far_pair(pick, spread, sums, rest, d):
@@ -540,12 +538,10 @@
             put_block(d_early, d_late, first, second, d_cat, (second * NX + first) * CAP)
     d_cat[NX * NX * CAP :] = spread_far(far_ref, spread_ref)
     ni, na = own_ref.shape[:2]
-    half_i = ni // 2
-    for h in range(2):
-        sums = jnp.dot(left_cat[h], d_cat[...], preferred_element_type=F32)
-        for u in range(half_i):
-            i = h * half_i + u
-            own_ref[i] = keep_pair(sums[u * na : (u + 1) * na], pick_ref[i])
+    left = left_cat[...].reshape(ni * na, left_cat.shape[2])
+    sums = jnp.dot(left, d_cat[...], preferred_element_type=F32)
+    for i in range(ni):
+        own_ref[i] = keep_pair(sums[i * na : (i + 1) * na], pick_ref[i])
 
 
 def own_pair(pick, spread, t_cat, late, d, rest, far):

time: 41 us -> 40.9 us (level)
  no operation moved by 1% of the time
where the time goes in v8:
time: 40.9 us; the launch traced here: 40.8 us
  starting transfers between devices  23.9 us (58%)
  Pallas kernels  8.86 us (22%)
  waiting for transfers between devices  7.11 us (17%)
  between operations  0.87 us (2%)
    ppermute x6, starting transfers between devices, lines(): return [lax.ppermute(piece, 'tr', line(first, flip)) for flip in (1, 2, 3)]  7.01 us
    ppermute x1, starting transfers between devices, gather(): a1 = lax.ppermute(d, 'su', ODD_LINKS)  4.55 us
    ppermute x1, starting transfers between devices, body(): lax.ppermute(far_pair(pick_other, spread, other, rest, b4), 'tr', SWAP)  4.52 us
    ppermute x6, waiting for transfers between devices, lines(): return [lax.ppermute(piece, 'tr', line(first, flip)) for flip in (1, 2, 3)]  4.4 us
    ppermute x1, starting transfers between devices, pack(): got = lax.ppermute(give, 'tr', SWAP)  3.33 us
    ppermute x1, starting transfers between devices, gather(): a2 = lax.ppermute(b1, 'su', ODD_LINKS)  2.08 us
    pallas_call x1, Pallas kernels, pack_give(): pl.pallas_call(kernel, out_shape=(jax.ShapeDtypeStruct((1, nk // 2, CAP,...  1.49 us
    ppermute x1, starting transfers between devices, gather(): a3 = lax.ppermute(b2, 'su', ODD_LINKS)  1.45 us
  transfers between devices with their start and end apart: 16, of which 5 were waited for; matrix products, arithmetic and copies ran while one was open for 0% of the time, Pallas kernels for 14%

profile of v8, /device:TPU:1, one launch (start us, length us, event | category | flops | bytes accessed | tf_op | source)
XLA Modules:
  0.0 40.8 jit_solution(6393513531142570662)
XLA Ops:
  0.0 1.5 %pack_give.2 = (bf16[1,2,64,384]{3,2,1,0:T(8,128)(2,1)S(1)}, s32[1,384]{1,0:T(1,128)S(1)}, s32[1,128]{1,0:T(1,128)S(1)}, bf16[16,48,384]{2,1,0:T(8,128)(2,1)S(1)}, bf16[2,384,384]{2,1,0:T(8,128)(2,1)S(1)}) custom-call(s32[384]{0:T(512)} %labels_ref.3, bf16[16,48,384]{2,1,0:T(8,128)(2,1)} %bitcast.15, bf16[4,384,384]{2,1,0:T(8,128)(2,1)} %bitcast.9.w_ref), custom_call_target="tpu_custom_call" | custom-call | tf_op jit(solution)/shard_map/pack_give/pallas_call | solution.py:133
  1.5 3.3 %collective-permute-start.21 = (bf16[1,2,64,384]{3,2,1,0:T(8,128)(2,1)S(1)}, bf16[1,2,64,384]{3,2,1,0:T(8,128)(2,1)S(1)}, u32[]{:S(2)}, u32[]{:S(2)}) collective-permute-start(bf16[1,2,64,384]{3,2,1,0:T(8,128)(2,1)S(1)} %get-tuple-element.109), channel_id=1, source_target_pairs={{0,8},{8,0},{16,24},{24,16},{32,40},{40,32},{48,56},{56,48},{64,72... | collective-permute-start | bytes 294920 | tf_op jit(solution)/shard_map/ppermute | solution.py:586
  4.8 0.4 %pack_keep.2 = (bf16[1,8,48,128]{3,2,1,0:T(8,128)(2,1)S(1)}, bf16[1,2,64,384]{3,2,1,0:T(8,128)(2,1)S(1)}) custom-call(s32[1,384]{1,0:T(1,128)S(1)} %get-tuple-element.99.pos_ref, bf16[16,48,384]{2,1,0:T(8,128)(2,1)S(1)} %get-tuple-element.105.t_ref, bf16[2,384,384]{2,1,0:T(8,128)(2,1)S(1)} %get-tuple-element.106.w_ref), custom_call_target="tpu_custom_call" | custom-call | bytes 4194304 | tf_op jit(solution)/shard_map/pack_keep/pallas_call | solution.py:158
  5.2 0.5 %collective-permute-done.21.refs_1_ = bf16[1,2,64,384]{3,2,1,0:T(8,128)(2,1)S(1)} collective-permute-done((bf16[1,2,64,384]{3,2,1,0:T(8,128)(2,1)S(1)}, bf16[1,2,64,384]{3,2,1,0:T(8,128)(2,1)S(1)}, u32[]{:S(2)}, u32[]{:S(2)}) %collective-permute-start.21) | collective-permute-done | bytes 98336 | tf_op jit(solution)/shard_map/ppermute | solution.py:586
  5.8 0.1 collective-permute-start.23
  5.9 4.6 %collective-permute-start.22 = (bf16[2,2,64,384]{3,2,1,0:T(8,128)(2,1)S(1)}, bf16[2,2,64,384]{3,2,1,0:T(8,128)(2,1)S(1)}, u32[]{:S(2)}, u32[]{:S(2)}) collective-permute-start(bf16[2,2,64,384]{3,2,1,0:T(8,128)(2,1)S(1)} %join_w.2.refs_0_), channel_id=1, source_target_pairs={{0,7},{1,2},{2,1},{3,4},{4,3},{5,6},{6,5},{7,0},{8,15},{9,10},{10,... | collective-permute-start | bytes 589832 | tf_op jit(solution)/shard_map/ppermute | solution.py:224
  10.4 2.7 %collective-permute-start.18 = (bf16[1,8,48,128]{3,2,1,0:T(8,128)(2,1)S(1)}, bf16[1,8,48,128]{3,2,1,0:T(8,128)(2,1)S(1)}, u32[]{:S(2)}, u32[]{:S(2)}) collective-permute-start(bf16[1,8,48,128]{3,2,1,0:T(8,128)(2,1)S(1)} %get-tuple-element.107.refs_0_), channel_id=1, source_target_pairs={{0,192},{8,56},{16,208},{24,40},{32,224},{40,24},{48,240},{56,8},{... | collective-permute-start | bytes 294920 | tf_op jit(solution)/shard_map/ppermute | solution.py:218
  13.2 0.3 collective-permute-start.17
  13.5 0.2 collective-permute-start.16
  13.8 0.0 collective-permute-done.23.refs_2_
  13.8 2.1 %collective-permute-start.24 = (bf16[2,2,64,384]{3,2,1,0:T(8,128)(2,1)S(1)}, bf16[2,2,64,384]{3,2,1,0:T(8,128)(2,1)S(1)}, u32[]{:S(2)}, u32[]{:S(2)}) collective-permute-start(bf16[2,2,64,384]{3,2,1,0:T(8,128)(2,1)S(1)} %collective-permute-done.23.refs_2_), channel_id=1, source_target_pairs={{0,7},{1,2},{2,1},{3,4},{4,3},{5,6},{6,5},{7,0},{8,15},{9,10},{10,... | collective-permute-start | bytes 589832 | tf_op jit(solution)/shard_map/ppermute | solution.py:228
  15.9 2.3 %collective-permute-done.17.refs_2_ = bf16[1,8,48,128]{3,2,1,0:T(8,128)(2,1)S(1)} collective-permute-done((bf16[1,8,48,128]{3,2,1,0:T(8,128)(2,1)S(1)}, bf16[1,8,48,128]{3,2,1,0:T(8,128)(2,1)S(1)}, u32[]{:S(2)}, u32[]{:S(2)}) %collective-permute-start.17) | collective-permute-done | bytes 98336 | tf_op jit(solution)/shard_map/ppermute | solution.py:218
  18.2 2.8 %collective-permute-start.20 = (bf16[4,8,48,128]{3,2,1,0:T(8,128)(2,1)S(1)}, bf16[4,8,48,128]{3,2,1,0:T(8,128)(2,1)S(1)}, u32[]{:S(2)}, u32[]{:S(2)}) collective-permute-start(bf16[4,8,48,128]{3,2,1,0:T(8,128)(2,1)S(1)} %join_row.2.refs_0_), channel_id=1, source_target_pairs={{0,32},{8,136},{16,48},{24,152},{32,0},{40,168},{48,16},{56,184},{... | collective-permute-start | bytes 1179656 | tf_op jit(solution)/shard_map/ppermute | solution.py:218
  21.0 0.3 collective-permute-start.19
  21.3 0.6 %collective-permute-start.28 = (bf16[4,8,48,128]{3,2,1,0:T(8,128)(2,1)S(1)}, bf16[4,8,48,128]{3,2,1,0:T(8,128)(2,1)S(1)}, u32[]{:S(2)}, u32[]{:S(2)}) collective-permute-start(bf16[4,8,48,128]{3,2,1,0:T(8,128)(2,1)S(1)} %join_row.2.refs_0_), channel_id=1, source_target_pairs={{0,48},{8,200},{16,32},{24,216},{32,16},{40,232},{48,0},{56,248},{... | collective-permute-start | bytes 1179656 | tf_op jit(solution)/shard_map/ppermute | solution.py:218
  21.9 0.0 collective-permute-done.24.refs_3_
  21.9 1.5 %collective-permute-start.26 = (bf16[2,2,64,384]{3,2,1,0:T(8,128)(2,1)S(1)}, bf16[2,2,64,384]{3,2,1,0:T(8,128)(2,1)S(1)}, u32[]{:S(2)}, u32[]{:S(2)}) collective-permute-start(bf16[2,2,64,384]{3,2,1,0:T(8,128)(2,1)S(1)} %collective-permute-done.25.refs_4_), channel_id=1, source_target_pairs={{0,7},{1,2},{2,1},{3,4},{4,3},{5,6},{6,5},{7,0},{8,15},{9,10},{10,... | collective-permute-start | bytes 589832 | tf_op jit(solution)/shard_map/ppermute | solution.py:230
  23.3 1.1 %prepare.1 = (s32[48,384]{1,0:T(8,128)S(1)}, s32[16,48,128]{2,1,0:T(8,128)S(1)}, s32[16,48,128]{2,1,0:T(8,128)S(1)}, s32[16,48,128]{2,1,0:T(8,128)S(1)}, bf16[51...) custom-call(s32[32]{0:T(128)S(1)} %copy-done.7, s32[384]{0:T(512)S(1)} %copy-done.6, ...), custom_call_target="tpu_custom_call" | custom-call | tf_op jit(solution)/shard_map/prepare/pallas_call | solution.py:175
  24.4 0.9 %spread.2 = (bf16[10,64,512]{2,1,0:T(8,128)(2,1)S(1)}, bf16[10,64,512]{2,1,0:T(8,128)(2,1)S(1)}) custom-call(bf16[512,384]{1,0:T(8,128)(2,1)S(1)} %get-tuple-element.104.spread_ref, bf16[2,2,64,384]{3,2,1,0:T(8,128)(2,1)S(1)} %join_w.2.refs_0_, bf16[2,2,64,384]{3,2,1,0:T(8,128)(2,1)S(1)} %collective-permute-done.22.refs_1_, ...), custom_call_target="tpu_custom_call" | custom-call | flops 503316480 | bytes 4194304 | tf_op jit(solution)/shard_map/spread/pallas_call | solution.py:363
  25.4 1.3 %collective-permute-done.27.refs_1_ = bf16[2,2,64,384]{3,2,1,0:T(8,128)(2,1)S(1)} collective-permute-done((bf16[2,2,64,384]{3,2,1,0:T(8,128)(2,1)S(1)}, bf16[2,2,64,384]{3,2,1,0:T(8,128)(2,1)S(1)}, u32[]{:S(2)}, u32[]{:S(2)}) %collective-permute-start.27) | collective-permute-done | bytes 196640 | tf_op jit(solution)/shard_map/ppermute | solution.py:231
  26.7 0.5 %collective-permute-start.29 = (bf16[1,2,64,384]{3,2,1,0:T(8,128)(2,1)S(1)}, bf16[1,2,64,384]{3,2,1,0:T(8,128)(2,1)S(1)}, u32[]{:S(2)}, u32[]{:S(2)}) collective-permute-start(bf16[1,2,64,384]{3,2,1,0:T(8,128)(2,1)S(1)} %slice.22), channel_id=1, source_target_pairs={{0,7},{1,2},{2,1},{3,4},{4,3},{5,6},{6,5},{7,0},{8,15},{9,10},{10,... | collective-permute-start | bytes 294920 | tf_op jit(solution)/shard_map/ppermute | solution.py:233
  27.2 0.8 %collective-permute-done.26.refs_0_ = bf16[2,2,64,384]{3,2,1,0:T(8,128)(2,1)S(1)} collective-permute-done((bf16[2,2,64,384]{3,2,1,0:T(8,128)(2,1)S(1)}, bf16[2,2,64,384]{3,2,1,0:T(8,128)(2,1)S(1)}, u32[]{:S(2)}, u32[]{:S(2)}) %collective-permute-start.26) | collective-permute-done | bytes 196640 | tf_op jit(solution)/shard_map/ppermute | solution.py:230
  28.0 0.4 %collective-permute-start.30 = (bf16[1,2,64,384]{3,2,1,0:T(8,128)(2,1)S(1)}, bf16[1,2,64,384]{3,2,1,0:T(8,128)(2,1)S(1)}, u32[]{:S(2)}, u32[]{:S(2)}) collective-permute-start(bf16[1,2,64,384]{3,2,1,0:T(8,128)(2,1)S(1)} %slice.19), channel_id=1, source_target_pairs={{0,1},{1,0},{2,3},{3,2},{4,5},{5,4},{6,7},{7,6},{8,9},{9,8},{10,11... | collective-permute-start | bytes 294920 | tf_op jit(solution)/shard_map/ppermute | solution.py:234
  28.5 0.5 %spread.3 = (bf16[4,64,512]{2,1,0:T(8,128)(2,1)S(1)}, bf16[4,64,512]{2,1,0:T(8,128)(2,1)S(1)}) custom-call(bf16[512,384]{1,0:T(8,128)(2,1)S(1)} %get-tuple-element.104.spread_ref, bf16[2,2,64,384]{3,2,1,0:T(8,128)(2,1)S(1)} %collective-permute-done.26.refs_0_, bf16[2,2,64,384]{3,2,1,0:T(8,128)(2,1)S(1)} %collective-permute-done.27.refs_1_), custom_call_target="tpu_custom_call" | custom-call | flops 201326592 | bytes 4194304 | tf_op jit(solution)/shard_map/spread/pallas_call | solution.py:363
  28.9 2.1 %collective-permute-done.19.refs_1_ = bf16[4,8,48,128]{3,2,1,0:T(8,128)(2,1)S(1)} collective-permute-done((bf16[4,8,48,128]{3,2,1,0:T(8,128)(2,1)S(1)}, bf16[4,8,48,128]{3,2,1,0:T(8,128)(2,1)S(1)}, u32[]{:S(2)}, u32[]{:S(2)}) %collective-permute-start.19) | collective-permute-done | bytes 393248 | tf_op jit(solution)/shard_map/ppermute | solution.py:218
  31.0 0.9 %early_sums.1 = (f32[2,384,512]{2,1,0:T(8,128)S(1)}, bf16[2,384,768]{2,1,0:T(8,128)(2,1)S(1)}) custom-call(bf16[4,8,48,128]{3,2,1,0:T(8,128)(2,1)S(1)} %join_row.2.refs_0_, bf16[4,8,48,128]{3,2,1,0:T(8,128)(2,1)S(1)} %collective-permute-done.19.refs_1_, bf16[4,8,48,128]{3,2,1,0:T(8,128)(2,1)S(1)} %collective-permute-done.20.refs_2_, ...), custom_call_target="tpu_custom_call" | custom-call | flops 603979776 | bytes 6291456 | tf_op jit(solution)/shard_map/early_sums/pallas_call | solution.py:427
  31.9 0.5 %other_pair.1 = (f32[16,48,128]{2,1,0:T(8,128)S(1)}, bf16[2,384,256]{2,1,0:T(8,128)(2,1)S(1)}, bf16[2,384,128]{2,1,0:T(8,128)(2,1)S(1)}) custom-call(s32[16,48,128]{2,1,0:T(8,128)S(1)} %get-tuple-element.116.pick_ref, bf16[4,8,48,128]{3,2,1,0:T(8,128)(2,1)S(1)} %join_row.2.refs_0_, bf16[4,8,48,128]{3,2,1,0:T(8,128)(2,1)S(1)} %collective-permute-done.19.refs_1_, ...), custom_call_target="tpu_custom_call" | custom-call | flops 201326592 | bytes 6291456 | tf_op jit(solution)/shard_map/other_pair/pallas_call | solution.py:484
  32.5 0.6 %far_pair.1 = f32[16,48,128]{2,1,0:T(8,128)S(1)} custom-call(s32[16,48,128]{2,1,0:T(8,128)S(1)} %get-tuple-element.116.pick_ref, bf16[512,384]{1,0:T(8,128)(2,1)S(1)} %get-tuple-element.104.spread_ref, f32[16,48,128]{2,1,0:T(8,128)S(1)} %get-tuple-element.124.sums_ref, bf16[2,384,128]{2,1,0:T(8,128)(2,1)S(1)} %get-tuple-element.121.rest_ref, ...), custom_call_target="tpu_custom_call" | custom-call | tf_op jit(solution)/shard_map/far_pair/pallas_call | solution.py:519
  33.1 4.5 %collective-permute-start.31 = (f32[16,48,128]{2,1,0:T(8,128)S(1)}, f32[16,48,128]{2,1,0:T(8,128)S(1)}, u32[]{:S(2)}, u32[]{:S(2)}) collective-permute-start(f32[16,48,128]{2,1,0:T(8,128)S(1)} %far_pair.1), channel_id=1, source_target_pairs={{0,8},{8,0},{16,24},{24,16},{32,40},{40,32},{48,56},{56,48},{64,72... | collective-permute-start | bytes 1179656 | tf_op jit(solution)/shard_map/ppermute | solution.py:598
  37.6 1.3 %own_pair.1.own_ref = f32[16,48,128]{2,1,0:T(8,128)S(1)} custom-call(s32[16,48,128]{2,1,0:T(8,128)S(1)} %get-tuple-element.103.pick_ref, bf16[512,384]{1,0:T(8,128)(2,1)S(1)} %get-tuple-element.104.spread_ref, bf16[2,384,768]{2,1,0:T(8,128)(2,1)S(1)} %get-tuple-element.115.t_cat, bf16[2,384,256]{2,1,0:T(8,128)(2,1)S(1)} %get-tuple-element.118.late_ref, ...), custom_call_target="tpu_custom_call" | custom-call | flops 905969664 | bytes 4194304 | tf_op jit(solution)/shard_map/own_pair/pallas_call | solution.py:551
  38.9 0.0 collective-permute-done.31.got_ref
  38.9 1.1 %last_part.1 = (bf16[16,48,384]{2,1,0:T(8,128)(2,1)}, s32[1]{0:T(128)}) custom-call(s32[1,128]{1,0:T(1,128)S(1)} %get-tuple-element.98.width_ref, s32[48,384]{1,0:T(8,128)S(1)} %get-tuple-element.100.bits_ref, s32[16,48,128]{2,1,0:T(8,128)S(1)} %get-tuple-element.101.half_ref, bf16[128,384]{1,0:T(8,128)(2,1)S(1)} %get-tuple-element.102.expand_ref, ...), custom_call_target="tpu_custom_call" | custom-call | tf_op jit(solution)/shard_map/last_part/pallas_call | solution.py:600
  (19 shorter events, 0.1 us)
Async XLA Ops:
  1.5 4.3 %collective-permute-start.21 = (bf16[1,2,64,384]{3,2,1,0:T(8,128)(2,1)S(1)}, bf16[1,2,64,384]{3,2,1,0:T(8,128)(2,1)S(1)}, u32[]{:S(2)}, u32[]{:S(2)}) collective-permute-start(bf16[1,2,64,384]{3,2,1,0:T(8,128)(2,1)S(1)} %get-tuple-element.109), channel_id=1, source_target_pairs={{0,8},{8,0},{16,24},{24,16},{32,40},{40,32},{48,56},{56,48},{64,72... | collective-permute-start | bytes 294920 | tf_op jit(solution)/shard_map/ppermute | solution.py:586
  4.8 18.5 %copy-start.6 = (s32[384]{0:T(512)S(1)}, s32[384]{0:T(512)}, u32[]{:S(2)}) copy-start(s32[384]{0:T(512)} %labels_ref.3) | copy-start | bytes 4612
  4.8 18.5 %copy-start.7 = (s32[32]{0:T(128)S(1)}, s32[32]{0:T(128)}, u32[]{:S(2)}) copy-start(s32[32]{0:T(128)} %occ_ref.1) | copy-start | bytes 388
  5.8 8.0 %collective-permute-start.23 = (bf16[2,2,64,384]{3,2,1,0:T(8,128)(2,1)S(1)}, bf16[2,2,64,384]{3,2,1,0:T(8,128)(2,1)S(1)}, u32[]{:S(2)}, u32[]{:S(2)}) collective-permute-start(bf16[2,2,64,384]{3,2,1,0:T(8,128)(2,1)S(1)} %join_w.2.refs_0_), channel_id=1, source_target_pairs={{0,1},{1,0},{2,3},{3,2},{4,5},{5,4},{6,7},{7,6},{8,9},{9,8},{10,11... | collective-permute-start | bytes 589832 | tf_op jit(solution)/shard_map/ppermute | solution.py:225
  5.9 10.0 %collective-permute-start.22 = (bf16[2,2,64,384]{3,2,1,0:T(8,128)(2,1)S(1)}, bf16[2,2,64,384]{3,2,1,0:T(8,128)(2,1)S(1)}, u32[]{:S(2)}, u32[]{:S(2)}) collective-permute-start(bf16[2,2,64,384]{3,2,1,0:T(8,128)(2,1)S(1)} %join_w.2.refs_0_), channel_id=1, source_target_pairs={{0,7},{1,2},{2,1},{3,4},{4,3},{5,6},{6,5},{7,0},{8,15},{9,10},{10,... | collective-permute-start | bytes 589832 | tf_op jit(solution)/shard_map/ppermute | solution.py:224
  10.4 5.4 %collective-permute-start.18 = (bf16[1,8,48,128]{3,2,1,0:T(8,128)(2,1)S(1)}, bf16[1,8,48,128]{3,2,1,0:T(8,128)(2,1)S(1)}, u32[]{:S(2)}, u32[]{:S(2)}) collective-permute-start(bf16[1,8,48,128]{3,2,1,0:T(8,128)(2,1)S(1)} %get-tuple-element.107.refs_0_), channel_id=1, source_target_pairs={{0,192},{8,56},{16,208},{24,40},{32,224},{40,24},{48,240},{56,8},{... | collective-permute-start | bytes 294920 | tf_op jit(solution)/shard_map/ppermute | solution.py:218
  13.2 5.0 %collective-permute-start.17 = (bf16[1,8,48,128]{3,2,1,0:T(8,128)(2,1)S(1)}, bf16[1,8,48,128]{3,2,1,0:T(8,128)(2,1)S(1)}, u32[]{:S(2)}, u32[]{:S(2)}) collective-permute-start(bf16[1,8,48,128]{3,2,1,0:T(8,128)(2,1)S(1)} %get-tuple-element.107.refs_0_), channel_id=1, source_target_pairs={{0,128},{8,40},{16,144},{24,56},{32,160},{40,8},{48,176},{56,24},{... | collective-permute-start | bytes 294920 | tf_op jit(solution)/shard_map/ppermute | solution.py:218
  13.5 4.6 %collective-permute-start.16 = (bf16[1,8,48,128]{3,2,1,0:T(8,128)(2,1)S(1)}, bf16[1,8,48,128]{3,2,1,0:T(8,128)(2,1)S(1)}, u32[]{:S(2)}, u32[]{:S(2)}) collective-permute-start(bf16[1,8,48,128]{3,2,1,0:T(8,128)(2,1)S(1)} %get-tuple-element.107.refs_0_), channel_id=1, source_target_pairs={{0,64},{8,24},{16,80},{24,8},{32,96},{40,56},{48,112},{56,40},{64,... | collective-permute-start | bytes 294920 | tf_op jit(solution)/shard_map/ppermute | solution.py:218
  13.8 8.1 %collective-permute-start.24 = (bf16[2,2,64,384]{3,2,1,0:T(8,128)(2,1)S(1)}, bf16[2,2,64,384]{3,2,1,0:T(8,128)(2,1)S(1)}, u32[]{:S(2)}, u32[]{:S(2)}) collective-permute-start(bf16[2,2,64,384]{3,2,1,0:T(8,128)(2,1)S(1)} %collective-permute-done.23.refs_2_), channel_id=1, source_target_pairs={{0,7},{1,2},{2,1},{3,4},{4,3},{5,6},{6,5},{7,0},{8,15},{9,10},{10,... | collective-permute-start | bytes 589832 | tf_op jit(solution)/shard_map/ppermute | solution.py:228
  15.9 6.0 %collective-permute-start.25 = (bf16[2,2,64,384]{3,2,1,0:T(8,128)(2,1)S(1)}, bf16[2,2,64,384]{3,2,1,0:T(8,128)(2,1)S(1)}, u32[]{:S(2)}, u32[]{:S(2)}) collective-permute-start(bf16[2,2,64,384]{3,2,1,0:T(8,128)(2,1)S(1)} %collective-permute-done.22.refs_1_), channel_id=1, source_target_pairs={{0,1},{1,0},{2,3},{3,2},{4,5},{5,4},{6,7},{7,6},{8,9},{9,8},{10,11... | collective-permute-start | bytes 589832 | tf_op jit(solution)/shard_map/ppermute | solution.py:229
  18.2 10.8 %collective-permute-start.20 = (bf16[4,8,48,128]{3,2,1,0:T(8,128)(2,1)S(1)}, bf16[4,8,48,128]{3,2,1,0:T(8,128)(2,1)S(1)}, u32[]{:S(2)}, u32[]{:S(2)}) collective-permute-start(bf16[4,8,48,128]{3,2,1,0:T(8,128)(2,1)S(1)} %join_row.2.refs_0_), channel_id=1, source_target_pairs={{0,32},{8,136},{16,48},{24,152},{32,0},{40,168},{48,16},{56,184},{... | collective-permute-start | bytes 1179656 | tf_op jit(solution)/shard_map/ppermute | solution.py:218
  21.0 10.0 %collective-permute-start.19 = (bf16[4,8,48,128]{3,2,1,0:T(8,128)(2,1)S(1)}, bf16[4,8,48,128]{3,2,1,0:T(8,128)(2,1)S(1)}, u32[]{:S(2)}, u32[]{:S(2)}) collective-permute-start(bf16[4,8,48,128]{3,2,1,0:T(8,128)(2,1)S(1)} %join_row.2.refs_0_), channel_id=1, source_target_pairs={{0,16},{8,72},{16,0},{24,88},{32,48},{40,104},{48,32},{56,120},{64... | collective-permute-start | bytes 1179656 | tf_op jit(solution)/shard_map/ppermute | solution.py:218
  21.3 10.6 %collective-permute-start.28 = (bf16[4,8,48,128]{3,2,1,0:T(8,128)(2,1)S(1)}, bf16[4,8,48,128]{3,2,1,0:T(8,128)(2,1)S(1)}, u32[]{:S(2)}, u32[]{:S(2)}) collective-permute-start(bf16[4,8,48,128]{3,2,1,0:T(8,128)(2,1)S(1)} %join_row.2.refs_0_), channel_id=1, source_target_pairs={{0,48},{8,200},{16,32},{24,216},{32,16},{40,232},{48,0},{56,248},{... | collective-permute-start | bytes 1179656 | tf_op jit(solution)/shard_map/ppermute | solution.py:218
  21.9 4.8 %collective-permute-start.27 = (bf16[2,2,64,384]{3,2,1,0:T(8,128)(2,1)S(1)}, bf16[2,2,64,384]{3,2,1,0:T(8,128)(2,1)S(1)}, u32[]{:S(2)}, u32[]{:S(2)}) collective-permute-start(bf16[2,2,64,384]{3,2,1,0:T(8,128)(2,1)S(1)} %collective-permute-done.24.refs_3_), channel_id=1, source_target_pairs={{0,1},{1,0},{2,3},{3,2},{4,5},{5,4},{6,7},{7,6},{8,9},{9,8},{10,11... | collective-permute-start | bytes 589832 | tf_op jit(solution)/shard_map/ppermute | solution.py:231
  21.9 6.1 %collective-permute-start.26 = (bf16[2,2,64,384]{3,2,1,0:T(8,128)(2,1)S(1)}, bf16[2,2,64,384]{3,2,1,0:T(8,128)(2,1)S(1)}, u32[]{:S(2)}, u32[]{:S(2)}) collective-permute-start(bf16[2,2,64,384]{3,2,1,0:T(8,128)(2,1)S(1)} %collective-permute-done.25.refs_4_), channel_id=1, source_target_pairs={{0,7},{1,2},{2,1},{3,4},{4,3},{5,6},{6,5},{7,0},{8,15},{9,10},{10,... | collective-permute-start | bytes 589832 | tf_op jit(solution)/shard_map/ppermute | solution.py:230
  26.7 5.7 %collective-permute-start.29 = (bf16[1,2,64,384]{3,2,1,0:T(8,128)(2,1)S(1)}, bf16[1,2,64,384]{3,2,1,0:T(8,128)(2,1)S(1)}, u32[]{:S(2)}, u32[]{:S(2)}) collective-permute-start(bf16[1,2,64,384]{3,2,1,0:T(8,128)(2,1)S(1)} %slice.22), channel_id=1, source_target_pairs={{0,7},{1,2},{2,1},{3,4},{4,3},{5,6},{6,5},{7,0},{8,15},{9,10},{10,... | collective-permute-start | bytes 294920 | tf_op jit(solution)/shard_map/ppermute | solution.py:233
  28.0 4.4 %collective-permute-start.30 = (bf16[1,2,64,384]{3,2,1,0:T(8,128)(2,1)S(1)}, bf16[1,2,64,384]{3,2,1,0:T(8,128)(2,1)S(1)}, u32[]{:S(2)}, u32[]{:S(2)}) collective-permute-start(bf16[1,2,64,384]{3,2,1,0:T(8,128)(2,1)S(1)} %slice.19), channel_id=1, source_target_pairs={{0,1},{1,0},{2,3},{3,2},{4,5},{5,4},{6,7},{7,6},{8,9},{9,8},{10,11... | collective-permute-start | bytes 294920 | tf_op jit(solution)/shard_map/ppermute | solution.py:234
  33.1 5.9 %collective-permute-start.31 = (f32[16,48,128]{2,1,0:T(8,128)S(1)}, f32[16,48,128]{2,1,0:T(8,128)S(1)}, u32[]{:S(2)}, u32[]{:S(2)}) collective-permute-start(f32[16,48,128]{2,1,0:T(8,128)S(1)} %far_pair.1), channel_id=1, source_target_pairs={{0,8},{8,0},{16,24},{24,16},{32,40},{40,32},{48,56},{56,48},{64,72... | collective-permute-start | bytes 1179656 | tf_op jit(solution)/shard_map/ppermute | solution.py:598
